TPU v7x, 32 devices: a whole 2x2x4 slice. The times are simulated.
32 devices in a mesh: groups: 2 (over x), tgt: 16 (over z, y, core).
Axes of the slice: x: 2, y: 2, z: 4, core: 2. Of those that a mesh axis runs over, the one named last changes fastest.
Arguments:
- target_features: bfloat16 [32768, 1024], P(('groups', 'tgt')), parts along dimension 0, may hold values from -16 to 16
- source_features: bfloat16 [2048, 1024], P(('groups', 'tgt')), parts along dimension 0, may hold values from -16 to 16
- vectors: bfloat16 [2048, 128], P(('groups', 'tgt')), parts along dimension 0, may hold values from -6 to 6
- current: float32 [32768, 128], P(('groups', 'tgt')), parts along dimension 0, may hold values from -6 to 6
- previous: float32 [32768, 128], P(('groups', 'tgt')), parts along dimension 0, may hold values from -100 to 100
Outputs:
- filtered: float32 [32768, 128], P(('groups', 'tgt')), parts along dimension 0
There are 2 independent parts, one for each index of `groups`. A program takes and returns all parts, laid end to end along the dimension named above; each array names one. Nothing has to cross between parts.
All inputs are finite; a program needn't handle non-finite values.
Results may differ from a plain program's by a relative error of at most 0.002.
Values may be sent and summed in bfloat16 or wider, within the bound.
No kernel may reach another device: no remote copies, remote signals or barrier semaphores. Data moves between devices by JAX's collectives and lax.ppermute only.
A program may use at most 128 MiB of HBM per device.

v0:
```python
import math

import jax
import jax.numpy as jnp
from jax import lax
from jax.sharding import PartitionSpec as P


def block_scores(target_features, feats, gamma):
    feat_float = feats.astype(jnp.float32)
    source_sq = jnp.sum(feat_float * feat_float, axis=1)
    dots = jnp.einsum("td,sd->ts", target_features, feats, preferred_element_type=jnp.float32)
    return 2.0 * gamma * dots - gamma * source_sq[None, :]


def on_device(target_features, source_features, vectors, current, previous):
    gamma = 0.25 / math.sqrt(target_features.shape[1])
    rows = target_features.shape[0]
    all_feats, all_vecs = (
        lax.all_gather(source_features, "tgt", axis=0, tiled=True),
        lax.all_gather(vectors, "tgt", axis=0, tiled=True),
    )
    scores = block_scores(target_features, all_feats, gamma)
    row_max = jnp.max(scores, axis=1, keepdims=True)
    weights = jnp.exp(scores - row_max)
    denominator = jnp.sum(weights, axis=1, keepdims=True)
    numer = jnp.dot(weights.astype(jnp.bfloat16), all_vecs, preferred_element_type=jnp.float32)
    applied = numer / denominator
    next_iter = 2.0 / 0.05 * (applied - 0.01 * current) - previous
    column_sq = lax.psum(jnp.sum(next_iter * next_iter, axis=0), "tgt")
    total_rows = rows * lax.axis_size("tgt")
    return next_iter / jnp.sqrt(column_sq / total_rows + 1e-06)


def solution(mesh):
    return jax.shard_map(
        on_device,
        mesh=mesh,
        in_specs=(
            P(("groups", "tgt"), None),
            P(("groups", "tgt"), None),
            P(("groups", "tgt"), None),
            P(("groups", "tgt"), None),
            P(("groups", "tgt"), None),
        ),
        out_specs=P(("groups", "tgt"), None),
        check_vma=False,
    )
```

profile of v0, /device:TPU:0, one launch (start us, length us, event | category | flops | bytes accessed | tf_op | source)
XLA Modules:
  0.0 101.4 jit_solution(1035351655079106904)
XLA Ops:
  6.5 0.0 copy-start
  6.5 0.0 all-gather.2.cloned.1.call-start
  6.5 0.7 all-gather.2.cloned.1.call-update
  7.3 24.1 %all_gather.7 = bf16[1024,128]{1,0:T(8,128)(2,1)S(1)} all-gather(bf16[64,128]{1,0:T(8,128)(2,1)} %param.7), channel_id=1, replica_groups=mesh['groups'=2,'tgt'=16] {'tgt'}, dimensions={0}, use_global_device_ids=true | all-gather | bytes 278528 | tf_op jit(solution)/shard_map/all_gather | solution.py:21
  31.3 22.4 %all-gather.2.cloned.1.call-done = bf16[1024,1024]{1,0:T(8,128)(2,1)} async-done(((bf16[64,1024]{1,0:T(8,128)(2,1)}), bf16[1024,1024]{1,0:T(8,128)(2,1)}) %all-gather.2.cloned.1.call-update) | async-done | bytes 2097168 | tf_op jit(solution)/shard_map/all_gather | solution.py:20
  53.7 2.1 %multiply_reduce_fusion = f32[1024]{0:T(1024)S(1)} fusion(bf16[1024,1024]{1,0:T(8,128)(2,1)} %all-gather.2.cloned.1.call-done), kind=kLoop, calls=%fused_computation.1 | loop fusion | flops 3144704 | bytes 2101248 | tf_op jit(solution)/shard_map/reduce_sum | solution.py:11
  55.8 0.0 copy-done
  55.8 4.0 %fusion = (f32[1024]{0:T(1024)S(1)}, f32[1024,1024]{0,1:T(8,128)S(1)}) fusion(f32[1024]{0:T(1024)S(1)} %broadcast_multiply_fusion, bf16[1024,1024]{1,0:T(8,128)(2,1)S(1)} %copy-done, bf16[1024,1024]{1,0:T(8,128)(2,1)} %all-gather.2.cloned.1.call-done), kind=kOutput, calls=%fused_computation.3 | convolution fusion | flops 2150628352 | bytes 8396800 | tf_op jit(solution)/shard_map/td,sd->ts/dot_general | solution.py:12
  59.8 0.0 copy-start.1
  59.8 0.0 copy-start.2
  59.8 0.9 fusion.1
  60.7 0.1 copy-done.1
  60.9 0.2 copy-done.2
  61.0 1.2 %multiply_reduce_fusion.1 = (f32[128]{0:T(128)S(1)}, f32[1024,128]{1,0:T(8,128)S(1)}) fusion(f32[1024,128]{1,0:T(8,128)S(1)} %copy-done.1, f32[1024,128]{1,0:T(8,128)S(1)} %copy-done.2, f32[1024]{0:T(1024)S(1)} %fusion.1, bf16[1024,128]{1,0:T(8,128)(2,1)S(1)} %all_gather.7, f32[1024,1024]{0,1:T(8,128)S(1)} %get-tuple-element.6, ...), kind=kOutput, calls=%fused_computation.11 | convolution fusion | flops 273547136 | bytes 6042112 | tf_op jit(solution)/shard_map/dot_general | solution.py:27
  62.2 31.4 %psum.7 = f32[128]{0:T(128)S(1)} all-reduce(f32[128]{0:T(128)S(1)} %get-tuple-element.7), channel_id=1, replica_groups=mesh['groups'=2,'tgt'=16] {'tgt'}, use_global_device_ids=true, to_apply=%region_4.0 | all-reduce | flops 128 | bytes 1024 | tf_op jit(solution)/shard_map/psum | solution.py:30
  93.7 0.8 broadcast_divide_fusion
  (2 shorter events, 0.0 us)
Async XLA Ops:
  6.5 49.3 %copy-start = (bf16[1024,1024]{1,0:T(8,128)(2,1)S(1)}, bf16[1024,1024]{1,0:T(8,128)(2,1)}, u32[]{:S(2)}) copy-start(bf16[1024,1024]{1,0:T(8,128)(2,1)} %param.5) | copy-start | bytes 6291460
  6.5 47.2 %all-gather.2.cloned.1.call-start = ((), (), s32[]{:S(2)}) async-start(), calls=%async_computation | async-start | bytes 2228224 | tf_op jit(solution)/shard_map/all_gather | solution.py:20
  59.8 1.0 %copy-start.1 = (f32[1024,128]{1,0:T(8,128)S(1)}, f32[1024,128]{1,0:T(8,128)}, u32[]{:S(2)}) copy-start(f32[1024,128]{1,0:T(8,128)} %param.9) | copy-start | bytes 1572868
  59.8 1.2 %copy-start.2 = (f32[1024,128]{1,0:T(8,128)S(1)}, f32[1024,128]{1,0:T(8,128)}, u32[]{:S(2)}) copy-start(f32[1024,128]{1,0:T(8,128)} %param.8) | copy-start | bytes 1572868
Sparse Core Ops, SparseCore 0:
  9.5 44.1 all-gather.1
where the time goes:
time: 102 us; the launch traced here: 101 us
  blocking collectives  55.5 us (54%)
  waiting for transfers between devices  23.1 us (23%)
  between operations  13.4 us (13%)
  matrix products  5.17 us (5%)
  other arithmetic  3.81 us (4%)
    psum x1, blocking collectives, on_device(): column_sq = lax.psum(jnp.sum(next_iter * next_iter, axis=0), 'tgt')  31.4 us
    all_gather x1, blocking collectives, on_device(): lax.all_gather(vectors, 'tgt', axis=0, tiled=True)  24.1 us
    all_gather x1, waiting for transfers between devices, on_device(): lax.all_gather(source_features, 'tgt', axis=0, tiled=True)  22.4 us
    dot_general x1, matrix products, block_scores(): jnp.einsum('td,sd->ts', target_features, feats, preferred_element_type=jn...  3.97 us
    reduce_sum x1, other arithmetic, block_scores(): source_sq = jnp.sum(feat_float * feat_float, axis=1)  2.07 us
  transfers between devices with their start and end apart: 1, of which 1 were waited for; matrix products, arithmetic and copies ran while one was open for 0% of the time, Pallas kernels for 0%

commit v1 on v0

v1 whole, which is shorter than its diff:
```python
import math

import jax
import jax.numpy as jnp
from jax import lax
from jax.sharding import PartitionSpec as P


def swap(x, bits):
    n = lax.axis_size("tgt")
    return lax.ppermute(x, "tgt", [(i, i ^ bits) for i in range(n)])


def gather(shard):
    n = lax.axis_size("tgt")
    if n & (n - 1) or n < 8:
        return lax.all_gather(shard, "tgt", axis=0, tiled=True)
    held = shard
    parts = []
    bit = n // 2
    far = []
    while bit > 4:
        far.append(bit)
        bit //= 2
    for bit in far[:-1]:
        held = jnp.concatenate([held, swap(held, bit)], axis=0)
    parts = [held]
    if far:
        parts.append(swap(held, far[-1]))
    parts = parts + [swap(x, k) for x in parts for k in (4, 2, 6)]
    parts = parts + [swap(x, 1) for x in parts]
    return jnp.concatenate(parts, axis=0)


def total(x):
    n = lax.axis_size("tgt")
    if n & (n - 1):
        return lax.psum(x, "tgt")
    bit = 1
    while bit < n:
        x = x + swap(x, bit)
        bit *= 2
    return x


def block_scores(target_features, feats, gamma):
    feat_float = feats.astype(jnp.float32)
    source_sq = jnp.sum(feat_float * feat_float, axis=1)
    dots = jnp.einsum("td,sd->ts", target_features, feats, preferred_element_type=jnp.float32)
    return 2.0 * gamma * dots - gamma * source_sq[None, :]


def on_device(target_features, source_features, vectors, current, previous):
    width = target_features.shape[1]
    gamma = 0.25 / math.sqrt(width)
    rows = target_features.shape[0]
    everything = gather(jnp.concatenate([source_features, vectors], axis=1))
    all_feats, all_vecs = everything[:, :width], everything[:, width:]
    scores = block_scores(target_features, all_feats, gamma)
    row_max = jnp.max(scores, axis=1, keepdims=True)
    weights = jnp.exp(scores - row_max)
    denominator = jnp.sum(weights, axis=1, keepdims=True)
    numer = jnp.dot(weights.astype(jnp.bfloat16), all_vecs, preferred_element_type=jnp.float32)
    applied = numer / denominator
    next_iter = 2.0 / 0.05 * (applied - 0.01 * current) - previous
    column_sq = total(jnp.sum(next_iter * next_iter, axis=0, keepdims=True))
    total_rows = rows * lax.axis_size("tgt")
    return next_iter / jnp.sqrt(column_sq / total_rows + 1e-06)


def solution(mesh):
    return jax.shard_map(
        on_device,
        mesh=mesh,
        in_specs=(P(("groups", "tgt"), None),) * 5,
        out_specs=P(("groups", "tgt"), None),
        check_vma=False,
    )
```

time: 102 us -> 55.9 us (0.55)
  blocking collectives: 55.5 us -> 0 us
  starting transfers between devices: 0.01 us -> 18.1 us
  between operations: 13.4 us -> 0.17 us
  waiting for transfers between devices: 23.1 us -> 29.2 us
  local copies, waits for them, and re-layouts: 0.3 us -> 2.38 us
  matrix products: 5.17 us -> 3.59 us
  other arithmetic: 3.81 us -> 2.23 us
    psum x1 -> x0, blocking collectives: 31.4 us -> none  [on_device(): column_sq = lax.psum(jnp.sum(next_iter * next_iter, axis=0), 'tgt')]
    ppermute x0 -> x19, waiting for transfers between devices: none -> 29.2 us  [swap(): return lax.ppermute(x, 'tgt', [(i, i ^ bits) for i in range(n)])]
    all_gather x1 -> x0, blocking collectives: 24.1 us -> none  [on_device(): lax.all_gather(vectors, 'tgt', axis=0, tiled=True)]
    all_gather x1 -> x0, waiting for transfers between devices: 22.4 us -> none  [on_device(): lax.all_gather(source_features, 'tgt', axis=0, tiled=True)]
    ppermute x0 -> x19, starting transfers between devices: none -> 18.1 us  [swap(): return lax.ppermute(x, 'tgt', [(i, i ^ bits) for i in range(n)])]
    reduce_sum x1, other arithmetic: 2.07 us -> 0.48 us  [block_scores(): source_sq = jnp.sum(feat_float * feat_float, axis=1)]
    dot_general x1, matrix products: 3.97 us -> 2.39 us  [block_scores(): jnp.einsum('td,sd->ts', target_features, feats, preferred_element_type=jn...]
    unnamed x6 -> x21, local copies, waits for them, and re-layouts: 0.3 us -> 1.63 us
  transfers between devices with their start and end apart: 1 -> 19, of which waited for: 1 -> 12; matrix products, arithmetic and copies ran while one was open for 0% -> 0% of each run, Pallas kernels for 0% -> 0%
where the time goes in v1:
time: 55.9 us; the launch traced here: 55.7 us
  waiting for transfers between devices  29.2 us (52%)
  starting transfers between devices  18.1 us (32%)
  matrix products  3.59 us (6%)
  local copies, waits for them, and re-layouts  2.38 us (4%)
  other arithmetic  2.23 us (4%)
    ppermute x19, waiting for transfers between devices, swap(): return lax.ppermute(x, 'tgt', [(i, i ^ bits) for i in range(n)])  29.2 us
    ppermute x19, starting transfers between devices, swap(): return lax.ppermute(x, 'tgt', [(i, i ^ bits) for i in range(n)])  18.1 us
    dot_general x1, matrix products, block_scores(): jnp.einsum('td,sd->ts', target_features, feats, preferred_element_type=jn...  2.39 us
    unnamed x21, local copies, waits for them, and re-layouts  1.63 us
    dot_general x1, matrix products, on_device(): jnp.dot(weights.astype(jnp.bfloat16), all_vecs, preferred_element_type=jn...  1.2 us
  transfers between devices with their start and end apart: 19, of which 12 were waited for; matrix products, arithmetic and copies ran while one was open for 0% of the time, Pallas kernels for 0%

profile of v1, /device:TPU:0, one launch (start us, length us, event | category | flops | bytes accessed | tf_op | source)
XLA Modules:
  0.0 55.7 jit_solution(2163334130016748144)
XLA Ops:
  0.0 1.1 %constant_dynamic-update-slice_fusion.1 = (bf16[64,1152]{1,0:T(8,128)(2,1)S(1)}, bf16[1024,1152]{1,0:T(8,128)(2,1)S(1)}) fusion(bf16[64,1024]{1,0:T(8,128)(2,1)} %param.6), kind=kLoop, calls=%fused_computation.17 | loop fusion | bytes 393216
  1.1 0.7 %constant_dynamic-update-slice_fusion = (bf16[64,1152]{1,0:T(8,128)(2,1)S(1)}, bf16[1024,1152]{1,0:T(8,128)(2,1)S(1)}) fusion(bf16[64,1152]{1,0:T(8,128)(2,1)S(1)} %get-tuple-element.5, bf16[64,128]{1,0:T(8,128)(2,1)} %param.7, bf16[1024,1152]{1,0:T(8,128)(2,1)S(1)} %get-tuple-element.6), kind=kLoop, calls=%fused_computation.16 | loop fusion | bytes 49152 | tf_op jit(solution)/shard_map/concatenate | solution.py:57
  1.8 4.0 %collective-permute-start.3 = (bf16[64,1152]{1,0:T(8,128)(2,1)S(1)}, bf16[64,1152]{1,0:T(8,128)(2,1)S(1)}, u32[]{:S(2)}, u32[]{:S(2)}) collective-permute-start(bf16[64,1152]{1,0:T(8,128)(2,1)S(1)} %get-tuple-element.7), channel_id=1, source_target_pairs={{0,6},{1,7},{2,4},{3,5},{4,2},{5,3},{6,0},{7,1},{8,14},{9,15},{10,... | collective-permute-start | bytes 442376 | tf_op jit(solution)/shard_map/ppermute | solution.py:11
  5.9 0.5 collective-permute-start.2
  6.4 0.1 collective-permute-start.1
  6.5 2.9 %collective-permute-start = (bf16[64,1152]{1,0:T(8,128)(2,1)S(1)}, bf16[64,1152]{1,0:T(8,128)(2,1)S(1)}, u32[]{:S(2)}, u32[]{:S(2)}) collective-permute-start(bf16[64,1152]{1,0:T(8,128)(2,1)S(1)} %get-tuple-element.7), channel_id=1, source_target_pairs={{0,8},{1,9},{2,10},{3,11},{4,12},{5,13},{6,14},{7,15},{8,0},{9,1},... | collective-permute-start | bytes 442376 | tf_op jit(solution)/shard_map/ppermute | solution.py:11
  9.4 0.0 collective-permute-start.7
  9.4 0.7 %collective-permute-done.3 = bf16[64,1152]{1,0:T(8,128)(2,1)S(1)} collective-permute-done((bf16[64,1152]{1,0:T(8,128)(2,1)S(1)}, bf16[64,1152]{1,0:T(8,128)(2,1)S(1)}, u32[]{:S(2)}, u32[]{:S(2)}) %collective-permute-start.3) | collective-permute-done | bytes 147488 | tf_op jit(solution)/shard_map/ppermute | solution.py:11
  10.2 0.0 collective-permute-start.11
  10.2 2.7 %collective-permute-done.2 = bf16[64,1152]{1,0:T(8,128)(2,1)S(1)} collective-permute-done((bf16[64,1152]{1,0:T(8,128)(2,1)S(1)}, bf16[64,1152]{1,0:T(8,128)(2,1)S(1)}, u32[]{:S(2)}, u32[]{:S(2)}) %collective-permute-start.2) | collective-permute-done | bytes 147488 | tf_op jit(solution)/shard_map/ppermute | solution.py:11
  12.9 0.0 collective-permute-start.10
  12.9 3.3 %collective-permute-done.1 = bf16[64,1152]{1,0:T(8,128)(2,1)S(1)} collective-permute-done((bf16[64,1152]{1,0:T(8,128)(2,1)S(1)}, bf16[64,1152]{1,0:T(8,128)(2,1)S(1)}, u32[]{:S(2)}, u32[]{:S(2)}) %collective-permute-start.1) | collective-permute-done | bytes 147488 | tf_op jit(solution)/shard_map/ppermute | solution.py:11
  16.2 0.0 collective-permute-start.9
  16.2 0.0 collective-permute-done
  16.2 2.6 %collective-permute-start.4 = (bf16[64,1152]{1,0:T(8,128)(2,1)S(1)}, bf16[64,1152]{1,0:T(8,128)(2,1)S(1)}, u32[]{:S(2)}, u32[]{:S(2)}) collective-permute-start(bf16[64,1152]{1,0:T(8,128)(2,1)S(1)} %collective-permute-done), channel_id=1, source_target_pairs={{0,4},{1,5},{2,6},{3,7},{4,0},{5,1},{6,2},{7,3},{8,12},{9,13},{10,... | collective-permute-start | bytes 442376 | tf_op jit(solution)/shard_map/ppermute | solution.py:11
  18.9 3.6 %collective-permute-done.4 = bf16[64,1152]{1,0:T(8,128)(2,1)S(1)} collective-permute-done((bf16[64,1152]{1,0:T(8,128)(2,1)S(1)}, bf16[64,1152]{1,0:T(8,128)(2,1)S(1)}, u32[]{:S(2)}, u32[]{:S(2)}) %collective-permute-start.4) | collective-permute-done | bytes 147488 | tf_op jit(solution)/shard_map/ppermute | solution.py:11
  22.5 0.4 collective-permute-start.5
  22.9 4.7 %collective-permute-done.5 = bf16[64,1152]{1,0:T(8,128)(2,1)S(1)} collective-permute-done((bf16[64,1152]{1,0:T(8,128)(2,1)S(1)}, bf16[64,1152]{1,0:T(8,128)(2,1)S(1)}, u32[]{:S(2)}, u32[]{:S(2)}) %collective-permute-start.5) | collective-permute-done | bytes 147488 | tf_op jit(solution)/shard_map/ppermute | solution.py:11
  27.6 1.4 %collective-permute-start.6 = (bf16[64,1152]{1,0:T(8,128)(2,1)S(1)}, bf16[64,1152]{1,0:T(8,128)(2,1)S(1)}, u32[]{:S(2)}, u32[]{:S(2)}) collective-permute-start(bf16[64,1152]{1,0:T(8,128)(2,1)S(1)} %collective-permute-done), channel_id=1, source_target_pairs={{0,6},{1,7},{2,4},{3,5},{4,2},{5,3},{6,0},{7,1},{8,14},{9,15},{10,... | collective-permute-start | bytes 442376 | tf_op jit(solution)/shard_map/ppermute | solution.py:11
  29.0 4.6 %collective-permute-done.6 = bf16[64,1152]{1,0:T(8,128)(2,1)S(1)} collective-permute-done((bf16[64,1152]{1,0:T(8,128)(2,1)S(1)}, bf16[64,1152]{1,0:T(8,128)(2,1)S(1)}, u32[]{:S(2)}, u32[]{:S(2)}) %collective-permute-start.6) | collective-permute-done | bytes 147488 | tf_op jit(solution)/shard_map/ppermute | solution.py:11
  33.7 0.0 collective-permute-start.8
  33.7 0.0 collective-permute-done.7
  33.7 0.6 %collective-permute-start.14 = (bf16[64,1152]{1,0:T(8,128)(2,1)S(1)}, bf16[64,1152]{1,0:T(8,128)(2,1)S(1)}, u32[]{:S(2)}, u32[]{:S(2)}) collective-permute-start(bf16[64,1152]{1,0:T(8,128)(2,1)S(1)} %collective-permute-done.6), channel_id=1, source_target_pairs={{0,1},{1,0},{2,3},{3,2},{4,5},{5,4},{6,7},{7,6},{8,9},{9,8},{10,11... | collective-permute-start | bytes 442376 | tf_op jit(solution)/shard_map/ppermute | solution.py:11
  34.3 0.7 %collective-permute-done.8 = bf16[64,1152]{1,0:T(8,128)(2,1)S(1)} collective-permute-done((bf16[64,1152]{1,0:T(8,128)(2,1)S(1)}, bf16[64,1152]{1,0:T(8,128)(2,1)S(1)}, u32[]{:S(2)}, u32[]{:S(2)}) %collective-permute-start.8) | collective-permute-done | bytes 147488 | tf_op jit(solution)/shard_map/ppermute | solution.py:11
  35.0 0.1 collective-permute-start.13
  35.2 0.0 collective-permute-done.9
  35.2 0.4 collective-permute-start.12
  35.7 0.0 collective-permute-done.10
  35.7 0.0 collective-permute-done.11
  35.7 0.9 %collective-permute-done.12 = bf16[64,1152]{1,0:T(8,128)(2,1)S(1)} collective-permute-done((bf16[64,1152]{1,0:T(8,128)(2,1)S(1)}, bf16[64,1152]{1,0:T(8,128)(2,1)S(1)}, u32[]{:S(2)}, u32[]{:S(2)}) %collective-permute-start.12) | collective-permute-done | bytes 147488 | tf_op jit(solution)/shard_map/ppermute | solution.py:11
  36.7 0.0 collective-permute-done.13
  36.7 0.5 multiply_reduce_fusion
  37.2 2.4 %fusion = (f32[1024]{0:T(1024)S(1)}, f32[1024,1024]{1,0:T(8,128)S(1)}) fusion(f32[1024]{0:T(1024)S(1)} %broadcast_multiply_fusion, bf16[1024,1024]{1,0:T(8,128)(2,1)S(1)} %copy-done, bf16[1024,1152]{1,0:T(8,128)(2,1)S(1)} %constant_dynamic-update-slice_fusion.2), kind=kOutput, calls=%fused_computation.3 | convolution fusion | flops 2150628352 | bytes 8396800 | tf_op jit(solution)/shard_map/td,sd->ts/dot_general | solution.py:49
  39.6 0.0 copy-start.1
  39.6 0.0 copy-start.2
  39.7 0.9 %fusion.1 = f32[1024]{0:T(1024)S(1)} fusion(f32[1024,1024]{1,0:T(8,128)S(1)} %get-tuple-element.10, f32[1024]{0:T(1024)S(1)} %get-tuple-element.9, f32[1024]{0:T(1024)S(1)} %broadcast_multiply_fusion), kind=kLoop, calls=%fused_computation.4 | loop fusion | flops 4193280 | bytes 4206592 | tf_op jit(solution)/shard_map/reduce_sum | solution.py:62
  40.6 0.1 copy-done.1
  40.7 0.2 copy-done.2
  40.8 1.2 %multiply_reduce_fusion.1 = (f32[128]{0:T(128)S(1)}, f32[1024,128]{1,0:T(8,128)S(1)}) fusion(f32[1024,128]{1,0:T(8,128)S(1)} %copy-done.1, f32[1024,128]{1,0:T(8,128)S(1)} %copy-done.2, f32[1024]{0:T(1024)S(1)} %fusion.1, bf16[1024,1152]{1,0:T(8,128)(2,1)S(1)} %constant_dynamic-update-slice_fusion.2, f32[1024,1024]{1,0:T(8,128)S(1)} %get-tuple-element.10, ...), kind=kOutput, calls=%fused_computation.13 | convolution fusion | flops 273547136 | bytes 6042112 | tf_op jit(solution)/shard_map/dot_general | solution.py:63
  42.0 0.4 collective-permute-start.15
  42.5 0.8 %collective-permute-done.15 = f32[1,128]{1,0:T(1,128)S(1)} collective-permute-done((f32[1,128]{1,0:T(1,128)S(1)}, f32[1,128]{1,0:T(1,128)S(1)}, u32[]{:S(2)}, u32[]{:S(2)}) %collective-permute-start.15) | collective-permute-done | bytes 544 | tf_op jit(solution)/shard_map/ppermute | solution.py:11
  43.3 0.4 collective-permute-start.16
  43.7 3.2 %collective-permute-done.16 = f32[1,128]{1,0:T(1,128)S(1)} collective-permute-done((f32[1,128]{1,0:T(1,128)S(1)}, f32[1,128]{1,0:T(1,128)S(1)}, u32[]{:S(2)}, u32[]{:S(2)}) %collective-permute-start.16) | collective-permute-done | bytes 544 | tf_op jit(solution)/shard_map/ppermute | solution.py:11
  46.8 1.5 %collective-permute-start.17 = (f32[1,128]{1,0:T(1,128)S(1)}, f32[1,128]{1,0:T(1,128)S(1)}, u32[]{:S(2)}, u32[]{:S(2)}) collective-permute-start(f32[1,128]{1,0:T(1,128)S(1)} %add.19), channel_id=1, source_target_pairs={{0,4},{1,5},{2,6},{3,7},{4,0},{5,1},{6,2},{7,3},{8,12},{9,13},{10,... | collective-permute-start | bytes 1544 | tf_op jit(solution)/shard_map/ppermute | solution.py:11
  48.3 2.1 %collective-permute-done.17 = f32[1,128]{1,0:T(1,128)S(1)} collective-permute-done((f32[1,128]{1,0:T(1,128)S(1)}, f32[1,128]{1,0:T(1,128)S(1)}, u32[]{:S(2)}, u32[]{:S(2)}) %collective-permute-start.17) | collective-permute-done | bytes 544 | tf_op jit(solution)/shard_map/ppermute | solution.py:11
  50.4 2.7 %collective-permute-start.18 = (f32[1,128]{1,0:T(1,128)S(1)}, f32[1,128]{1,0:T(1,128)S(1)}, u32[]{:S(2)}, u32[]{:S(2)}) collective-permute-start(f32[1,128]{1,0:T(1,128)S(1)} %add.20), channel_id=1, source_target_pairs={{0,8},{1,9},{2,10},{3,11},{4,12},{5,13},{6,14},{7,15},{8,0},{9,1},... | collective-permute-start | bytes 1544 | tf_op jit(solution)/shard_map/ppermute | solution.py:11
  53.1 1.7 %collective-permute-done.18 = f32[1,128]{1,0:T(1,128)S(1)} collective-permute-done((f32[1,128]{1,0:T(1,128)S(1)}, f32[1,128]{1,0:T(1,128)S(1)}, u32[]{:S(2)}, u32[]{:S(2)}) %collective-permute-start.18) | collective-permute-done | bytes 544 | tf_op jit(solution)/shard_map/ppermute | solution.py:11
  54.8 0.8 %broadcast_divide_fusion = f32[1024,128]{1,0:T(8,128)} fusion(f32[1024,128]{1,0:T(8,128)S(1)} %get-tuple-element.12, f32[128]{0:T(128)S(1)} %sqrt_bitcast_fusion), kind=kLoop, calls=%fused_computation.15 | loop fusion | flops 131072 | bytes 1049088 | tf_op jit(solution)/shard_map/div | solution.py:68
  (23 shorter events, 0.3 us)
Async XLA Ops:
  0.0 37.2 %copy-start = (bf16[1024,1024]{1,0:T(8,128)(2,1)S(1)}, bf16[1024,1024]{1,0:T(8,128)(2,1)}, u32[]{:S(2)}) copy-start(bf16[1024,1024]{1,0:T(8,128)(2,1)} %param.5) | copy-start | bytes 6291460
  1.8 8.3 %collective-permute-start.3 = (bf16[64,1152]{1,0:T(8,128)(2,1)S(1)}, bf16[64,1152]{1,0:T(8,128)(2,1)S(1)}, u32[]{:S(2)}, u32[]{:S(2)}) collective-permute-start(bf16[64,1152]{1,0:T(8,128)(2,1)S(1)} %get-tuple-element.7), channel_id=1, source_target_pairs={{0,6},{1,7},{2,4},{3,5},{4,2},{5,3},{6,0},{7,1},{8,14},{9,15},{10,... | collective-permute-start | bytes 442376 | tf_op jit(solution)/shard_map/ppermute | solution.py:11
  5.9 7.0 %collective-permute-start.2 = (bf16[64,1152]{1,0:T(8,128)(2,1)S(1)}, bf16[64,1152]{1,0:T(8,128)(2,1)S(1)}, u32[]{:S(2)}, u32[]{:S(2)}) collective-permute-start(bf16[64,1152]{1,0:T(8,128)(2,1)S(1)} %get-tuple-element.7), channel_id=1, source_target_pairs={{0,2},{1,3},{2,0},{3,1},{4,6},{5,7},{6,4},{7,5},{8,10},{9,11},{10,... | collective-permute-start | bytes 442376 | tf_op jit(solution)/shard_map/ppermute | solution.py:11
  6.4 9.8 %collective-permute-start.1 = (bf16[64,1152]{1,0:T(8,128)(2,1)S(1)}, bf16[64,1152]{1,0:T(8,128)(2,1)S(1)}, u32[]{:S(2)}, u32[]{:S(2)}) collective-permute-start(bf16[64,1152]{1,0:T(8,128)(2,1)S(1)} %get-tuple-element.7), channel_id=1, source_target_pairs={{0,4},{1,5},{2,6},{3,7},{4,0},{5,1},{6,2},{7,3},{8,12},{9,13},{10,... | collective-permute-start | bytes 442376 | tf_op jit(solution)/shard_map/ppermute | solution.py:11
  6.5 9.7 %collective-permute-start = (bf16[64,1152]{1,0:T(8,128)(2,1)S(1)}, bf16[64,1152]{1,0:T(8,128)(2,1)S(1)}, u32[]{:S(2)}, u32[]{:S(2)}) collective-permute-start(bf16[64,1152]{1,0:T(8,128)(2,1)S(1)} %get-tuple-element.7), channel_id=1, source_target_pairs={{0,8},{1,9},{2,10},{3,11},{4,12},{5,13},{6,14},{7,15},{8,0},{9,1},... | collective-permute-start | bytes 442376 | tf_op jit(solution)/shard_map/ppermute | solution.py:11
  9.4 24.3 %collective-permute-start.7 = (bf16[64,1152]{1,0:T(8,128)(2,1)S(1)}, bf16[64,1152]{1,0:T(8,128)(2,1)S(1)}, u32[]{:S(2)}, u32[]{:S(2)}) collective-permute-start(bf16[64,1152]{1,0:T(8,128)(2,1)S(1)} %get-tuple-element.7), channel_id=1, source_target_pairs={{0,1},{1,0},{2,3},{3,2},{4,5},{5,4},{6,7},{7,6},{8,9},{9,8},{10,11... | collective-permute-start | bytes 442376 | tf_op jit(solution)/shard_map/ppermute | solution.py:11
  10.2 25.5 %collective-permute-start.11 = (bf16[64,1152]{1,0:T(8,128)(2,1)S(1)}, bf16[64,1152]{1,0:T(8,128)(2,1)S(1)}, u32[]{:S(2)}, u32[]{:S(2)}) collective-permute-start(bf16[64,1152]{1,0:T(8,128)(2,1)S(1)} %collective-permute-done.3), channel_id=1, source_target_pairs={{0,1},{1,0},{2,3},{3,2},{4,5},{5,4},{6,7},{7,6},{8,9},{9,8},{10,11... | collective-permute-start | bytes 442376 | tf_op jit(solution)/shard_map/ppermute | solution.py:11
  12.9 22.8 %collective-permute-start.10 = (bf16[64,1152]{1,0:T(8,128)(2,1)S(1)}, bf16[64,1152]{1,0:T(8,128)(2,1)S(1)}, u32[]{:S(2)}, u32[]{:S(2)}) collective-permute-start(bf16[64,1152]{1,0:T(8,128)(2,1)S(1)} %collective-permute-done.2), channel_id=1, source_target_pairs={{0,1},{1,0},{2,3},{3,2},{4,5},{5,4},{6,7},{7,6},{8,9},{9,8},{10,11... | collective-permute-start | bytes 442376 | tf_op jit(solution)/shard_map/ppermute | solution.py:11
  16.2 19.0 %collective-permute-start.9 = (bf16[64,1152]{1,0:T(8,128)(2,1)S(1)}, bf16[64,1152]{1,0:T(8,128)(2,1)S(1)}, u32[]{:S(2)}, u32[]{:S(2)}) collective-permute-start(bf16[64,1152]{1,0:T(8,128)(2,1)S(1)} %collective-permute-done.1), channel_id=1, source_target_pairs={{0,1},{1,0},{2,3},{3,2},{4,5},{5,4},{6,7},{7,6},{8,9},{9,8},{10,11... | collective-permute-start | bytes 442376 | tf_op jit(solution)/shard_map/ppermute | solution.py:11
  16.2 6.3 %collective-permute-start.4 = (bf16[64,1152]{1,0:T(8,128)(2,1)S(1)}, bf16[64,1152]{1,0:T(8,128)(2,1)S(1)}, u32[]{:S(2)}, u32[]{:S(2)}) collective-permute-start(bf16[64,1152]{1,0:T(8,128)(2,1)S(1)} %collective-permute-done), channel_id=1, source_target_pairs={{0,4},{1,5},{2,6},{3,7},{4,0},{5,1},{6,2},{7,3},{8,12},{9,13},{10,... | collective-permute-start | bytes 442376 | tf_op jit(solution)/shard_map/ppermute | solution.py:11
  22.5 5.1 %collective-permute-start.5 = (bf16[64,1152]{1,0:T(8,128)(2,1)S(1)}, bf16[64,1152]{1,0:T(8,128)(2,1)S(1)}, u32[]{:S(2)}, u32[]{:S(2)}) collective-permute-start(bf16[64,1152]{1,0:T(8,128)(2,1)S(1)} %collective-permute-done), channel_id=1, source_target_pairs={{0,2},{1,3},{2,0},{3,1},{4,6},{5,7},{6,4},{7,5},{8,10},{9,11},{10,... | collective-permute-start | bytes 442376 | tf_op jit(solution)/shard_map/ppermute | solution.py:11
  27.6 6.0 %collective-permute-start.6 = (bf16[64,1152]{1,0:T(8,128)(2,1)S(1)}, bf16[64,1152]{1,0:T(8,128)(2,1)S(1)}, u32[]{:S(2)}, u32[]{:S(2)}) collective-permute-start(bf16[64,1152]{1,0:T(8,128)(2,1)S(1)} %collective-permute-done), channel_id=1, source_target_pairs={{0,6},{1,7},{2,4},{3,5},{4,2},{5,3},{6,0},{7,1},{8,14},{9,15},{10,... | collective-permute-start | bytes 442376 | tf_op jit(solution)/shard_map/ppermute | solution.py:11
  33.7 1.4 %collective-permute-start.8 = (bf16[64,1152]{1,0:T(8,128)(2,1)S(1)}, bf16[64,1152]{1,0:T(8,128)(2,1)S(1)}, u32[]{:S(2)}, u32[]{:S(2)}) collective-permute-start(bf16[64,1152]{1,0:T(8,128)(2,1)S(1)} %collective-permute-done), channel_id=1, source_target_pairs={{0,1},{1,0},{2,3},{3,2},{4,5},{5,4},{6,7},{7,6},{8,9},{9,8},{10,11... | collective-permute-start | bytes 442376 | tf_op jit(solution)/shard_map/ppermute | solution.py:11
  33.7 3.0 %collective-permute-start.14 = (bf16[64,1152]{1,0:T(8,128)(2,1)S(1)}, bf16[64,1152]{1,0:T(8,128)(2,1)S(1)}, u32[]{:S(2)}, u32[]{:S(2)}) collective-permute-start(bf16[64,1152]{1,0:T(8,128)(2,1)S(1)} %collective-permute-done.6), channel_id=1, source_target_pairs={{0,1},{1,0},{2,3},{3,2},{4,5},{5,4},{6,7},{7,6},{8,9},{9,8},{10,11... | collective-permute-start | bytes 442376 | tf_op jit(solution)/shard_map/ppermute | solution.py:11
  35.0 1.6 %collective-permute-start.13 = (bf16[64,1152]{1,0:T(8,128)(2,1)S(1)}, bf16[64,1152]{1,0:T(8,128)(2,1)S(1)}, u32[]{:S(2)}, u32[]{:S(2)}) collective-permute-start(bf16[64,1152]{1,0:T(8,128)(2,1)S(1)} %collective-permute-done.5), channel_id=1, source_target_pairs={{0,1},{1,0},{2,3},{3,2},{4,5},{5,4},{6,7},{7,6},{8,9},{9,8},{10,11... | collective-permute-start | bytes 442376 | tf_op jit(solution)/shard_map/ppermute | solution.py:11
  35.2 1.4 %collective-permute-start.12 = (bf16[64,1152]{1,0:T(8,128)(2,1)S(1)}, bf16[64,1152]{1,0:T(8,128)(2,1)S(1)}, u32[]{:S(2)}, u32[]{:S(2)}) collective-permute-start(bf16[64,1152]{1,0:T(8,128)(2,1)S(1)} %collective-permute-done.4), channel_id=1, source_target_pairs={{0,1},{1,0},{2,3},{3,2},{4,5},{5,4},{6,7},{7,6},{8,9},{9,8},{10,11... | collective-permute-start | bytes 442376 | tf_op jit(solution)/shard_map/ppermute | solution.py:11
  39.6 1.0 %copy-start.1 = (f32[1024,128]{1,0:T(8,128)S(1)}, f32[1024,128]{1,0:T(8,128)}, u32[]{:S(2)}) copy-start(f32[1024,128]{1,0:T(8,128)} %param.9) | copy-start | bytes 1572868
  39.6 1.2 %copy-start.2 = (f32[1024,128]{1,0:T(8,128)S(1)}, f32[1024,128]{1,0:T(8,128)}, u32[]{:S(2)}) copy-start(f32[1024,128]{1,0:T(8,128)} %param.8) | copy-start | bytes 1572868
  42.0 1.2 %collective-permute-start.15 = (f32[1,128]{1,0:T(1,128)S(1)}, f32[1,128]{1,0:T(1,128)S(1)}, u32[]{:S(2)}, u32[]{:S(2)}) collective-permute-start(f32[1,128]{1,0:T(1,128)S(1)} %bitcast.5), channel_id=1, source_target_pairs={{0,1},{1,0},{2,3},{3,2},{4,5},{5,4},{6,7},{7,6},{8,9},{9,8},{10,11... | collective-permute-start | bytes 1544 | tf_op jit(solution)/shard_map/ppermute | solution.py:11
  43.3 3.5 %collective-permute-start.16 = (f32[1,128]{1,0:T(1,128)S(1)}, f32[1,128]{1,0:T(1,128)S(1)}, u32[]{:S(2)}, u32[]{:S(2)}) collective-permute-start(f32[1,128]{1,0:T(1,128)S(1)} %bitcast_add_fusion), channel_id=1, source_target_pairs={{0,2},{1,3},{2,0},{3,1},{4,6},{5,7},{6,4},{7,5},{8,10},{9,11},{10,... | collective-permute-start | bytes 1544 | tf_op jit(solution)/shard_map/ppermute | solution.py:11
  46.8 3.5 %collective-permute-start.17 = (f32[1,128]{1,0:T(1,128)S(1)}, f32[1,128]{1,0:T(1,128)S(1)}, u32[]{:S(2)}, u32[]{:S(2)}) collective-permute-start(f32[1,128]{1,0:T(1,128)S(1)} %add.19), channel_id=1, source_target_pairs={{0,4},{1,5},{2,6},{3,7},{4,0},{5,1},{6,2},{7,3},{8,12},{9,13},{10,... | collective-permute-start | bytes 1544 | tf_op jit(solution)/shard_map/ppermute | solution.py:11
  50.4 4.4 %collective-permute-start.18 = (f32[1,128]{1,0:T(1,128)S(1)}, f32[1,128]{1,0:T(1,128)S(1)}, u32[]{:S(2)}, u32[]{:S(2)}) collective-permute-start(f32[1,128]{1,0:T(1,128)S(1)} %add.20), channel_id=1, source_target_pairs={{0,8},{1,9},{2,10},{3,11},{4,12},{5,13},{6,14},{7,15},{8,0},{9,1},... | collective-permute-start | bytes 1544 | tf_op jit(solution)/shard_map/ppermute | solution.py:11

commit v2 on v1

v2 whole, which is shorter than its diff:
```python
import functools
import math

import jax
import jax.numpy as jnp
from jax import lax
from jax.experimental import pallas as pl
from jax.experimental.pallas import tpu as pltpu
from jax.sharding import PartitionSpec as P

VMEM = pl.BlockSpec(memory_space=pltpu.VMEM)
ANYWHERE = pl.BlockSpec(memory_space=pl.ANY)


def swap(x, bits):
    n = lax.axis_size("tgt")
    return lax.ppermute(x, "tgt", [(i, i ^ bits) for i in range(n)])


def total(x):
    n = lax.axis_size("tgt")
    if n & (n - 1):
        return lax.psum(x, "tgt")
    bit = 1
    while bit < n:
        x = x + swap(x, bit)
        bit *= 2
    return x


def pack_kernel(feats_ref, vecs_ref, out_ref, sems):
    width = feats_ref.shape[1]
    first = pltpu.make_async_copy(feats_ref, out_ref.at[:, :width], sems.at[0])
    second = pltpu.make_async_copy(vecs_ref, out_ref.at[:, width:], sems.at[1])
    first.start()
    second.start()
    first.wait()
    second.wait()


def pack(feats, vecs):
    rows, width = feats.shape
    return pl.pallas_call(
        pack_kernel,
        out_shape=jax.ShapeDtypeStruct((rows, width + vecs.shape[1]), feats.dtype),
        in_specs=[ANYWHERE] * 2,
        out_specs=VMEM,
        scratch_shapes=[pltpu.SemaphoreType.DMA((2,))],
        compiler_params=pltpu.CompilerParams(vmem_limit_bytes=4 * 2**20),
    )(feats, vecs)


def block(target, packed, scale):
    width = target.shape[1]
    feats = packed[:, :width]
    return lax.dot_general(target, feats, (((1,), (1,)), ((), ())), preferred_element_type=jnp.float32) * scale


def square_sums(packed, width, scale):
    feats = packed[:, :width].astype(jnp.float32)
    square = feats * feats
    high = square.astype(jnp.bfloat16)
    low = (square - high.astype(jnp.float32)).astype(jnp.bfloat16)
    ones = jnp.ones((8, width), jnp.bfloat16)
    over = functools.partial(
        lax.dot_general, dimension_numbers=(((1,), (1,)), ((), ())), preferred_element_type=jnp.float32
    )
    return (over(ones, high) + over(ones, low))[:1] * (0.5 * scale)


def first_kernel(tile, scale, count, target_ref, *refs):
    packed_refs, (top_ref, denom_ref, numer_ref) = refs[:count], refs[count:]
    width = target_ref.shape[1]
    packed = jnp.concatenate([r[...] for r in packed_refs], axis=0)
    offset = square_sums(packed, width, scale)
    vecs = packed[:, width:]
    for at in range(0, target_ref.shape[0], tile):
        rows = pl.ds(at, tile)
        scores = block(target_ref[rows, :], packed, scale) - offset
        top = jnp.max(scores, axis=1, keepdims=True)
        weights = jnp.exp2(scores - top)
        top_ref[rows, :] = jnp.broadcast_to(top, (tile, top_ref.shape[1]))
        denom_ref[rows, :] = jnp.broadcast_to(jnp.sum(weights, axis=1, keepdims=True), (tile, denom_ref.shape[1]))
        numer_ref[rows, :] = jnp.dot(weights.astype(jnp.bfloat16), vecs, preferred_element_type=jnp.float32)


def last_kernel(tile, scale, count, target_ref, top_ref, denom_ref, numer_ref, current_ref, previous_ref, *refs):
    packed_refs, (next_ref, column_ref) = refs[:count], refs[count:]
    width = target_ref.shape[1]
    packed = jnp.concatenate([r[...] for r in packed_refs], axis=0)
    offset = square_sums(packed, width, scale)
    vecs = packed[:, width:]
    column = jnp.zeros((8, vecs.shape[1]), jnp.float32)
    for at in range(0, target_ref.shape[0], tile):
        rows = pl.ds(at, tile)
        scores = block(target_ref[rows, :], packed, scale) - offset
        before = top_ref[rows, :1]
        top = jnp.maximum(before, jnp.max(scores, axis=1, keepdims=True))
        weights = jnp.exp2(scores - top)
        shrink = jnp.exp2(before - top)
        denom = shrink * denom_ref[rows, :1] + jnp.sum(weights, axis=1, keepdims=True)
        numer = shrink * numer_ref[rows, :] + jnp.dot(
            weights.astype(jnp.bfloat16), vecs, preferred_element_type=jnp.float32
        )
        step = 2.0 / 0.05 * (numer / denom - 0.01 * current_ref[rows, :]) - previous_ref[rows, :]
        next_ref[rows, :] = step
        column = column + jnp.sum((step * step).reshape(tile // 8, 8, -1), axis=0)
    column_ref[...] = jnp.sum(column, axis=0, keepdims=True)


def cost(rows, width, cols, sources):
    return pl.CostEstimate(
        flops=2 * rows * sources * (width + cols), bytes_accessed=2 * rows * width, transcendentals=rows * sources
    )


def first_part(target, pieces, scale):
    rows, width = target.shape
    cols = pieces[0].shape[1] - width
    sources = sum(p.shape[0] for p in pieces)
    return pl.pallas_call(
        functools.partial(first_kernel, min(rows, 256), scale, len(pieces)),
        out_shape=[jax.ShapeDtypeStruct((rows, cols), jnp.float32)] * 3,
        in_specs=[VMEM] * (1 + len(pieces)),
        out_specs=[VMEM] * 3,
        compiler_params=pltpu.CompilerParams(vmem_limit_bytes=20 * 2**20),
        cost_estimate=cost(rows, width, cols, sources),
    )(target, *pieces)


def last_part(target, state, current, previous, pieces, scale):
    rows, width = target.shape
    cols = current.shape[1]
    sources = sum(p.shape[0] for p in pieces)
    return pl.pallas_call(
        functools.partial(last_kernel, min(rows, 256), scale, len(pieces)),
        out_shape=[jax.ShapeDtypeStruct((rows, cols), jnp.float32), jax.ShapeDtypeStruct((1, cols), jnp.float32)],
        in_specs=[VMEM] * (6 + len(pieces)),
        out_specs=[VMEM] * 2,
        compiler_params=pltpu.CompilerParams(vmem_limit_bytes=20 * 2**20),
        cost_estimate=cost(rows, width, cols, sources),
    )(target, *state, current, previous, *pieces)


def gather(shard):
    n = lax.axis_size("tgt")
    if n & (n - 1) or n < 16:
        everything = lax.all_gather(shard, "tgt", axis=0, tiled=True)
        half = everything.shape[0] // 2
        return [everything[:half]], [everything[half:]]
    near, bit = shard, n // 2
    while bit > 8:
        near = jnp.concatenate([near, swap(near, bit)], axis=0)
        bit //= 2
    far = swap(near, bit)
    around = [swap(near, k) for k in (4, 2, 6)]
    beyond = [swap(far, k) for k in (4, 2, 6)]
    early = [near] + around + [far]
    early = early + [swap(x, 1) for x in early]
    late = beyond + [swap(x, 1) for x in beyond]
    return early, late


def on_device(target_features, source_features, vectors, current, previous):
    rows, width = target_features.shape
    gamma = 0.25 / math.sqrt(width)
    scale = 2.0 * gamma * math.log2(math.e)
    early, late = gather(pack(source_features, vectors))
    state = first_part(target_features, early, scale)
    next_iter, column = last_part(target_features, state, current, previous, late, scale)
    column_sq = total(column)
    total_rows = rows * lax.axis_size("tgt")
    return next_iter / jnp.sqrt(column_sq / total_rows + 1e-06)


def solution(mesh):
    return jax.shard_map(
        on_device,
        mesh=mesh,
        in_specs=(P(("groups", "tgt"), None),) * 5,
        out_specs=P(("groups", "tgt"), None),
        check_vma=False,
    )
```

time: 55.9 us -> 49.3 us (0.88)
  waiting for transfers between devices: 29.2 us -> 20.2 us
  Pallas kernels: 0 us -> 7.81 us
  matrix products: 3.59 us -> 0 us
  other arithmetic: 2.23 us -> 0.86 us
  starting transfers between devices: 18.1 us -> 16.9 us
  local copies, waits for them, and re-layouts: 2.38 us -> 3.22 us
    ppermute x19, waiting for transfers between devices: 29.2 us -> 20.2 us  [swap(): return lax.ppermute(x, 'tgt', [(i, i ^ bits) for i in range(n)])]
    pallas_call x0 -> x3, Pallas kernels: none -> 7.81 us  [the longest x1 4.31 us: first_part(): pl.pallas_call(functools.partial(first_kernel, min(rows, 256), scale, len...]
    dot_general x2 -> x0, matrix products: 3.59 us -> none  [the longest x1 2.39 us: block_scores(): jnp.einsum('td,sd->ts', target_features, feats, preferred_element_type=jn...]
    unnamed x21 -> x12, local copies, waits for them, and re-layouts: 1.63 us -> 3.22 us
    reduce_sum x2 -> x0, other arithmetic: 1.36 us -> none  [the longest x1 0.89 us: on_device(): denominator = jnp.sum(weights, axis=1, keepdims=True)]
    ppermute x19, starting transfers between devices: 18.1 us -> 16.9 us  [swap(): return lax.ppermute(x, 'tgt', [(i, i ^ bits) for i in range(n)])]
    concatenate x2 -> x0, local copies, waits for them, and re-layouts: 0.75 us -> none  [the longest x1 0.73 us: on_device(): everything = gather(jnp.concatenate([source_features, vectors], axis=1))]
  transfers between devices with their start and end apart: 19 -> 19, of which waited for: 12 -> 8; matrix products, arithmetic and copies ran while one was open for 0% -> 0% of each run, Pallas kernels for 0% -> 9%
where the time goes in v2:
time: 49.3 us; the launch traced here: 49.1 us
  waiting for transfers between devices  20.2 us (41%)
  starting transfers between devices  16.9 us (34%)
  Pallas kernels  7.81 us (16%)
  local copies, waits for them, and re-layouts  3.22 us (7%)
  other arithmetic  0.86 us (2%)
    ppermute x19, waiting for transfers between devices, swap(): return lax.ppermute(x, 'tgt', [(i, i ^ bits) for i in range(n)])  20.2 us
    ppermute x19, starting transfers between devices, swap(): return lax.ppermute(x, 'tgt', [(i, i ^ bits) for i in range(n)])  16.9 us
    pallas_call x1, Pallas kernels, first_part(): pl.pallas_call(functools.partial(first_kernel, min(rows, 256), scale, len...  4.31 us
    pallas_call x1, Pallas kernels, last_part(): pl.pallas_call(functools.partial(last_kernel, min(rows, 256), scale, len(...  3.46 us
    unnamed x12, local copies, waits for them, and re-layouts  3.22 us
  transfers between devices with their start and end apart: 19, of which 8 were waited for; matrix products, arithmetic and copies ran while one was open for 0% of the time, Pallas kernels for 9%

profile of v2, /device:TPU:0, one launch (start us, length us, event | category | flops | bytes accessed | tf_op | source)
XLA Modules:
  0.0 49.1 jit_solution(7479566077133020673)
XLA Ops:
  0.0 0.0 copy-start.4
  0.0 0.9 %copy-done.4 = bf16[64,1024]{1,0:T(8,128)(2,1)S(1)} copy-done((bf16[64,1024]{1,0:T(8,128)(2,1)S(1)}, bf16[64,1024]{1,0:T(8,128)(2,1)}, u32[]{:S(2)}) %copy-start.4) | copy-done | bytes 131096
  0.9 0.7 %copy-done.5 = bf16[64,128]{1,0:T(8,128)(2,1)S(1)} copy-done((bf16[64,128]{1,0:T(8,128)(2,1)S(1)}, bf16[64,128]{1,0:T(8,128)(2,1)}, u32[]{:S(2)}) %copy-start.5) | copy-done | bytes 16408
  1.7 4.1 %collective-permute-start.3 = (bf16[64,1152]{1,0:T(8,128)(2,1)S(1)}, bf16[64,1152]{1,0:T(8,128)(2,1)S(1)}, u32[]{:S(2)}, u32[]{:S(2)}) collective-permute-start(bf16[64,1152]{1,0:T(8,128)(2,1)S(1)} %shard_map.55.refs_0_), channel_id=1, source_target_pairs={{0,8},{1,9},{2,10},{3,11},{4,12},{5,13},{6,14},{7,15},{8,0},{9,1},... | collective-permute-start | bytes 442376 | tf_op jit(solution)/shard_map/ppermute | solution.py:17
  5.8 1.6 %collective-permute-start = (bf16[64,1152]{1,0:T(8,128)(2,1)S(1)}, bf16[64,1152]{1,0:T(8,128)(2,1)S(1)}, u32[]{:S(2)}, u32[]{:S(2)}) collective-permute-start(bf16[64,1152]{1,0:T(8,128)(2,1)S(1)} %shard_map.55.refs_0_), channel_id=1, source_target_pairs={{0,4},{1,5},{2,6},{3,7},{4,0},{5,1},{6,2},{7,3},{8,12},{9,13},{10,... | collective-permute-start | bytes 442376 | tf_op jit(solution)/shard_map/ppermute | solution.py:17
  7.4 1.5 %collective-permute-start.1 = (bf16[64,1152]{1,0:T(8,128)(2,1)S(1)}, bf16[64,1152]{1,0:T(8,128)(2,1)S(1)}, u32[]{:S(2)}, u32[]{:S(2)}) collective-permute-start(bf16[64,1152]{1,0:T(8,128)(2,1)S(1)} %shard_map.55.refs_0_), channel_id=1, source_target_pairs={{0,2},{1,3},{2,0},{3,1},{4,6},{5,7},{6,4},{7,5},{8,10},{9,11},{10,... | collective-permute-start | bytes 442376 | tf_op jit(solution)/shard_map/ppermute | solution.py:17
  8.9 0.4 collective-permute-start.2
  9.3 0.0 collective-permute-start.4
  9.3 3.6 %collective-permute-done.3.refs_4_ = bf16[64,1152]{1,0:T(8,128)(2,1)S(1)} collective-permute-done((bf16[64,1152]{1,0:T(8,128)(2,1)S(1)}, bf16[64,1152]{1,0:T(8,128)(2,1)S(1)}, u32[]{:S(2)}, u32[]{:S(2)}) %collective-permute-start.3) | collective-permute-done | bytes 147488 | tf_op jit(solution)/shard_map/ppermute | solution.py:17
  12.9 0.0 collective-permute-start.8
  12.9 1.2 %collective-permute-done.refs_1_ = bf16[64,1152]{1,0:T(8,128)(2,1)S(1)} collective-permute-done((bf16[64,1152]{1,0:T(8,128)(2,1)S(1)}, bf16[64,1152]{1,0:T(8,128)(2,1)S(1)}, u32[]{:S(2)}, u32[]{:S(2)}) %collective-permute-start) | collective-permute-done | bytes 147488 | tf_op jit(solution)/shard_map/ppermute | solution.py:17
  14.1 0.0 collective-permute-start.5
  14.1 0.0 collective-permute-done.1.refs_2_
  14.1 1.6 %collective-permute-start.9 = (bf16[64,1152]{1,0:T(8,128)(2,1)S(1)}, bf16[64,1152]{1,0:T(8,128)(2,1)S(1)}, u32[]{:S(2)}, u32[]{:S(2)}) collective-permute-start(bf16[64,1152]{1,0:T(8,128)(2,1)S(1)} %collective-permute-done.3.refs_4_), channel_id=1, source_target_pairs={{0,4},{1,5},{2,6},{3,7},{4,0},{5,1},{6,2},{7,3},{8,12},{9,13},{10,... | collective-permute-start | bytes 442376 | tf_op jit(solution)/shard_map/ppermute | solution.py:17
  15.7 1.5 %collective-permute-done.2.refs_3_ = bf16[64,1152]{1,0:T(8,128)(2,1)S(1)} collective-permute-done((bf16[64,1152]{1,0:T(8,128)(2,1)S(1)}, bf16[64,1152]{1,0:T(8,128)(2,1)S(1)}, u32[]{:S(2)}, u32[]{:S(2)}) %collective-permute-start.2) | collective-permute-done | bytes 147488 | tf_op jit(solution)/shard_map/ppermute | solution.py:17
  17.2 0.5 collective-permute-start.10
  17.7 0.0 collective-permute-done.4.refs_5_
  17.7 2.4 %collective-permute-start.11 = (bf16[64,1152]{1,0:T(8,128)(2,1)S(1)}, bf16[64,1152]{1,0:T(8,128)(2,1)S(1)}, u32[]{:S(2)}, u32[]{:S(2)}) collective-permute-start(bf16[64,1152]{1,0:T(8,128)(2,1)S(1)} %collective-permute-done.3.refs_4_), channel_id=1, source_target_pairs={{0,6},{1,7},{2,4},{3,5},{4,2},{5,3},{6,0},{7,1},{8,14},{9,15},{10,... | collective-permute-start | bytes 442376 | tf_op jit(solution)/shard_map/ppermute | solution.py:17
  20.2 0.0 collective-permute-done.8.refs_9_
  20.2 0.0 collective-permute-start.6
  20.2 0.0 collective-permute-done.5.refs_6_
  20.2 0.5 %collective-permute-start.7 = (bf16[64,1152]{1,0:T(8,128)(2,1)S(1)}, bf16[64,1152]{1,0:T(8,128)(2,1)S(1)}, u32[]{:S(2)}, u32[]{:S(2)}) collective-permute-start(bf16[64,1152]{1,0:T(8,128)(2,1)S(1)} %collective-permute-done.2.refs_3_), channel_id=1, source_target_pairs={{0,1},{1,0},{2,3},{3,2},{4,5},{5,4},{6,7},{7,6},{8,9},{9,8},{10,11... | collective-permute-start | bytes 442376 | tf_op jit(solution)/shard_map/ppermute | solution.py:17
  20.7 0.0 collective-permute-done.9.refs_0_
  20.7 0.1 collective-permute-start.12
  20.7 4.8 %collective-permute-done.10.refs_1_ = bf16[64,1152]{1,0:T(8,128)(2,1)S(1)} collective-permute-done((bf16[64,1152]{1,0:T(8,128)(2,1)S(1)}, bf16[64,1152]{1,0:T(8,128)(2,1)S(1)}, u32[]{:S(2)}, u32[]{:S(2)}) %collective-permute-start.10) | collective-permute-done | bytes 147488 | tf_op jit(solution)/shard_map/ppermute | solution.py:17
  25.6 0.0 collective-permute-start.13
  25.6 0.0 collective-permute-done.11.refs_2_
  25.6 0.5 %collective-permute-start.14 = (bf16[64,1152]{1,0:T(8,128)(2,1)S(1)}, bf16[64,1152]{1,0:T(8,128)(2,1)S(1)}, u32[]{:S(2)}, u32[]{:S(2)}) collective-permute-start(bf16[64,1152]{1,0:T(8,128)(2,1)S(1)} %collective-permute-done.11.refs_2_), channel_id=1, source_target_pairs={{0,1},{1,0},{2,3},{3,2},{4,5},{5,4},{6,7},{7,6},{8,9},{9,8},{10,11... | collective-permute-start | bytes 442376 | tf_op jit(solution)/shard_map/ppermute | solution.py:17
  26.1 0.0 collective-permute-done.6.refs_7_
  26.1 0.0 collective-permute-done.7.refs_8_
  26.1 1.6 %copy-done = bf16[1024,1024]{1,0:T(8,128)(2,1)S(1)} copy-done((bf16[1024,1024]{1,0:T(8,128)(2,1)S(1)}, bf16[1024,1024]{1,0:T(8,128)(2,1)}, u32[]{:S(2)}) %copy-start) | copy-done | bytes 2097176
  27.7 4.3 %shard_map.56 = (f32[1024,128]{1,0:T(8,128)S(1)}, f32[1024,128]{1,0:T(8,128)S(1)}, f32[1024,128]{1,0:T(8,128)S(1)}) custom-call(bf16[1024,1024]{1,0:T(8,128)(2,1)S(1)} %copy-done, bf16[64,1152]{1,0:T(8,128)(2,1)S(1)} %shard_map.55.refs_0_, bf16[64,1152]{1,0:T(8,128)(2,1)S(1)} %collective-permute-done.refs_1_, ...), custom_call_target="tpu_custom_call" | custom-call | flops 1509949440 | bytes 2097152 | tf_op jit(solution)/shard_map/pallas_call | solution.py:121
  32.0 0.0 collective-permute-done.12.refs_3_
  32.0 0.0 collective-permute-done.13.refs_4_
  32.0 0.0 collective-permute-done.14.refs_5_
  32.0 0.0 copy-done.1
  32.0 0.0 copy-done.2
  32.0 0.0 copy-done.3
  32.0 3.5 %shard_map.57 = (f32[1024,128]{1,0:T(8,128)S(1)}, f32[1,128]{1,0:T(1,128)S(1)}) custom-call(bf16[1024,1024]{1,0:T(8,128)(2,1)S(1)} %copy-done.1, f32[1024,128]{1,0:T(8,128)S(1)} %get-tuple-element.10.top_ref, f32[1024,128]{1,0:T(8,128)S(1)} %get-tuple-element.11.denom_ref, f32[1024,128]{1,0:T(8,128)S(1)} %get-tuple-element.12.numer_ref, ...), custom_call_target="tpu_custom_call" | custom-call | flops 905969664 | bytes 2097152 | tf_op jit(solution)/shard_map/pallas_call | solution.py:135
  35.5 0.1 collective-permute-start.15
  35.6 1.1 %collective-permute-done.15 = f32[1,128]{1,0:T(1,128)S(1)} collective-permute-done((f32[1,128]{1,0:T(1,128)S(1)}, f32[1,128]{1,0:T(1,128)S(1)}, u32[]{:S(2)}, u32[]{:S(2)}) %collective-permute-start.15) | collective-permute-done | bytes 544 | tf_op jit(solution)/shard_map/ppermute | solution.py:17
  36.7 0.8 %collective-permute-start.16 = (f32[1,128]{1,0:T(1,128)S(1)}, f32[1,128]{1,0:T(1,128)S(1)}, u32[]{:S(2)}, u32[]{:S(2)}) collective-permute-start(f32[1,128]{1,0:T(1,128)S(1)} %add.18), channel_id=1, source_target_pairs={{0,2},{1,3},{2,0},{3,1},{4,6},{5,7},{6,4},{7,5},{8,10},{9,11},{10,... | collective-permute-start | bytes 1544 | tf_op jit(solution)/shard_map/ppermute | solution.py:17
  37.5 2.7 %collective-permute-done.16 = f32[1,128]{1,0:T(1,128)S(1)} collective-permute-done((f32[1,128]{1,0:T(1,128)S(1)}, f32[1,128]{1,0:T(1,128)S(1)}, u32[]{:S(2)}, u32[]{:S(2)}) %collective-permute-start.16) | collective-permute-done | bytes 544 | tf_op jit(solution)/shard_map/ppermute | solution.py:17
  40.3 1.4 %collective-permute-start.17 = (f32[1,128]{1,0:T(1,128)S(1)}, f32[1,128]{1,0:T(1,128)S(1)}, u32[]{:S(2)}, u32[]{:S(2)}) collective-permute-start(f32[1,128]{1,0:T(1,128)S(1)} %add.19), channel_id=1, source_target_pairs={{0,4},{1,5},{2,6},{3,7},{4,0},{5,1},{6,2},{7,3},{8,12},{9,13},{10,... | collective-permute-start | bytes 1544 | tf_op jit(solution)/shard_map/ppermute | solution.py:17
  41.7 2.1 %collective-permute-done.17 = f32[1,128]{1,0:T(1,128)S(1)} collective-permute-done((f32[1,128]{1,0:T(1,128)S(1)}, f32[1,128]{1,0:T(1,128)S(1)}, u32[]{:S(2)}, u32[]{:S(2)}) %collective-permute-start.17) | collective-permute-done | bytes 544 | tf_op jit(solution)/shard_map/ppermute | solution.py:17
  43.8 1.3 %collective-permute-start.18 = (f32[1,128]{1,0:T(1,128)S(1)}, f32[1,128]{1,0:T(1,128)S(1)}, u32[]{:S(2)}, u32[]{:S(2)}) collective-permute-start(f32[1,128]{1,0:T(1,128)S(1)} %add.20), channel_id=1, source_target_pairs={{0,8},{1,9},{2,10},{3,11},{4,12},{5,13},{6,14},{7,15},{8,0},{9,1},... | collective-permute-start | bytes 1544 | tf_op jit(solution)/shard_map/ppermute | solution.py:17
  45.1 3.1 %collective-permute-done.18 = f32[1,128]{1,0:T(1,128)S(1)} collective-permute-done((f32[1,128]{1,0:T(1,128)S(1)}, f32[1,128]{1,0:T(1,128)S(1)}, u32[]{:S(2)}, u32[]{:S(2)}) %collective-permute-start.18) | collective-permute-done | bytes 544 | tf_op jit(solution)/shard_map/ppermute | solution.py:17
  48.2 0.8 %broadcast_divide_fusion = f32[1024,128]{1,0:T(8,128)} fusion(f32[1024,128]{1,0:T(8,128)S(1)} %get-tuple-element.13, f32[128]{0:T(128)S(1)} %sqrt_bitcast_fusion), kind=kLoop, calls=%fused_computation | loop fusion | flops 131072 | bytes 1049088 | tf_op jit(solution)/shard_map/div | solution.py:173
  (10 shorter events, 0.1 us)
Async XLA Ops:
  0.0 0.9 %copy-start.4 = (bf16[64,1024]{1,0:T(8,128)(2,1)S(1)}, bf16[64,1024]{1,0:T(8,128)(2,1)}, u32[]{:S(2)}) copy-start(bf16[64,1024]{1,0:T(8,128)(2,1)} %feats_ref.1) | copy-start | bytes 393220
  0.9 0.7 %copy-start.5 = (bf16[64,128]{1,0:T(8,128)(2,1)S(1)}, bf16[64,128]{1,0:T(8,128)(2,1)}, u32[]{:S(2)}) copy-start(bf16[64,128]{1,0:T(8,128)(2,1)} %vecs_ref.1) | copy-start | bytes 49156
  1.7 11.2 %collective-permute-start.3 = (bf16[64,1152]{1,0:T(8,128)(2,1)S(1)}, bf16[64,1152]{1,0:T(8,128)(2,1)S(1)}, u32[]{:S(2)}, u32[]{:S(2)}) collective-permute-start(bf16[64,1152]{1,0:T(8,128)(2,1)S(1)} %shard_map.55.refs_0_), channel_id=1, source_target_pairs={{0,8},{1,9},{2,10},{3,11},{4,12},{5,13},{6,14},{7,15},{8,0},{9,1},... | collective-permute-start | bytes 442376 | tf_op jit(solution)/shard_map/ppermute | solution.py:17
  5.8 8.3 %collective-permute-start = (bf16[64,1152]{1,0:T(8,128)(2,1)S(1)}, bf16[64,1152]{1,0:T(8,128)(2,1)S(1)}, u32[]{:S(2)}, u32[]{:S(2)}) collective-permute-start(bf16[64,1152]{1,0:T(8,128)(2,1)S(1)} %shard_map.55.refs_0_), channel_id=1, source_target_pairs={{0,4},{1,5},{2,6},{3,7},{4,0},{5,1},{6,2},{7,3},{8,12},{9,13},{10,... | collective-permute-start | bytes 442376 | tf_op jit(solution)/shard_map/ppermute | solution.py:17
  7.4 6.7 %collective-permute-start.1 = (bf16[64,1152]{1,0:T(8,128)(2,1)S(1)}, bf16[64,1152]{1,0:T(8,128)(2,1)S(1)}, u32[]{:S(2)}, u32[]{:S(2)}) collective-permute-start(bf16[64,1152]{1,0:T(8,128)(2,1)S(1)} %shard_map.55.refs_0_), channel_id=1, source_target_pairs={{0,2},{1,3},{2,0},{3,1},{4,6},{5,7},{6,4},{7,5},{8,10},{9,11},{10,... | collective-permute-start | bytes 442376 | tf_op jit(solution)/shard_map/ppermute | solution.py:17
  8.9 8.4 %collective-permute-start.2 = (bf16[64,1152]{1,0:T(8,128)(2,1)S(1)}, bf16[64,1152]{1,0:T(8,128)(2,1)S(1)}, u32[]{:S(2)}, u32[]{:S(2)}) collective-permute-start(bf16[64,1152]{1,0:T(8,128)(2,1)S(1)} %shard_map.55.refs_0_), channel_id=1, source_target_pairs={{0,6},{1,7},{2,4},{3,5},{4,2},{5,3},{6,0},{7,1},{8,14},{9,15},{10,... | collective-permute-start | bytes 442376 | tf_op jit(solution)/shard_map/ppermute | solution.py:17
  9.3 8.4 %collective-permute-start.4 = (bf16[64,1152]{1,0:T(8,128)(2,1)S(1)}, bf16[64,1152]{1,0:T(8,128)(2,1)S(1)}, u32[]{:S(2)}, u32[]{:S(2)}) collective-permute-start(bf16[64,1152]{1,0:T(8,128)(2,1)S(1)} %shard_map.55.refs_0_), channel_id=1, source_target_pairs={{0,1},{1,0},{2,3},{3,2},{4,5},{5,4},{6,7},{7,6},{8,9},{9,8},{10,11... | collective-permute-start | bytes 442376 | tf_op jit(solution)/shard_map/ppermute | solution.py:17
  12.9 7.3 %collective-permute-start.8 = (bf16[64,1152]{1,0:T(8,128)(2,1)S(1)}, bf16[64,1152]{1,0:T(8,128)(2,1)S(1)}, u32[]{:S(2)}, u32[]{:S(2)}) collective-permute-start(bf16[64,1152]{1,0:T(8,128)(2,1)S(1)} %collective-permute-done.3.refs_4_), channel_id=1, source_target_pairs={{0,1},{1,0},{2,3},{3,2},{4,5},{5,4},{6,7},{7,6},{8,9},{9,8},{10,11... | collective-permute-start | bytes 442376 | tf_op jit(solution)/shard_map/ppermute | solution.py:17
  14.1 6.1 %collective-permute-start.5 = (bf16[64,1152]{1,0:T(8,128)(2,1)S(1)}, bf16[64,1152]{1,0:T(8,128)(2,1)S(1)}, u32[]{:S(2)}, u32[]{:S(2)}) collective-permute-start(bf16[64,1152]{1,0:T(8,128)(2,1)S(1)} %collective-permute-done.refs_1_), channel_id=1, source_target_pairs={{0,1},{1,0},{2,3},{3,2},{4,5},{5,4},{6,7},{7,6},{8,9},{9,8},{10,11... | collective-permute-start | bytes 442376 | tf_op jit(solution)/shard_map/ppermute | solution.py:17
  14.1 6.6 %collective-permute-start.9 = (bf16[64,1152]{1,0:T(8,128)(2,1)S(1)}, bf16[64,1152]{1,0:T(8,128)(2,1)S(1)}, u32[]{:S(2)}, u32[]{:S(2)}) collective-permute-start(bf16[64,1152]{1,0:T(8,128)(2,1)S(1)} %collective-permute-done.3.refs_4_), channel_id=1, source_target_pairs={{0,4},{1,5},{2,6},{3,7},{4,0},{5,1},{6,2},{7,3},{8,12},{9,13},{10,... | collective-permute-start | bytes 442376 | tf_op jit(solution)/shard_map/ppermute | solution.py:17
  17.2 8.3 %collective-permute-start.10 = (bf16[64,1152]{1,0:T(8,128)(2,1)S(1)}, bf16[64,1152]{1,0:T(8,128)(2,1)S(1)}, u32[]{:S(2)}, u32[]{:S(2)}) collective-permute-start(bf16[64,1152]{1,0:T(8,128)(2,1)S(1)} %collective-permute-done.3.refs_4_), channel_id=1, source_target_pairs={{0,2},{1,3},{2,0},{3,1},{4,6},{5,7},{6,4},{7,5},{8,10},{9,11},{10,... | collective-permute-start | bytes 442376 | tf_op jit(solution)/shard_map/ppermute | solution.py:17
  17.7 7.8 %collective-permute-start.11 = (bf16[64,1152]{1,0:T(8,128)(2,1)S(1)}, bf16[64,1152]{1,0:T(8,128)(2,1)S(1)}, u32[]{:S(2)}, u32[]{:S(2)}) collective-permute-start(bf16[64,1152]{1,0:T(8,128)(2,1)S(1)} %collective-permute-done.3.refs_4_), channel_id=1, source_target_pairs={{0,6},{1,7},{2,4},{3,5},{4,2},{5,3},{6,0},{7,1},{8,14},{9,15},{10,... | collective-permute-start | bytes 442376 | tf_op jit(solution)/shard_map/ppermute | solution.py:17
  20.2 5.9 %collective-permute-start.6 = (bf16[64,1152]{1,0:T(8,128)(2,1)S(1)}, bf16[64,1152]{1,0:T(8,128)(2,1)S(1)}, u32[]{:S(2)}, u32[]{:S(2)}) collective-permute-start(bf16[64,1152]{1,0:T(8,128)(2,1)S(1)} %collective-permute-done.1.refs_2_), channel_id=1, source_target_pairs={{0,1},{1,0},{2,3},{3,2},{4,5},{5,4},{6,7},{7,6},{8,9},{9,8},{10,11... | collective-permute-start | bytes 442376 | tf_op jit(solution)/shard_map/ppermute | solution.py:17
  20.2 5.9 %collective-permute-start.7 = (bf16[64,1152]{1,0:T(8,128)(2,1)S(1)}, bf16[64,1152]{1,0:T(8,128)(2,1)S(1)}, u32[]{:S(2)}, u32[]{:S(2)}) collective-permute-start(bf16[64,1152]{1,0:T(8,128)(2,1)S(1)} %collective-permute-done.2.refs_3_), channel_id=1, source_target_pairs={{0,1},{1,0},{2,3},{3,2},{4,5},{5,4},{6,7},{7,6},{8,9},{9,8},{10,11... | collective-permute-start | bytes 442376 | tf_op jit(solution)/shard_map/ppermute | solution.py:17
  20.7 11.3 %collective-permute-start.12 = (bf16[64,1152]{1,0:T(8,128)(2,1)S(1)}, bf16[64,1152]{1,0:T(8,128)(2,1)S(1)}, u32[]{:S(2)}, u32[]{:S(2)}) collective-permute-start(bf16[64,1152]{1,0:T(8,128)(2,1)S(1)} %collective-permute-done.9.refs_0_), channel_id=1, source_target_pairs={{0,1},{1,0},{2,3},{3,2},{4,5},{5,4},{6,7},{7,6},{8,9},{9,8},{10,11... | collective-permute-start | bytes 442376 | tf_op jit(solution)/shard_map/ppermute | solution.py:17
  25.6 6.4 %collective-permute-start.13 = (bf16[64,1152]{1,0:T(8,128)(2,1)S(1)}, bf16[64,1152]{1,0:T(8,128)(2,1)S(1)}, u32[]{:S(2)}, u32[]{:S(2)}) collective-permute-start(bf16[64,1152]{1,0:T(8,128)(2,1)S(1)} %collective-permute-done.10.refs_1_), channel_id=1, source_target_pairs={{0,1},{1,0},{2,3},{3,2},{4,5},{5,4},{6,7},{7,6},{8,9},{9,8},{10,11... | collective-permute-start | bytes 442376 | tf_op jit(solution)/shard_map/ppermute | solution.py:17
  25.6 6.5 %collective-permute-start.14 = (bf16[64,1152]{1,0:T(8,128)(2,1)S(1)}, bf16[64,1152]{1,0:T(8,128)(2,1)S(1)}, u32[]{:S(2)}, u32[]{:S(2)}) collective-permute-start(bf16[64,1152]{1,0:T(8,128)(2,1)S(1)} %collective-permute-done.11.refs_2_), channel_id=1, source_target_pairs={{0,1},{1,0},{2,3},{3,2},{4,5},{5,4},{6,7},{7,6},{8,9},{9,8},{10,11... | collective-permute-start | bytes 442376 | tf_op jit(solution)/shard_map/ppermute | solution.py:17
  26.1 1.6 %copy-start = (bf16[1024,1024]{1,0:T(8,128)(2,1)S(1)}, bf16[1024,1024]{1,0:T(8,128)(2,1)}, u32[]{:S(2)}) copy-start(bf16[1024,1024]{1,0:T(8,128)(2,1)} %target_ref.3) | copy-start | bytes 6291460
  27.7 4.4 %copy-start.1 = (bf16[1024,1024]{1,0:T(8,128)(2,1)S(1)}, bf16[1024,1024]{1,0:T(8,128)(2,1)}, u32[]{:S(2)}) copy-start(bf16[1024,1024]{1,0:T(8,128)(2,1)} %target_ref.3) | copy-start | bytes 6291460
  27.7 4.4 %copy-start.2 = (f32[1024,128]{1,0:T(8,128)S(1)}, f32[1024,128]{1,0:T(8,128)}, u32[]{:S(2)}) copy-start(f32[1024,128]{1,0:T(8,128)} %current_ref.1) | copy-start | bytes 1572868
  27.7 4.4 %copy-start.3 = (f32[1024,128]{1,0:T(8,128)S(1)}, f32[1024,128]{1,0:T(8,128)}, u32[]{:S(2)}) copy-start(f32[1024,128]{1,0:T(8,128)} %previous_ref.1) | copy-start | bytes 1572868
  35.5 1.2 %collective-permute-start.15 = (f32[1,128]{1,0:T(1,128)S(1)}, f32[1,128]{1,0:T(1,128)S(1)}, u32[]{:S(2)}, u32[]{:S(2)}) collective-permute-start(f32[1,128]{1,0:T(1,128)S(1)} %get-tuple-element.14), channel_id=1, source_target_pairs={{0,1},{1,0},{2,3},{3,2},{4,5},{5,4},{6,7},{7,6},{8,9},{9,8},{10,11... | collective-permute-start | bytes 1544 | tf_op jit(solution)/shard_map/ppermute | solution.py:17
  36.7 3.5 %collective-permute-start.16 = (f32[1,128]{1,0:T(1,128)S(1)}, f32[1,128]{1,0:T(1,128)S(1)}, u32[]{:S(2)}, u32[]{:S(2)}) collective-permute-start(f32[1,128]{1,0:T(1,128)S(1)} %add.18), channel_id=1, source_target_pairs={{0,2},{1,3},{2,0},{3,1},{4,6},{5,7},{6,4},{7,5},{8,10},{9,11},{10,... | collective-permute-start | bytes 1544 | tf_op jit(solution)/shard_map/ppermute | solution.py:17
  40.3 3.5 %collective-permute-start.17 = (f32[1,128]{1,0:T(1,128)S(1)}, f32[1,128]{1,0:T(1,128)S(1)}, u32[]{:S(2)}, u32[]{:S(2)}) collective-permute-start(f32[1,128]{1,0:T(1,128)S(1)} %add.19), channel_id=1, source_target_pairs={{0,4},{1,5},{2,6},{3,7},{4,0},{5,1},{6,2},{7,3},{8,12},{9,13},{10,... | collective-permute-start | bytes 1544 | tf_op jit(solution)/shard_map/ppermute | solution.py:17
  43.8 4.4 %collective-permute-start.18 = (f32[1,128]{1,0:T(1,128)S(1)}, f32[1,128]{1,0:T(1,128)S(1)}, u32[]{:S(2)}, u32[]{:S(2)}) collective-permute-start(f32[1,128]{1,0:T(1,128)S(1)} %add.20), channel_id=1, source_target_pairs={{0,8},{1,9},{2,10},{3,11},{4,12},{5,13},{6,14},{7,15},{8,0},{9,1},... | collective-permute-start | bytes 1544 | tf_op jit(solution)/shard_map/ppermute | solution.py:17

commit v3 on v1

v3 whole, which is shorter than its diff:
```python
import functools
import math

import jax
import jax.numpy as jnp
from jax import lax
from jax.experimental import pallas as pl
from jax.experimental.pallas import tpu as pltpu
from jax.sharding import PartitionSpec as P

VMEM = pl.BlockSpec(memory_space=pltpu.VMEM)
SMALL = pl.CostEstimate(flops=1, bytes_accessed=1, transcendentals=0)
IN_HBM = pl.BlockSpec(memory_space=pltpu.HBM)


def hbm(x):
    return pltpu.with_memory_space_constraint(x, pltpu.HBM)


def swap(x, bits):
    n = lax.axis_size("tgt")
    return lax.ppermute(x, "tgt", [(i, i ^ bits) for i in range(n)])


def total(x):
    n = lax.axis_size("tgt")
    if n & (n - 1):
        return lax.psum(x, "tgt")
    bit = 1
    while bit < n:
        x = x + swap(x, bit)
        bit *= 2
    return x


def pack_kernel(feats_ref, vecs_ref, out_ref, sems):
    width = feats_ref.shape[1]
    first = pltpu.make_async_copy(feats_ref, out_ref.at[:, :width], sems.at[0])
    second = pltpu.make_async_copy(vecs_ref, out_ref.at[:, width:], sems.at[1])
    first.start()
    second.start()
    first.wait()
    second.wait()


def pack(feats, vecs):
    rows, width = feats.shape
    return pl.pallas_call(
        pack_kernel,
        out_shape=jax.ShapeDtypeStruct((rows, width + vecs.shape[1]), feats.dtype),
        in_specs=[IN_HBM] * 2,
        out_specs=VMEM,
        scratch_shapes=[pltpu.SemaphoreType.DMA((2,))],
        compiler_params=pltpu.CompilerParams(vmem_limit_bytes=4 * 2**20),
    )(hbm(feats), hbm(vecs))


def join_kernel(count, *refs):
    out_ref = refs[-1]
    at = 0
    for piece in refs[:count]:
        out_ref[at : at + piece.shape[0], :] = piece[...]
        at += piece.shape[0]


def joined(pieces, *tokens):
    rows = sum(p.shape[0] for p in pieces)
    return pl.pallas_call(
        functools.partial(join_kernel, len(pieces)),
        out_shape=jax.ShapeDtypeStruct((rows, pieces[0].shape[1]), pieces[0].dtype),
        in_specs=[VMEM] * len(pieces) + [pl.BlockSpec(memory_space=pl.ANY)] * len(tokens),
        out_specs=VMEM,
        compiler_params=pltpu.CompilerParams(vmem_limit_bytes=8 * 2**20),
        cost_estimate=SMALL,
    )(*pieces, *tokens)


def tie(x, *tokens):
    return joined([x], *tokens)


def load_kernel(array_ref, token_ref, out_ref, sem):
    del token_ref
    parts = sem.shape[0]
    rows = array_ref.shape[0] // parts
    copies = [
        pltpu.make_async_copy(array_ref.at[pl.ds(k * rows, rows)], out_ref.at[pl.ds(k * rows, rows)], sem.at[k])
        for k in range(parts)
    ]
    for copy in copies:
        copy.start()
    for copy in copies:
        copy.wait()


def load(array, token):
    return pl.pallas_call(
        load_kernel,
        out_shape=jax.ShapeDtypeStruct(array.shape, array.dtype),
        in_specs=[IN_HBM, pl.BlockSpec(memory_space=pl.ANY)],
        out_specs=VMEM,
        scratch_shapes=[pltpu.SemaphoreType.DMA((8 if array.shape[0] % 128 == 0 else 1,))],
        compiler_params=pltpu.CompilerParams(vmem_limit_bytes=4 * 2**20),
        cost_estimate=SMALL,
    )(hbm(array), token)


def scores_of(target, feats):
    wide = feats.astype(jnp.float32)
    square = wide * wide
    lanes = min(128, square.shape[1])
    part = square[:, :lanes]
    for at in range(lanes, square.shape[1], lanes):
        part = part + square[:, at : at + lanes]
    half = 0.5 * jnp.sum(part.T, axis=0, keepdims=True)
    dots = lax.dot_general(target, feats, (((1,), (1,)), ((), ())), preferred_element_type=jnp.float32)
    return dots - half


def step_kernel(scale, count, first, last, target_ref, *refs):
    pieces, refs = refs[:count], refs[count:]
    width = target_ref.shape[1]
    packed = jnp.concatenate([r[...] for r in pieces], axis=0)
    vecs = packed[:, width:]
    scores = scores_of(target_ref[...], packed[:, :width])
    top = jnp.max(scores, axis=1, keepdims=True)
    top = jnp.broadcast_to(top, (scores.shape[0], vecs.shape[1]))
    if not first:
        (before, denom, numer), refs = [r[...] for r in refs[:3]], refs[3:]
        top = jnp.maximum(before, top)
    across = scores.shape[1]
    level = jnp.concatenate([top] * pl.cdiv(across, top.shape[1]), axis=1)[:, :across]
    weights = jnp.exp2((scores - level) * scale)
    added = jnp.broadcast_to(jnp.sum(weights, axis=1, keepdims=True), top.shape)
    product = jnp.dot(weights.astype(jnp.bfloat16), vecs, preferred_element_type=jnp.float32)
    if not first:
        shrink = jnp.exp2((before - top) * scale)
        added = shrink * denom + added
        product = shrink * numer + product
    if not last:
        top_ref, denom_ref, numer_ref = refs
        top_ref[...] = top
        denom_ref[...] = added
        numer_ref[...] = product
        return
    current_ref, previous_ref, next_ref, column_ref = refs
    step = 2.0 / 0.05 * (product / added - 0.01 * current_ref[...]) - previous_ref[...]
    next_ref[...] = step
    column_ref[...] = jnp.sum(step * step, axis=0, keepdims=True)


def step(target, pieces, state, ends, scale):
    rows, width = target.shape
    cols = pieces[0].shape[1] - width
    whole = jax.ShapeDtypeStruct((rows, cols), jnp.float32)
    return pl.pallas_call(
        functools.partial(step_kernel, scale, len(pieces), not state, bool(ends)),
        out_shape=[whole, jax.ShapeDtypeStruct((1, cols), jnp.float32)] if ends else [whole] * 3,
        in_specs=[VMEM] * (1 + len(pieces) + len(state) + len(ends)),
        out_specs=[VMEM] * (2 if ends else 3),
        compiler_params=pltpu.CompilerParams(vmem_limit_bytes=20 * 2**20),
        cost_estimate=SMALL,
    )(target, *pieces, *state, *ends)


def gather(shard, target, scale):
    n = lax.axis_size("tgt")
    if n & (n - 1) or n < 16:
        everything = lax.all_gather(shard, "tgt", axis=0, tiled=True)
        return target, [everything], []
    near, bit = shard, n // 2
    while bit > 8:
        near = jnp.concatenate([near, swap(near, bit)], axis=0)
        bit //= 2
    near_other = swap(near, 1)
    far = swap(near, bit)
    later = tie(near, near_other)
    around = [swap(later, k) for k in (4, 2, 6)]
    target = load(target, later)
    beyond = [swap(far, k) for k in (4, 2, 6)]
    state = step(target, [near, near_other] + around + [far], [], [], scale)
    own = joined(around + [far], state[0])
    state = step(target, beyond, state, [], scale)
    return target, [swap(own, 1), swap(joined(beyond), 1)], state


def on_device(target_features, source_features, vectors, current, previous):
    rows, width = target_features.shape
    gamma = 0.25 / math.sqrt(width)
    scale = 2.0 * gamma * math.log2(math.e)
    target, pieces, state = gather(pack(source_features, vectors), target_features, scale)
    next_iter, column = step(target, pieces, state, [current, previous], scale)
    column_sq = total(column)
    total_rows = rows * lax.axis_size("tgt")
    return next_iter / jnp.sqrt(column_sq / total_rows + 1e-06)


def solution(mesh):
    return jax.shard_map(
        on_device,
        mesh=mesh,
        in_specs=(P(("groups", "tgt"), None),) * 5,
        out_specs=P(("groups", "tgt"), None),
        check_vma=False,
    )
```

time: 55.9 us -> 41.2 us (0.74)
  waiting for transfers between devices: 29.2 us -> 17 us
  Pallas kernels: 0 us -> 7.57 us
  matrix products: 3.59 us -> 0 us
  starting transfers between devices: 18.1 us -> 15.5 us
  local copies, waits for them, and re-layouts: 2.38 us -> 0.01 us
  other arithmetic: 2.23 us -> 0.86 us
    ppermute x19 -> x14, waiting for transfers between devices: 29.2 us -> 17 us  [swap(): return lax.ppermute(x, 'tgt', [(i, i ^ bits) for i in range(n)])]
    pallas_call x0 -> x8, Pallas kernels: none -> 7.57 us  [the longest x3 4.98 us: step(): pl.pallas_call(functools.partial(step_kernel, scale, len(pieces), not sta...]
    dot_general x2 -> x0, matrix products: 3.59 us -> none  [the longest x1 2.39 us: block_scores(): jnp.einsum('td,sd->ts', target_features, feats, preferred_element_type=jn...]
    ppermute x19 -> x14, starting transfers between devices: 18.1 us -> 15.5 us  [swap(): return lax.ppermute(x, 'tgt', [(i, i ^ bits) for i in range(n)])]
    unnamed x21 -> x4, local copies, waits for them, and re-layouts: 1.63 us -> 0.01 us
    reduce_sum x2 -> x0, other arithmetic: 1.36 us -> none  [the longest x1 0.89 us: on_device(): denominator = jnp.sum(weights, axis=1, keepdims=True)]
    concatenate x2 -> x0, local copies, waits for them, and re-layouts: 0.75 us -> none  [the longest x1 0.73 us: on_device(): everything = gather(jnp.concatenate([source_features, vectors], axis=1))]
  transfers between devices with their start and end apart: 19 -> 14, of which waited for: 12 -> 10; matrix products, arithmetic and copies ran while one was open for 0% -> 0% of each run, Pallas kernels for 0% -> 11%
where the time goes in v3:
time: 41.2 us; the launch traced here: 41.1 us
  waiting for transfers between devices  17 us (41%)
  starting transfers between devices  15.5 us (38%)
  Pallas kernels  7.57 us (18%)
  other arithmetic  0.86 us (2%)
    ppermute x14, waiting for transfers between devices, swap(): return lax.ppermute(x, 'tgt', [(i, i ^ bits) for i in range(n)])  17 us
    ppermute x14, starting transfers between devices, swap(): return lax.ppermute(x, 'tgt', [(i, i ^ bits) for i in range(n)])  15.5 us
    pallas_call x3, Pallas kernels, step(): pl.pallas_call(functools.partial(step_kernel, scale, len(pieces), not sta...  4.98 us
    pallas_call x1, Pallas kernels, load(): pl.pallas_call(load_kernel, out_shape=jax.ShapeDtypeStruct(array.shape, a...  1.57 us
    pallas_call x1, Pallas kernels, pack(): pl.pallas_call(pack_kernel, out_shape=jax.ShapeDtypeStruct((rows, width +...  0.92 us
    div x2, other arithmetic, on_device(): return next_iter / jnp.sqrt(column_sq / total_rows + 1e-06)  0.85 us
  transfers between devices with their start and end apart: 14, of which 10 were waited for; matrix products, arithmetic and copies ran while one was open for 0% of the time, Pallas kernels for 11%

profile of v3, /device:TPU:0, one launch (start us, length us, event | category | flops | bytes accessed | tf_op | source)
XLA Modules:
  0.0 41.1 jit_solution(12263484450572794390)
XLA Ops:
  0.0 0.9 %shard_map.55.refs_0_ = bf16[64,1152]{1,0:T(8,128)(2,1)S(1)} custom-call(bf16[64,1024]{1,0:T(8,128)(2,1)} %feats_ref.1, bf16[64,128]{1,0:T(8,128)(2,1)} %vecs_ref.1), custom_call_target="tpu_custom_call" | custom-call | tf_op jit(solution)/shard_map/pallas_call | solution.py:48
  0.9 0.5 %collective-permute-start = (bf16[64,1152]{1,0:T(8,128)(2,1)S(1)}, bf16[64,1152]{1,0:T(8,128)(2,1)S(1)}, u32[]{:S(2)}, u32[]{:S(2)}) collective-permute-start(bf16[64,1152]{1,0:T(8,128)(2,1)S(1)} %shard_map.55.refs_0_), channel_id=1, source_target_pairs={{0,1},{1,0},{2,3},{3,2},{4,5},{5,4},{6,7},{7,6},{8,9},{9,8},{10,11... | collective-permute-start | bytes 442376 | tf_op jit(solution)/shard_map/ppermute | solution.py:22
  1.4 3.7 %collective-permute-start.4 = (bf16[64,1152]{1,0:T(8,128)(2,1)S(1)}, bf16[64,1152]{1,0:T(8,128)(2,1)S(1)}, u32[]{:S(2)}, u32[]{:S(2)}) collective-permute-start(bf16[64,1152]{1,0:T(8,128)(2,1)S(1)} %shard_map.55.refs_0_), channel_id=1, source_target_pairs={{0,8},{1,9},{2,10},{3,11},{4,12},{5,13},{6,14},{7,15},{8,0},{9,1},... | collective-permute-start | bytes 442376 | tf_op jit(solution)/shard_map/ppermute | solution.py:22
  5.1 0.0 collective-permute-done.refs_1_
  5.1 1.6 %collective-permute-start.1 = (bf16[64,1152]{1,0:T(8,128)(2,1)S(1)}, bf16[64,1152]{1,0:T(8,128)(2,1)S(1)}, u32[]{:S(2)}, u32[]{:S(2)}) collective-permute-start(bf16[64,1152]{1,0:T(8,128)(2,1)S(1)} %shard_map.56.token_ref), channel_id=1, source_target_pairs={{0,4},{1,5},{2,6},{3,7},{4,0},{5,1},{6,2},{7,3},{8,12},{9,13},{10,... | collective-permute-start | bytes 442376 | tf_op jit(solution)/shard_map/ppermute | solution.py:22
  6.8 1.5 %collective-permute-start.2 = (bf16[64,1152]{1,0:T(8,128)(2,1)S(1)}, bf16[64,1152]{1,0:T(8,128)(2,1)S(1)}, u32[]{:S(2)}, u32[]{:S(2)}) collective-permute-start(bf16[64,1152]{1,0:T(8,128)(2,1)S(1)} %shard_map.56.token_ref), channel_id=1, source_target_pairs={{0,2},{1,3},{2,0},{3,1},{4,6},{5,7},{6,4},{7,5},{8,10},{9,11},{10,... | collective-permute-start | bytes 442376 | tf_op jit(solution)/shard_map/ppermute | solution.py:22
  8.3 0.4 collective-permute-start.3
  8.7 1.6 %shard_map.57.target_ref = bf16[1024,1024]{1,0:T(8,128)(2,1)S(1)} custom-call(bf16[1024,1024]{1,0:T(8,128)(2,1)} %array_ref.1, bf16[64,1152]{1,0:T(8,128)(2,1)S(1)} %shard_map.56.token_ref), custom_call_target="tpu_custom_call" | custom-call | flops 1 | bytes 1 | tf_op jit(solution)/shard_map/pallas_call | solution.py:97
  10.3 2.6 %collective-permute-done.4.refs_5_.refs_3_ = bf16[64,1152]{1,0:T(8,128)(2,1)S(1)} collective-permute-done((bf16[64,1152]{1,0:T(8,128)(2,1)S(1)}, bf16[64,1152]{1,0:T(8,128)(2,1)S(1)}, u32[]{:S(2)}, u32[]{:S(2)}) %collective-permute-start.4) | collective-permute-done | bytes 147488 | tf_op jit(solution)/shard_map/ppermute | solution.py:22
  12.8 0.7 %collective-permute-start.6 = (bf16[64,1152]{1,0:T(8,128)(2,1)S(1)}, bf16[64,1152]{1,0:T(8,128)(2,1)S(1)}, u32[]{:S(2)}, u32[]{:S(2)}) collective-permute-start(bf16[64,1152]{1,0:T(8,128)(2,1)S(1)} %collective-permute-done.4.refs_5_.refs_3_), channel_id=1, source_target_pairs={{0,4},{1,5},{2,6},{3,7},{4,0},{5,1},{6,2},{7,3},{8,12},{9,13},{10,... | collective-permute-start | bytes 442376 | tf_op jit(solution)/shard_map/ppermute | solution.py:22
  13.5 1.5 %collective-permute-start.7 = (bf16[64,1152]{1,0:T(8,128)(2,1)S(1)}, bf16[64,1152]{1,0:T(8,128)(2,1)S(1)}, u32[]{:S(2)}, u32[]{:S(2)}) collective-permute-start(bf16[64,1152]{1,0:T(8,128)(2,1)S(1)} %collective-permute-done.4.refs_5_.refs_3_), channel_id=1, source_target_pairs={{0,2},{1,3},{2,0},{3,1},{4,6},{5,7},{6,4},{7,5},{8,10},{9,11},{10,... | collective-permute-start | bytes 442376 | tf_op jit(solution)/shard_map/ppermute | solution.py:22
  15.0 0.0 collective-permute-done.1.refs_2_.refs_0_
  15.0 1.3 %collective-permute-start.8 = (bf16[64,1152]{1,0:T(8,128)(2,1)S(1)}, bf16[64,1152]{1,0:T(8,128)(2,1)S(1)}, u32[]{:S(2)}, u32[]{:S(2)}) collective-permute-start(bf16[64,1152]{1,0:T(8,128)(2,1)S(1)} %collective-permute-done.4.refs_5_.refs_3_), channel_id=1, source_target_pairs={{0,6},{1,7},{2,4},{3,5},{4,2},{5,3},{6,0},{7,1},{8,14},{9,15},{10,... | collective-permute-start | bytes 442376 | tf_op jit(solution)/shard_map/ppermute | solution.py:22
  16.3 0.0 collective-permute-done.2.refs_3_.refs_1_
  16.3 1.6 %collective-permute-done.3.refs_4_.refs_2_ = bf16[64,1152]{1,0:T(8,128)(2,1)S(1)} collective-permute-done((bf16[64,1152]{1,0:T(8,128)(2,1)S(1)}, bf16[64,1152]{1,0:T(8,128)(2,1)S(1)}, u32[]{:S(2)}, u32[]{:S(2)}) %collective-permute-start.3) | collective-permute-done | bytes 147488 | tf_op jit(solution)/shard_map/ppermute | solution.py:22
  17.9 1.9 %shard_map.58 = (f32[1024,128]{1,0:T(8,128)S(1)}, f32[1024,128]{1,0:T(8,128)S(1)}, f32[1024,128]{1,0:T(8,128)S(1)}) custom-call(bf16[1024,1024]{1,0:T(8,128)(2,1)S(1)} %shard_map.57.target_ref, bf16[64,1152]{1,0:T(8,128)(2,1)S(1)} %shard_map.55.refs_0_, bf16[64,1152]{1,0:T(8,128)(2,1)S(1)} %collective-permute-done.refs_1_, ...), custom_call_target="tpu_custom_call" | custom-call | flops 1 | bytes 1 | tf_op jit(solution)/shard_map/pallas_call | solution.py:156
  19.9 0.1 collective-permute-start.5
  20.0 0.1 collective-permute-done.6.refs_0_
  20.1 1.0 %collective-permute-done.7.refs_1_ = bf16[64,1152]{1,0:T(8,128)(2,1)S(1)} collective-permute-done((bf16[64,1152]{1,0:T(8,128)(2,1)S(1)}, bf16[64,1152]{1,0:T(8,128)(2,1)S(1)}, u32[]{:S(2)}, u32[]{:S(2)}) %collective-permute-start.7) | collective-permute-done | bytes 147488 | tf_op jit(solution)/shard_map/ppermute | solution.py:22
  21.1 2.5 %collective-permute-done.8.refs_2_ = bf16[64,1152]{1,0:T(8,128)(2,1)S(1)} collective-permute-done((bf16[64,1152]{1,0:T(8,128)(2,1)S(1)}, bf16[64,1152]{1,0:T(8,128)(2,1)S(1)}, u32[]{:S(2)}, u32[]{:S(2)}) %collective-permute-start.8) | collective-permute-done | bytes 147488 | tf_op jit(solution)/shard_map/ppermute | solution.py:22
  23.6 0.0 copy-start
  23.6 0.0 copy-start.1
  23.7 0.1 collective-permute-start.9
  23.7 1.1 %shard_map.61 = (f32[1024,128]{1,0:T(8,128)S(1)}, f32[1024,128]{1,0:T(8,128)S(1)}, f32[1024,128]{1,0:T(8,128)S(1)}) custom-call(bf16[1024,1024]{1,0:T(8,128)(2,1)S(1)} %shard_map.57.target_ref, bf16[64,1152]{1,0:T(8,128)(2,1)S(1)} %collective-permute-done.6.refs_0_, bf16[64,1152]{1,0:T(8,128)(2,1)S(1)} %collective-permute-done.7.refs_1_, ...), custom_call_target="tpu_custom_call" | custom-call | flops 1 | bytes 1 | tf_op jit(solution)/shard_map/pallas_call | solution.py:156
  24.9 0.6 %collective-permute-done.9.refs_1_ = bf16[192,1152]{1,0:T(8,128)(2,1)S(1)} collective-permute-done((bf16[192,1152]{1,0:T(8,128)(2,1)S(1)}, bf16[192,1152]{1,0:T(8,128)(2,1)S(1)}, u32[]{:S(2)}, u32[]{:S(2)}) %collective-permute-start.9) | collective-permute-done | bytes 442400 | tf_op jit(solution)/shard_map/ppermute | solution.py:22
  25.5 0.0 collective-permute-done.5.refs_0_
  25.5 0.0 copy-done
  25.5 0.0 copy-done.1
  25.5 2.0 %shard_map.62 = (f32[1024,128]{1,0:T(8,128)S(1)}, f32[1,128]{1,0:T(1,128)S(1)}) custom-call(bf16[1024,1024]{1,0:T(8,128)(2,1)S(1)} %shard_map.57.target_ref, bf16[256,1152]{1,0:T(8,128)(2,1)S(1)} %collective-permute-done.5.refs_0_, bf16[192,1152]{1,0:T(8,128)(2,1)S(1)} %collective-permute-done.9.refs_1_, f32[1024,128]{1,0:T(8,128)S(1)} %get-tuple-element.16.refs_2_, ...), custom_call_target="tpu_custom_call" | custom-call | flops 1 | bytes 1 | tf_op jit(solution)/shard_map/pallas_call | solution.py:156
  27.5 0.2 collective-permute-start.10
  27.7 1.0 %collective-permute-done.10 = f32[1,128]{1,0:T(1,128)S(1)} collective-permute-done((f32[1,128]{1,0:T(1,128)S(1)}, f32[1,128]{1,0:T(1,128)S(1)}, u32[]{:S(2)}, u32[]{:S(2)}) %collective-permute-start.10) | collective-permute-done | bytes 544 | tf_op jit(solution)/shard_map/ppermute | solution.py:22
  28.7 0.6 %collective-permute-start.11 = (f32[1,128]{1,0:T(1,128)S(1)}, f32[1,128]{1,0:T(1,128)S(1)}, u32[]{:S(2)}, u32[]{:S(2)}) collective-permute-start(f32[1,128]{1,0:T(1,128)S(1)} %add.18), channel_id=1, source_target_pairs={{0,2},{1,3},{2,0},{3,1},{4,6},{5,7},{6,4},{7,5},{8,10},{9,11},{10,... | collective-permute-start | bytes 1544 | tf_op jit(solution)/shard_map/ppermute | solution.py:22
  29.3 2.9 %collective-permute-done.11 = f32[1,128]{1,0:T(1,128)S(1)} collective-permute-done((f32[1,128]{1,0:T(1,128)S(1)}, f32[1,128]{1,0:T(1,128)S(1)}, u32[]{:S(2)}, u32[]{:S(2)}) %collective-permute-start.11) | collective-permute-done | bytes 544 | tf_op jit(solution)/shard_map/ppermute | solution.py:22
  32.2 1.4 %collective-permute-start.12 = (f32[1,128]{1,0:T(1,128)S(1)}, f32[1,128]{1,0:T(1,128)S(1)}, u32[]{:S(2)}, u32[]{:S(2)}) collective-permute-start(f32[1,128]{1,0:T(1,128)S(1)} %add.19), channel_id=1, source_target_pairs={{0,4},{1,5},{2,6},{3,7},{4,0},{5,1},{6,2},{7,3},{8,12},{9,13},{10,... | collective-permute-start | bytes 1544 | tf_op jit(solution)/shard_map/ppermute | solution.py:22
  33.6 2.2 %collective-permute-done.12 = f32[1,128]{1,0:T(1,128)S(1)} collective-permute-done((f32[1,128]{1,0:T(1,128)S(1)}, f32[1,128]{1,0:T(1,128)S(1)}, u32[]{:S(2)}, u32[]{:S(2)}) %collective-permute-start.12) | collective-permute-done | bytes 544 | tf_op jit(solution)/shard_map/ppermute | solution.py:22
  35.8 2.0 %collective-permute-start.13 = (f32[1,128]{1,0:T(1,128)S(1)}, f32[1,128]{1,0:T(1,128)S(1)}, u32[]{:S(2)}, u32[]{:S(2)}) collective-permute-start(f32[1,128]{1,0:T(1,128)S(1)} %add.20), channel_id=1, source_target_pairs={{0,8},{1,9},{2,10},{3,11},{4,12},{5,13},{6,14},{7,15},{8,0},{9,1},... | collective-permute-start | bytes 1544 | tf_op jit(solution)/shard_map/ppermute | solution.py:22
  37.8 2.5 %collective-permute-done.13 = f32[1,128]{1,0:T(1,128)S(1)} collective-permute-done((f32[1,128]{1,0:T(1,128)S(1)}, f32[1,128]{1,0:T(1,128)S(1)}, u32[]{:S(2)}, u32[]{:S(2)}) %collective-permute-start.13) | collective-permute-done | bytes 544 | tf_op jit(solution)/shard_map/ppermute | solution.py:22
  40.2 0.8 %broadcast_divide_fusion = f32[1024,128]{1,0:T(8,128)} fusion(f32[1024,128]{1,0:T(8,128)S(1)} %get-tuple-element.19, f32[128]{0:T(128)S(1)} %sqrt_bitcast_fusion), kind=kLoop, calls=%fused_computation | loop fusion | flops 131072 | bytes 1049088 | tf_op jit(solution)/shard_map/div | solution.py:195
  (7 shorter events, 0.1 us)
Async XLA Ops:
  0.9 4.2 %collective-permute-start = (bf16[64,1152]{1,0:T(8,128)(2,1)S(1)}, bf16[64,1152]{1,0:T(8,128)(2,1)S(1)}, u32[]{:S(2)}, u32[]{:S(2)}) collective-permute-start(bf16[64,1152]{1,0:T(8,128)(2,1)S(1)} %shard_map.55.refs_0_), channel_id=1, source_target_pairs={{0,1},{1,0},{2,3},{3,2},{4,5},{5,4},{6,7},{7,6},{8,9},{9,8},{10,11... | collective-permute-start | bytes 442376 | tf_op jit(solution)/shard_map/ppermute | solution.py:22
  1.4 11.4 %collective-permute-start.4 = (bf16[64,1152]{1,0:T(8,128)(2,1)S(1)}, bf16[64,1152]{1,0:T(8,128)(2,1)S(1)}, u32[]{:S(2)}, u32[]{:S(2)}) collective-permute-start(bf16[64,1152]{1,0:T(8,128)(2,1)S(1)} %shard_map.55.refs_0_), channel_id=1, source_target_pairs={{0,8},{1,9},{2,10},{3,11},{4,12},{5,13},{6,14},{7,15},{8,0},{9,1},... | collective-permute-start | bytes 442376 | tf_op jit(solution)/shard_map/ppermute | solution.py:22
  5.1 9.9 %collective-permute-start.1 = (bf16[64,1152]{1,0:T(8,128)(2,1)S(1)}, bf16[64,1152]{1,0:T(8,128)(2,1)S(1)}, u32[]{:S(2)}, u32[]{:S(2)}) collective-permute-start(bf16[64,1152]{1,0:T(8,128)(2,1)S(1)} %shard_map.56.token_ref), channel_id=1, source_target_pairs={{0,4},{1,5},{2,6},{3,7},{4,0},{5,1},{6,2},{7,3},{8,12},{9,13},{10,... | collective-permute-start | bytes 442376 | tf_op jit(solution)/shard_map/ppermute | solution.py:22
  6.8 9.5 %collective-permute-start.2 = (bf16[64,1152]{1,0:T(8,128)(2,1)S(1)}, bf16[64,1152]{1,0:T(8,128)(2,1)S(1)}, u32[]{:S(2)}, u32[]{:S(2)}) collective-permute-start(bf16[64,1152]{1,0:T(8,128)(2,1)S(1)} %shard_map.56.token_ref), channel_id=1, source_target_pairs={{0,2},{1,3},{2,0},{3,1},{4,6},{5,7},{6,4},{7,5},{8,10},{9,11},{10,... | collective-permute-start | bytes 442376 | tf_op jit(solution)/shard_map/ppermute | solution.py:22
  8.3 9.6 %collective-permute-start.3 = (bf16[64,1152]{1,0:T(8,128)(2,1)S(1)}, bf16[64,1152]{1,0:T(8,128)(2,1)S(1)}, u32[]{:S(2)}, u32[]{:S(2)}) collective-permute-start(bf16[64,1152]{1,0:T(8,128)(2,1)S(1)} %shard_map.56.token_ref), channel_id=1, source_target_pairs={{0,6},{1,7},{2,4},{3,5},{4,2},{5,3},{6,0},{7,1},{8,14},{9,15},{10,... | collective-permute-start | bytes 442376 | tf_op jit(solution)/shard_map/ppermute | solution.py:22
  12.8 7.3 %collective-permute-start.6 = (bf16[64,1152]{1,0:T(8,128)(2,1)S(1)}, bf16[64,1152]{1,0:T(8,128)(2,1)S(1)}, u32[]{:S(2)}, u32[]{:S(2)}) collective-permute-start(bf16[64,1152]{1,0:T(8,128)(2,1)S(1)} %collective-permute-done.4.refs_5_.refs_3_), channel_id=1, source_target_pairs={{0,4},{1,5},{2,6},{3,7},{4,0},{5,1},{6,2},{7,3},{8,12},{9,13},{10,... | collective-permute-start | bytes 442376 | tf_op jit(solution)/shard_map/ppermute | solution.py:22
  13.5 7.6 %collective-permute-start.7 = (bf16[64,1152]{1,0:T(8,128)(2,1)S(1)}, bf16[64,1152]{1,0:T(8,128)(2,1)S(1)}, u32[]{:S(2)}, u32[]{:S(2)}) collective-permute-start(bf16[64,1152]{1,0:T(8,128)(2,1)S(1)} %collective-permute-done.4.refs_5_.refs_3_), channel_id=1, source_target_pairs={{0,2},{1,3},{2,0},{3,1},{4,6},{5,7},{6,4},{7,5},{8,10},{9,11},{10,... | collective-permute-start | bytes 442376 | tf_op jit(solution)/shard_map/ppermute | solution.py:22
  15.0 8.6 %collective-permute-start.8 = (bf16[64,1152]{1,0:T(8,128)(2,1)S(1)}, bf16[64,1152]{1,0:T(8,128)(2,1)S(1)}, u32[]{:S(2)}, u32[]{:S(2)}) collective-permute-start(bf16[64,1152]{1,0:T(8,128)(2,1)S(1)} %collective-permute-done.4.refs_5_.refs_3_), channel_id=1, source_target_pairs={{0,6},{1,7},{2,4},{3,5},{4,2},{5,3},{6,0},{7,1},{8,14},{9,15},{10,... | collective-permute-start | bytes 442376 | tf_op jit(solution)/shard_map/ppermute | solution.py:22
  19.9 5.6 %collective-permute-start.5 = (bf16[256,1152]{1,0:T(8,128)(2,1)S(1)}, bf16[256,1152]{1,0:T(8,128)(2,1)S(1)}, u32[]{:S(2)}, u32[]{:S(2)}) collective-permute-start(bf16[256,1152]{1,0:T(8,128)(2,1)S(1)} %shard_map.59), channel_id=1, source_target_pairs={{0,1},{1,0},{2,3},{3,2},{4,5},{5,4},{6,7},{7,6},{8,9},{9,8},{10,11... | collective-permute-start | bytes 1769480 | tf_op jit(solution)/shard_map/ppermute | solution.py:22
  23.6 1.9 %copy-start = (f32[1024,128]{1,0:T(8,128)S(1)}, f32[1024,128]{1,0:T(8,128)}, u32[]{:S(2)}) copy-start(f32[1024,128]{1,0:T(8,128)} %refs_5_.1) | copy-start | bytes 1572868
  23.6 1.9 %copy-start.1 = (f32[1024,128]{1,0:T(8,128)S(1)}, f32[1024,128]{1,0:T(8,128)}, u32[]{:S(2)}) copy-start(f32[1024,128]{1,0:T(8,128)} %refs_6_.1) | copy-start | bytes 1572868
  23.7 1.9 %collective-permute-start.9 = (bf16[192,1152]{1,0:T(8,128)(2,1)S(1)}, bf16[192,1152]{1,0:T(8,128)(2,1)S(1)}, u32[]{:S(2)}, u32[]{:S(2)}) collective-permute-start(bf16[192,1152]{1,0:T(8,128)(2,1)S(1)} %shard_map.60), channel_id=1, source_target_pairs={{0,1},{1,0},{2,3},{3,2},{4,5},{5,4},{6,7},{7,6},{8,9},{9,8},{10,11... | collective-permute-start | bytes 1327112 | tf_op jit(solution)/shard_map/ppermute | solution.py:22
  27.5 1.2 %collective-permute-start.10 = (f32[1,128]{1,0:T(1,128)S(1)}, f32[1,128]{1,0:T(1,128)S(1)}, u32[]{:S(2)}, u32[]{:S(2)}) collective-permute-start(f32[1,128]{1,0:T(1,128)S(1)} %get-tuple-element.20), channel_id=1, source_target_pairs={{0,1},{1,0},{2,3},{3,2},{4,5},{5,4},{6,7},{7,6},{8,9},{9,8},{10,11... | collective-permute-start | bytes 1544 | tf_op jit(solution)/shard_map/ppermute | solution.py:22
  28.7 3.5 %collective-permute-start.11 = (f32[1,128]{1,0:T(1,128)S(1)}, f32[1,128]{1,0:T(1,128)S(1)}, u32[]{:S(2)}, u32[]{:S(2)}) collective-permute-start(f32[1,128]{1,0:T(1,128)S(1)} %add.18), channel_id=1, source_target_pairs={{0,2},{1,3},{2,0},{3,1},{4,6},{5,7},{6,4},{7,5},{8,10},{9,11},{10,... | collective-permute-start | bytes 1544 | tf_op jit(solution)/shard_map/ppermute | solution.py:22
  32.2 3.5 %collective-permute-start.12 = (f32[1,128]{1,0:T(1,128)S(1)}, f32[1,128]{1,0:T(1,128)S(1)}, u32[]{:S(2)}, u32[]{:S(2)}) collective-permute-start(f32[1,128]{1,0:T(1,128)S(1)} %add.19), channel_id=1, source_target_pairs={{0,4},{1,5},{2,6},{3,7},{4,0},{5,1},{6,2},{7,3},{8,12},{9,13},{10,... | collective-permute-start | bytes 1544 | tf_op jit(solution)/shard_map/ppermute | solution.py:22
  35.8 4.4 %collective-permute-start.13 = (f32[1,128]{1,0:T(1,128)S(1)}, f32[1,128]{1,0:T(1,128)S(1)}, u32[]{:S(2)}, u32[]{:S(2)}) collective-permute-start(f32[1,128]{1,0:T(1,128)S(1)} %add.20), channel_id=1, source_target_pairs={{0,8},{1,9},{2,10},{3,11},{4,12},{5,13},{6,14},{7,15},{8,0},{9,1},... | collective-permute-start | bytes 1544 | tf_op jit(solution)/shard_map/ppermute | solution.py:22

commit v4 on v3

--- a/solution.py
+++ b/solution.py
@@ -22,11 +22,22 @@
     return lax.ppermute(x, "tgt", [(i, i ^ bits) for i in range(n)])
 
 
+def cross(x, low, high, ends_first):
+    n = lax.axis_size("tgt")
+    pairs = []
+    for i in range(n):
+        at_end = (i // low + i // high) % 2 == 0
+        pairs.append((i, i ^ (low if at_end == ends_first else high)))
+    return lax.ppermute(x, "tgt", pairs)
+
+
 def total(x):
     n = lax.axis_size("tgt")
-    if n & (n - 1):
+    if n & (n - 1) or n < 16:
         return lax.psum(x, "tgt")
-    bit = 1
+    x = x + swap(x, 1)
+    x = x + sum(swap(x, k) for k in (2, 4, 6))
+    bit = 8
     while bit < n:
         x = x + swap(x, bit)
         bit *= 2
@@ -149,7 +160,7 @@
     column_ref[...] = jnp.sum(step * step, axis=0, keepdims=True)
 
 
-def step(target, pieces, state, ends, scale):
+def step(target, pieces, state, ends, scale, micros=0):
     rows, width = target.shape
     cols = pieces[0].shape[1] - width
     whole = jax.ShapeDtypeStruct((rows, cols), jnp.float32)
@@ -159,7 +170,7 @@
         in_specs=[VMEM] * (1 + len(pieces) + len(state) + len(ends)),
         out_specs=[VMEM] * (2 if ends else 3),
         compiler_params=pltpu.CompilerParams(vmem_limit_bytes=20 * 2**20),
-        cost_estimate=SMALL,
+        cost_estimate=pl.CostEstimate(flops=1 + micros * 10**9, bytes_accessed=1, transcendentals=0),
     )(target, *pieces, *state, *ends)
 
 
@@ -173,15 +184,20 @@
         near = jnp.concatenate([near, swap(near, bit)], axis=0)
         bit //= 2
     near_other = swap(near, 1)
-    far = swap(near, bit)
+    one = cross(near, 4, bit, True)
     later = tie(near, near_other)
-    around = [swap(later, k) for k in (4, 2, 6)]
+    two = cross(later, 4, bit, False)
+    around = [one, two] + [swap(later, k) for k in (2, 6)]
     target = load(target, later)
+    place = lax.axis_index("tgt")
+    far = jnp.where((place // 4 + place // bit) % 2 == 0, one, two)
     beyond = [swap(far, k) for k in (4, 2, 6)]
-    state = step(target, [near, near_other] + around + [far], [], [], scale)
-    own = joined(around + [far], state[0])
-    state = step(target, beyond, state, [], scale)
-    return target, [swap(own, 1), swap(joined(beyond), 1)], state
+    state = step(target, [near, near_other] + around, [], [], scale, 20)
+    early = swap(joined(around), 1)
+    state = step(target, [early], state, [], scale, 20)
+    own = joined(beyond, state[0])
+    state = step(target, [own], state, [], scale, 20)
+    return target, [swap(own, 1)], state
 
 
 def on_device(target_features, source_features, vectors, current, previous):

time: 41.2 us -> 39.3 us (0.954)
  waiting for transfers between devices: 17 us -> 12.5 us
  starting transfers between devices: 15.5 us -> 17.7 us
    ppermute x14 -> x13, waiting for transfers between devices: 17 us -> 9.62 us  [swap(): return lax.ppermute(x, 'tgt', [(i, i ^ bits) for i in range(n)])]
    ppermute x0 -> x2, starting transfers between devices: none -> 5 us  [cross(): return lax.ppermute(x, 'tgt', pairs)]
    ppermute x0 -> x2, waiting for transfers between devices: none -> 2.84 us  [cross(): return lax.ppermute(x, 'tgt', pairs)]
    ppermute x14 -> x13, starting transfers between devices: 15.5 us -> 12.7 us  [swap(): return lax.ppermute(x, 'tgt', [(i, i ^ bits) for i in range(n)])]
    pallas_call x3 -> x4, Pallas kernels: 4.98 us -> 5.38 us  [step(): pl.pallas_call(functools.partial(step_kernel, scale, len(pieces), not sta...]
  transfers between devices with their start and end apart: 14 -> 15, of which waited for: 10 -> 11; matrix products, arithmetic and copies ran while one was open for 0% -> 0% of each run, Pallas kernels for 11% -> 15%
where the time goes in v4:
time: 39.3 us; the launch traced here: 39.2 us
  starting transfers between devices  17.7 us (45%)
  waiting for transfers between devices  12.5 us (32%)
  Pallas kernels  7.96 us (20%)
  other arithmetic  0.88 us (2%)
    ppermute x13, starting transfers between devices, swap(): return lax.ppermute(x, 'tgt', [(i, i ^ bits) for i in range(n)])  12.7 us
    ppermute x13, waiting for transfers between devices, swap(): return lax.ppermute(x, 'tgt', [(i, i ^ bits) for i in range(n)])  9.62 us
    pallas_call x4, Pallas kernels, step(): pl.pallas_call(functools.partial(step_kernel, scale, len(pieces), not sta...  5.38 us
    ppermute x2, starting transfers between devices, cross(): return lax.ppermute(x, 'tgt', pairs)  5 us
    ppermute x2, waiting for transfers between devices, cross(): return lax.ppermute(x, 'tgt', pairs)  2.84 us
    pallas_call x1, Pallas kernels, load(): pl.pallas_call(load_kernel, out_shape=jax.ShapeDtypeStruct(array.shape, a...  1.57 us
    pallas_call x1, Pallas kernels, pack(): pl.pallas_call(pack_kernel, out_shape=jax.ShapeDtypeStruct((rows, width +...  0.92 us
    div x2, other arithmetic, on_device(): return next_iter / jnp.sqrt(column_sq / total_rows + 1e-06)  0.85 us
  transfers between devices with their start and end apart: 15, of which 11 were waited for; matrix products, arithmetic and copies ran while one was open for 0% of the time, Pallas kernels for 15%

profile of v4, /device:TPU:0, one launch (start us, length us, event | category | flops | bytes accessed | tf_op | source)
XLA Modules:
  0.0 39.2 jit_solution(12562149856011181170)
XLA Ops:
  0.0 0.9 %shard_map.55.refs_0_ = bf16[64,1152]{1,0:T(8,128)(2,1)S(1)} custom-call(bf16[64,1024]{1,0:T(8,128)(2,1)} %feats_ref.1, bf16[64,128]{1,0:T(8,128)(2,1)} %vecs_ref.1), custom_call_target="tpu_custom_call" | custom-call | tf_op jit(solution)/shard_map/pallas_call | solution.py:59
  0.9 0.5 %collective-permute-start = (bf16[64,1152]{1,0:T(8,128)(2,1)S(1)}, bf16[64,1152]{1,0:T(8,128)(2,1)S(1)}, u32[]{:S(2)}, u32[]{:S(2)}) collective-permute-start(bf16[64,1152]{1,0:T(8,128)(2,1)S(1)} %shard_map.55.refs_0_), channel_id=1, source_target_pairs={{0,1},{1,0},{2,3},{3,2},{4,5},{5,4},{6,7},{7,6},{8,9},{9,8},{10,11... | collective-permute-start | bytes 442376 | tf_op jit(solution)/shard_map/ppermute | solution.py:22
  1.4 2.6 %collective-permute-start.1 = (bf16[64,1152]{1,0:T(8,128)(2,1)S(1)}, bf16[64,1152]{1,0:T(8,128)(2,1)S(1)}, u32[]{:S(2)}, u32[]{:S(2)}) collective-permute-start(bf16[64,1152]{1,0:T(8,128)(2,1)S(1)} %shard_map.55.refs_0_), channel_id=1, source_target_pairs={{0,4},{1,5},{2,6},{3,7},{4,12},{5,13},{6,14},{7,15},{8,0},{9,1},{1... | collective-permute-start | bytes 442376 | tf_op jit(solution)/shard_map/ppermute | solution.py:31
  4.1 0.0 collective-permute-done.refs_1_
  4.1 2.4 %collective-permute-start.2 = (bf16[64,1152]{1,0:T(8,128)(2,1)S(1)}, bf16[64,1152]{1,0:T(8,128)(2,1)S(1)}, u32[]{:S(2)}, u32[]{:S(2)}) collective-permute-start(bf16[64,1152]{1,0:T(8,128)(2,1)S(1)} %shard_map.56.token_ref), channel_id=1, source_target_pairs={{0,8},{1,9},{2,10},{3,11},{4,0},{5,1},{6,2},{7,3},{8,12},{9,13},{1... | collective-permute-start | bytes 442376 | tf_op jit(solution)/shard_map/ppermute | solution.py:31
  6.5 1.5 %collective-permute-start.6 = (bf16[64,1152]{1,0:T(8,128)(2,1)S(1)}, bf16[64,1152]{1,0:T(8,128)(2,1)S(1)}, u32[]{:S(2)}, u32[]{:S(2)}) collective-permute-start(bf16[64,1152]{1,0:T(8,128)(2,1)S(1)} %shard_map.56.token_ref), channel_id=1, source_target_pairs={{0,2},{1,3},{2,0},{3,1},{4,6},{5,7},{6,4},{7,5},{8,10},{9,11},{10,... | collective-permute-start | bytes 442376 | tf_op jit(solution)/shard_map/ppermute | solution.py:22
  8.0 0.3 collective-permute-start.7
  8.3 1.6 %shard_map.57.target_ref = bf16[1024,1024]{1,0:T(8,128)(2,1)S(1)} custom-call(bf16[1024,1024]{1,0:T(8,128)(2,1)} %array_ref.1, bf16[64,1152]{1,0:T(8,128)(2,1)S(1)} %shard_map.56.token_ref), custom_call_target="tpu_custom_call" | custom-call | flops 1 | bytes 1 | tf_op jit(solution)/shard_map/pallas_call | solution.py:108
  9.9 0.0 collective-permute-done.1.refs_0_.refs_2_
  9.9 2.8 %collective-permute-done.2.refs_1_.refs_3_ = bf16[64,1152]{1,0:T(8,128)(2,1)S(1)} collective-permute-done((bf16[64,1152]{1,0:T(8,128)(2,1)S(1)}, bf16[64,1152]{1,0:T(8,128)(2,1)S(1)}, u32[]{:S(2)}, u32[]{:S(2)}) %collective-permute-start.2) | collective-permute-done | bytes 147488 | tf_op jit(solution)/shard_map/ppermute | solution.py:31
  12.8 2.2 %collective-permute-start.3 = (bf16[64,1152]{1,0:T(8,128)(2,1)S(1)}, bf16[64,1152]{1,0:T(8,128)(2,1)S(1)}, u32[]{:S(2)}, u32[]{:S(2)}) collective-permute-start(bf16[64,1152]{1,0:T(8,128)(2,1)S(1)} %broadcast_select_fusion), channel_id=1, source_target_pairs={{0,4},{1,5},{2,6},{3,7},{4,0},{5,1},{6,2},{7,3},{8,12},{9,13},{10,... | collective-permute-start | bytes 442376 | tf_op jit(solution)/shard_map/ppermute | solution.py:22
  15.0 1.5 %collective-permute-start.4 = (bf16[64,1152]{1,0:T(8,128)(2,1)S(1)}, bf16[64,1152]{1,0:T(8,128)(2,1)S(1)}, u32[]{:S(2)}, u32[]{:S(2)}) collective-permute-start(bf16[64,1152]{1,0:T(8,128)(2,1)S(1)} %broadcast_select_fusion), channel_id=1, source_target_pairs={{0,2},{1,3},{2,0},{3,1},{4,6},{5,7},{6,4},{7,5},{8,10},{9,11},{10,... | collective-permute-start | bytes 442376 | tf_op jit(solution)/shard_map/ppermute | solution.py:22
  16.5 0.0 collective-permute-start.5
  16.5 0.0 collective-permute-done.6.refs_2_.refs_4_
  16.5 0.4 collective-permute-done.7.refs_3_.refs_5_
  17.0 0.1 collective-permute-start.8
  17.1 1.9 %shard_map.59 = (f32[1024,128]{1,0:T(8,128)S(1)}, f32[1024,128]{1,0:T(8,128)S(1)}, f32[1024,128]{1,0:T(8,128)S(1)}) custom-call(bf16[1024,1024]{1,0:T(8,128)(2,1)S(1)} %shard_map.57.target_ref, bf16[64,1152]{1,0:T(8,128)(2,1)S(1)} %shard_map.55.refs_0_, bf16[64,1152]{1,0:T(8,128)(2,1)S(1)} %collective-permute-done.refs_1_, ...), custom_call_target="tpu_custom_call" | custom-call | flops 20000000000 | bytes 1 | tf_op jit(solution)/shard_map/pallas_call | solution.py:167
  18.9 0.1 collective-permute-done.8.refs_0_
  19.0 1.1 %shard_map.60 = (f32[1024,128]{1,0:T(8,128)S(1)}, f32[1024,128]{1,0:T(8,128)S(1)}, f32[1024,128]{1,0:T(8,128)S(1)}) custom-call(bf16[1024,1024]{1,0:T(8,128)(2,1)S(1)} %shard_map.57.target_ref, bf16[256,1152]{1,0:T(8,128)(2,1)S(1)} %collective-permute-done.8.refs_0_, f32[1024,128]{1,0:T(8,128)S(1)} %get-tuple-element.16.refs_1_, ...), custom_call_target="tpu_custom_call" | custom-call | flops 20000000000 | bytes 1 | tf_op jit(solution)/shard_map/pallas_call | solution.py:167
  20.2 0.0 collective-permute-done.3.refs_0_
  20.2 2.0 %collective-permute-done.4.refs_1_ = bf16[64,1152]{1,0:T(8,128)(2,1)S(1)} collective-permute-done((bf16[64,1152]{1,0:T(8,128)(2,1)S(1)}, bf16[64,1152]{1,0:T(8,128)(2,1)S(1)}, u32[]{:S(2)}, u32[]{:S(2)}) %collective-permute-start.4) | collective-permute-done | bytes 147488 | tf_op jit(solution)/shard_map/ppermute | solution.py:22
  22.2 1.1 %collective-permute-done.5.refs_2_ = bf16[64,1152]{1,0:T(8,128)(2,1)S(1)} collective-permute-done((bf16[64,1152]{1,0:T(8,128)(2,1)S(1)}, bf16[64,1152]{1,0:T(8,128)(2,1)S(1)}, u32[]{:S(2)}, u32[]{:S(2)}) %collective-permute-start.5) | collective-permute-done | bytes 147488 | tf_op jit(solution)/shard_map/ppermute | solution.py:22
  23.3 0.1 collective-permute-start.9
  23.4 0.0 copy-start
  23.4 0.0 copy-start.1
  23.4 1.1 %shard_map.62 = (f32[1024,128]{1,0:T(8,128)S(1)}, f32[1024,128]{1,0:T(8,128)S(1)}, f32[1024,128]{1,0:T(8,128)S(1)}) custom-call(bf16[1024,1024]{1,0:T(8,128)(2,1)S(1)} %shard_map.57.target_ref, bf16[192,1152]{1,0:T(8,128)(2,1)S(1)} %shard_map.61.refs_0_, f32[1024,128]{1,0:T(8,128)S(1)} %get-tuple-element.19.refs_3_.refs_1_, ...), custom_call_target="tpu_custom_call" | custom-call | flops 20000000000 | bytes 1 | tf_op jit(solution)/shard_map/pallas_call | solution.py:167
  24.6 0.6 %collective-permute-done.9.refs_0_ = bf16[192,1152]{1,0:T(8,128)(2,1)S(1)} collective-permute-done((bf16[192,1152]{1,0:T(8,128)(2,1)S(1)}, bf16[192,1152]{1,0:T(8,128)(2,1)S(1)}, u32[]{:S(2)}, u32[]{:S(2)}) %collective-permute-start.9) | collective-permute-done | bytes 442400 | tf_op jit(solution)/shard_map/ppermute | solution.py:22
  25.2 0.0 copy-done
  25.2 0.0 copy-done.1
  25.2 1.2 %shard_map.63 = (f32[1024,128]{1,0:T(8,128)S(1)}, f32[1,128]{1,0:T(1,128)S(1)}) custom-call(bf16[1024,1024]{1,0:T(8,128)(2,1)S(1)} %shard_map.57.target_ref, bf16[192,1152]{1,0:T(8,128)(2,1)S(1)} %collective-permute-done.9.refs_0_, f32[1024,128]{1,0:T(8,128)S(1)} %get-tuple-element.22.refs_1_, f32[1024,128]{1,0:T(8,128)S(1)} %get-tuple-element.23.refs_2_, ...), custom_call_target="tpu_custom_call" | custom-call | flops 1 | bytes 1 | tf_op jit(solution)/shard_map/pallas_call | solution.py:167
  26.4 0.2 collective-permute-start.10
  26.6 1.0 %collective-permute-done.10 = f32[1,128]{1,0:T(1,128)S(1)} collective-permute-done((f32[1,128]{1,0:T(1,128)S(1)}, f32[1,128]{1,0:T(1,128)S(1)}, u32[]{:S(2)}, u32[]{:S(2)}) %collective-permute-start.10) | collective-permute-done | bytes 544 | tf_op jit(solution)/shard_map/ppermute | solution.py:22
  27.6 1.4 %collective-permute-start.11 = (f32[1,128]{1,0:T(1,128)S(1)}, f32[1,128]{1,0:T(1,128)S(1)}, u32[]{:S(2)}, u32[]{:S(2)}) collective-permute-start(f32[1,128]{1,0:T(1,128)S(1)} %add.32), channel_id=1, source_target_pairs={{0,2},{1,3},{2,0},{3,1},{4,6},{5,7},{6,4},{7,5},{8,10},{9,11},{10,... | collective-permute-start | bytes 1544 | tf_op jit(solution)/shard_map/ppermute | solution.py:22
  29.0 0.4 %collective-permute-start.12 = (f32[1,128]{1,0:T(1,128)S(1)}, f32[1,128]{1,0:T(1,128)S(1)}, u32[]{:S(2)}, u32[]{:S(2)}) collective-permute-start(f32[1,128]{1,0:T(1,128)S(1)} %add.32), channel_id=1, source_target_pairs={{0,4},{1,5},{2,6},{3,7},{4,0},{5,1},{6,2},{7,3},{8,12},{9,13},{10,... | collective-permute-start | bytes 1544 | tf_op jit(solution)/shard_map/ppermute | solution.py:22
  29.4 1.7 %collective-permute-start.13 = (f32[1,128]{1,0:T(1,128)S(1)}, f32[1,128]{1,0:T(1,128)S(1)}, u32[]{:S(2)}, u32[]{:S(2)}) collective-permute-start(f32[1,128]{1,0:T(1,128)S(1)} %add.32), channel_id=1, source_target_pairs={{0,6},{1,7},{2,4},{3,5},{4,2},{5,3},{6,0},{7,1},{8,14},{9,15},{10,... | collective-permute-start | bytes 1544 | tf_op jit(solution)/shard_map/ppermute | solution.py:22
  31.1 0.1 collective-permute-done.11
  31.2 1.4 %collective-permute-done.12 = f32[1,128]{1,0:T(1,128)S(1)} collective-permute-done((f32[1,128]{1,0:T(1,128)S(1)}, f32[1,128]{1,0:T(1,128)S(1)}, u32[]{:S(2)}, u32[]{:S(2)}) %collective-permute-start.12) | collective-permute-done | bytes 544 | tf_op jit(solution)/shard_map/ppermute | solution.py:22
  32.5 1.3 %collective-permute-done.13 = f32[1,128]{1,0:T(1,128)S(1)} collective-permute-done((f32[1,128]{1,0:T(1,128)S(1)}, f32[1,128]{1,0:T(1,128)S(1)}, u32[]{:S(2)}, u32[]{:S(2)}) %collective-permute-start.13) | collective-permute-done | bytes 544 | tf_op jit(solution)/shard_map/ppermute | solution.py:22
  33.9 2.8 %collective-permute-start.14 = (f32[1,128]{1,0:T(1,128)S(1)}, f32[1,128]{1,0:T(1,128)S(1)}, u32[]{:S(2)}, u32[]{:S(2)}) collective-permute-start(f32[1,128]{1,0:T(1,128)S(1)} %add_add_fusion), channel_id=1, source_target_pairs={{0,8},{1,9},{2,10},{3,11},{4,12},{5,13},{6,14},{7,15},{8,0},{9,1},... | collective-permute-start | bytes 1544 | tf_op jit(solution)/shard_map/ppermute | solution.py:22
  36.7 1.7 %collective-permute-done.14 = f32[1,128]{1,0:T(1,128)S(1)} collective-permute-done((f32[1,128]{1,0:T(1,128)S(1)}, f32[1,128]{1,0:T(1,128)S(1)}, u32[]{:S(2)}, u32[]{:S(2)}) %collective-permute-start.14) | collective-permute-done | bytes 544 | tf_op jit(solution)/shard_map/ppermute | solution.py:22
  38.3 0.8 %broadcast_divide_fusion = f32[1024,128]{1,0:T(8,128)} fusion(f32[1024,128]{1,0:T(8,128)S(1)} %get-tuple-element.25, f32[128]{0:T(128)S(1)} %sqrt_bitcast_fusion), kind=kLoop, calls=%fused_computation | loop fusion | flops 131072 | bytes 1049088 | tf_op jit(solution)/shard_map/div | solution.py:211
  (7 shorter events, 0.1 us)
Async XLA Ops:
  0.9 3.2 %collective-permute-start = (bf16[64,1152]{1,0:T(8,128)(2,1)S(1)}, bf16[64,1152]{1,0:T(8,128)(2,1)S(1)}, u32[]{:S(2)}, u32[]{:S(2)}) collective-permute-start(bf16[64,1152]{1,0:T(8,128)(2,1)S(1)} %shard_map.55.refs_0_), channel_id=1, source_target_pairs={{0,1},{1,0},{2,3},{3,2},{4,5},{5,4},{6,7},{7,6},{8,9},{9,8},{10,11... | collective-permute-start | bytes 442376 | tf_op jit(solution)/shard_map/ppermute | solution.py:22
  1.4 8.5 %collective-permute-start.1 = (bf16[64,1152]{1,0:T(8,128)(2,1)S(1)}, bf16[64,1152]{1,0:T(8,128)(2,1)S(1)}, u32[]{:S(2)}, u32[]{:S(2)}) collective-permute-start(bf16[64,1152]{1,0:T(8,128)(2,1)S(1)} %shard_map.55.refs_0_), channel_id=1, source_target_pairs={{0,4},{1,5},{2,6},{3,7},{4,12},{5,13},{6,14},{7,15},{8,0},{9,1},{1... | collective-permute-start | bytes 442376 | tf_op jit(solution)/shard_map/ppermute | solution.py:31
  4.1 8.7 %collective-permute-start.2 = (bf16[64,1152]{1,0:T(8,128)(2,1)S(1)}, bf16[64,1152]{1,0:T(8,128)(2,1)S(1)}, u32[]{:S(2)}, u32[]{:S(2)}) collective-permute-start(bf16[64,1152]{1,0:T(8,128)(2,1)S(1)} %shard_map.56.token_ref), channel_id=1, source_target_pairs={{0,8},{1,9},{2,10},{3,11},{4,0},{5,1},{6,2},{7,3},{8,12},{9,13},{1... | collective-permute-start | bytes 442376 | tf_op jit(solution)/shard_map/ppermute | solution.py:31
  6.5 10.1 %collective-permute-start.6 = (bf16[64,1152]{1,0:T(8,128)(2,1)S(1)}, bf16[64,1152]{1,0:T(8,128)(2,1)S(1)}, u32[]{:S(2)}, u32[]{:S(2)}) collective-permute-start(bf16[64,1152]{1,0:T(8,128)(2,1)S(1)} %shard_map.56.token_ref), channel_id=1, source_target_pairs={{0,2},{1,3},{2,0},{3,1},{4,6},{5,7},{6,4},{7,5},{8,10},{9,11},{10,... | collective-permute-start | bytes 442376 | tf_op jit(solution)/shard_map/ppermute | solution.py:22
  8.0 8.9 %collective-permute-start.7 = (bf16[64,1152]{1,0:T(8,128)(2,1)S(1)}, bf16[64,1152]{1,0:T(8,128)(2,1)S(1)}, u32[]{:S(2)}, u32[]{:S(2)}) collective-permute-start(bf16[64,1152]{1,0:T(8,128)(2,1)S(1)} %shard_map.56.token_ref), channel_id=1, source_target_pairs={{0,6},{1,7},{2,4},{3,5},{4,2},{5,3},{6,0},{7,1},{8,14},{9,15},{10,... | collective-permute-start | bytes 442376 | tf_op jit(solution)/shard_map/ppermute | solution.py:22
  12.8 7.4 %collective-permute-start.3 = (bf16[64,1152]{1,0:T(8,128)(2,1)S(1)}, bf16[64,1152]{1,0:T(8,128)(2,1)S(1)}, u32[]{:S(2)}, u32[]{:S(2)}) collective-permute-start(bf16[64,1152]{1,0:T(8,128)(2,1)S(1)} %broadcast_select_fusion), channel_id=1, source_target_pairs={{0,4},{1,5},{2,6},{3,7},{4,0},{5,1},{6,2},{7,3},{8,12},{9,13},{10,... | collective-permute-start | bytes 442376 | tf_op jit(solution)/shard_map/ppermute | solution.py:22
  15.0 7.2 %collective-permute-start.4 = (bf16[64,1152]{1,0:T(8,128)(2,1)S(1)}, bf16[64,1152]{1,0:T(8,128)(2,1)S(1)}, u32[]{:S(2)}, u32[]{:S(2)}) collective-permute-start(bf16[64,1152]{1,0:T(8,128)(2,1)S(1)} %broadcast_select_fusion), channel_id=1, source_target_pairs={{0,2},{1,3},{2,0},{3,1},{4,6},{5,7},{6,4},{7,5},{8,10},{9,11},{10,... | collective-permute-start | bytes 442376 | tf_op jit(solution)/shard_map/ppermute | solution.py:22
  16.5 6.8 %collective-permute-start.5 = (bf16[64,1152]{1,0:T(8,128)(2,1)S(1)}, bf16[64,1152]{1,0:T(8,128)(2,1)S(1)}, u32[]{:S(2)}, u32[]{:S(2)}) collective-permute-start(bf16[64,1152]{1,0:T(8,128)(2,1)S(1)} %broadcast_select_fusion), channel_id=1, source_target_pairs={{0,6},{1,7},{2,4},{3,5},{4,2},{5,3},{6,0},{7,1},{8,14},{9,15},{10,... | collective-permute-start | bytes 442376 | tf_op jit(solution)/shard_map/ppermute | solution.py:22
  17.0 2.1 %collective-permute-start.8 = (bf16[256,1152]{1,0:T(8,128)(2,1)S(1)}, bf16[256,1152]{1,0:T(8,128)(2,1)S(1)}, u32[]{:S(2)}, u32[]{:S(2)}) collective-permute-start(bf16[256,1152]{1,0:T(8,128)(2,1)S(1)} %shard_map.58), channel_id=1, source_target_pairs={{0,1},{1,0},{2,3},{3,2},{4,5},{5,4},{6,7},{7,6},{8,9},{9,8},{10,11... | collective-permute-start | bytes 1769480 | tf_op jit(solution)/shard_map/ppermute | solution.py:22
  23.3 1.9 %collective-permute-start.9 = (bf16[192,1152]{1,0:T(8,128)(2,1)S(1)}, bf16[192,1152]{1,0:T(8,128)(2,1)S(1)}, u32[]{:S(2)}, u32[]{:S(2)}) collective-permute-start(bf16[192,1152]{1,0:T(8,128)(2,1)S(1)} %shard_map.61.refs_0_), channel_id=1, source_target_pairs={{0,1},{1,0},{2,3},{3,2},{4,5},{5,4},{6,7},{7,6},{8,9},{9,8},{10,11... | collective-permute-start | bytes 1327112 | tf_op jit(solution)/shard_map/ppermute | solution.py:22
  23.4 1.8 %copy-start = (f32[1024,128]{1,0:T(8,128)S(1)}, f32[1024,128]{1,0:T(8,128)}, u32[]{:S(2)}) copy-start(f32[1024,128]{1,0:T(8,128)} %refs_4_.1) | copy-start | bytes 1572868
  23.4 1.8 %copy-start.1 = (f32[1024,128]{1,0:T(8,128)S(1)}, f32[1024,128]{1,0:T(8,128)}, u32[]{:S(2)}) copy-start(f32[1024,128]{1,0:T(8,128)} %refs_5_.1) | copy-start | bytes 1572868
  26.4 1.2 %collective-permute-start.10 = (f32[1,128]{1,0:T(1,128)S(1)}, f32[1,128]{1,0:T(1,128)S(1)}, u32[]{:S(2)}, u32[]{:S(2)}) collective-permute-start(f32[1,128]{1,0:T(1,128)S(1)} %get-tuple-element.26), channel_id=1, source_target_pairs={{0,1},{1,0},{2,3},{3,2},{4,5},{5,4},{6,7},{7,6},{8,9},{9,8},{10,11... | collective-permute-start | bytes 1544 | tf_op jit(solution)/shard_map/ppermute | solution.py:22
  27.6 3.5 %collective-permute-start.11 = (f32[1,128]{1,0:T(1,128)S(1)}, f32[1,128]{1,0:T(1,128)S(1)}, u32[]{:S(2)}, u32[]{:S(2)}) collective-permute-start(f32[1,128]{1,0:T(1,128)S(1)} %add.32), channel_id=1, source_target_pairs={{0,2},{1,3},{2,0},{3,1},{4,6},{5,7},{6,4},{7,5},{8,10},{9,11},{10,... | collective-permute-start | bytes 1544 | tf_op jit(solution)/shard_map/ppermute | solution.py:22
  29.0 3.5 %collective-permute-start.12 = (f32[1,128]{1,0:T(1,128)S(1)}, f32[1,128]{1,0:T(1,128)S(1)}, u32[]{:S(2)}, u32[]{:S(2)}) collective-permute-start(f32[1,128]{1,0:T(1,128)S(1)} %add.32), channel_id=1, source_target_pairs={{0,4},{1,5},{2,6},{3,7},{4,0},{5,1},{6,2},{7,3},{8,12},{9,13},{10,... | collective-permute-start | bytes 1544 | tf_op jit(solution)/shard_map/ppermute | solution.py:22
  29.4 4.4 %collective-permute-start.13 = (f32[1,128]{1,0:T(1,128)S(1)}, f32[1,128]{1,0:T(1,128)S(1)}, u32[]{:S(2)}, u32[]{:S(2)}) collective-permute-start(f32[1,128]{1,0:T(1,128)S(1)} %add.32), channel_id=1, source_target_pairs={{0,6},{1,7},{2,4},{3,5},{4,2},{5,3},{6,0},{7,1},{8,14},{9,15},{10,... | collective-permute-start | bytes 1544 | tf_op jit(solution)/shard_map/ppermute | solution.py:22
  33.9 4.4 %collective-permute-start.14 = (f32[1,128]{1,0:T(1,128)S(1)}, f32[1,128]{1,0:T(1,128)S(1)}, u32[]{:S(2)}, u32[]{:S(2)}) collective-permute-start(f32[1,128]{1,0:T(1,128)S(1)} %add_add_fusion), channel_id=1, source_target_pairs={{0,8},{1,9},{2,10},{3,11},{4,12},{5,13},{6,14},{7,15},{8,0},{9,1},... | collective-permute-start | bytes 1544 | tf_op jit(solution)/shard_map/ppermute | solution.py:22

commit v5 on v4

--- a/solution.py
+++ b/solution.py
@@ -128,7 +128,7 @@
     return dots - half
 
 
-def step_kernel(scale, count, first, last, target_ref, *refs):
+def step_kernel(scale, count, first, last, exact, target_ref, *refs):
     pieces, refs = refs[:count], refs[count:]
     width = target_ref.shape[1]
     packed = jnp.concatenate([r[...] for r in pieces], axis=0)
@@ -143,7 +143,11 @@
     level = jnp.concatenate([top] * pl.cdiv(across, top.shape[1]), axis=1)[:, :across]
     weights = jnp.exp2((scores - level) * scale)
     added = jnp.broadcast_to(jnp.sum(weights, axis=1, keepdims=True), top.shape)
-    product = jnp.dot(weights.astype(jnp.bfloat16), vecs, preferred_element_type=jnp.float32)
+    high = weights.astype(jnp.bfloat16)
+    product = jnp.dot(high, vecs, preferred_element_type=jnp.float32)
+    if exact:
+        low = (weights - high.astype(jnp.float32)).astype(jnp.bfloat16)
+        product = product + jnp.dot(low, vecs, preferred_element_type=jnp.float32)
     if not first:
         shrink = jnp.exp2((before - top) * scale)
         added = shrink * denom + added
@@ -160,12 +164,12 @@
     column_ref[...] = jnp.sum(step * step, axis=0, keepdims=True)
 
 
-def step(target, pieces, state, ends, scale, micros=0):
+def step(target, pieces, state, ends, scale, micros=0, exact=False):
     rows, width = target.shape
     cols = pieces[0].shape[1] - width
     whole = jax.ShapeDtypeStruct((rows, cols), jnp.float32)
     return pl.pallas_call(
-        functools.partial(step_kernel, scale, len(pieces), not state, bool(ends)),
+        functools.partial(step_kernel, scale, len(pieces), not state, bool(ends), exact),
         out_shape=[whole, jax.ShapeDtypeStruct((1, cols), jnp.float32)] if ends else [whole] * 3,
         in_specs=[VMEM] * (1 + len(pieces) + len(state) + len(ends)),
         out_specs=[VMEM] * (2 if ends else 3),
@@ -192,12 +196,12 @@
     place = lax.axis_index("tgt")
     far = jnp.where((place // 4 + place // bit) % 2 == 0, one, two)
     beyond = [swap(far, k) for k in (4, 2, 6)]
-    state = step(target, [near, near_other] + around, [], [], scale, 20)
+    state = step(target, [near, near_other] + around, [], [], scale, 20, True)
     early = swap(joined(around), 1)
-    state = step(target, [early], state, [], scale, 20)
-    own = joined(beyond, state[0])
-    state = step(target, [own], state, [], scale, 20)
-    return target, [swap(own, 1)], state
+    state = step(target, [early], state, [], scale, 20, True)
+    others = [swap(joined(beyond[:2], state[0]), 1), swap(beyond[2], 1)]
+    state = step(target, beyond, state, [], scale, 0)
+    return target, others, state
 
 
 def on_device(target_features, source_features, vectors, current, previous):

time: 39.3 us -> 39.3 us (level)
    ppermute x13 -> x14, starting transfers between devices: 12.7 us -> 12.4 us  [swap(): return lax.ppermute(x, 'tgt', [(i, i ^ bits) for i in range(n)])]
    ppermute x13 -> x14, waiting for transfers between devices: 9.62 us -> 9.63 us  [swap(): return lax.ppermute(x, 'tgt', [(i, i ^ bits) for i in range(n)])]
  transfers between devices with their start and end apart: 15 -> 16, of which waited for: 11 -> 11; matrix products, arithmetic and copies ran while one was open for 0% -> 0% of each run, Pallas kernels for 15% -> 16%
where the time goes in v5:
time: 39.3 us; the launch traced here: 39.2 us
  starting transfers between devices  17.4 us (44%)
  waiting for transfers between devices  12.5 us (32%)
  Pallas kernels  8.33 us (21%)
  other arithmetic  0.88 us (2%)
    ppermute x14, starting transfers between devices, swap(): return lax.ppermute(x, 'tgt', [(i, i ^ bits) for i in range(n)])  12.4 us
    ppermute x14, waiting for transfers between devices, swap(): return lax.ppermute(x, 'tgt', [(i, i ^ bits) for i in range(n)])  9.63 us
    pallas_call x4, Pallas kernels, step(): pl.pallas_call(functools.partial(step_kernel, scale, len(pieces), not sta...  5.76 us
    ppermute x2, starting transfers between devices, cross(): return lax.ppermute(x, 'tgt', pairs)  5 us
    ppermute x2, waiting for transfers between devices, cross(): return lax.ppermute(x, 'tgt', pairs)  2.84 us
    pallas_call x1, Pallas kernels, load(): pl.pallas_call(load_kernel, out_shape=jax.ShapeDtypeStruct(array.shape, a...  1.57 us
    pallas_call x1, Pallas kernels, pack(): pl.pallas_call(pack_kernel, out_shape=jax.ShapeDtypeStruct((rows, width +...  0.92 us
    div x2, other arithmetic, on_device(): return next_iter / jnp.sqrt(column_sq / total_rows + 1e-06)  0.85 us
  transfers between devices with their start and end apart: 16, of which 11 were waited for; matrix products, arithmetic and copies ran while one was open for 0% of the time, Pallas kernels for 16%

profile of v5, /device:TPU:0, one launch (start us, length us, event | category | flops | bytes accessed | tf_op | source)
XLA Modules:
  0.0 39.2 jit_solution(14841512228781793438)
XLA Ops:
  0.0 0.9 %shard_map.55.refs_0_ = bf16[64,1152]{1,0:T(8,128)(2,1)S(1)} custom-call(bf16[64,1024]{1,0:T(8,128)(2,1)} %feats_ref.1, bf16[64,128]{1,0:T(8,128)(2,1)} %vecs_ref.1), custom_call_target="tpu_custom_call" | custom-call | tf_op jit(solution)/shard_map/pallas_call | solution.py:59
  0.9 0.5 %collective-permute-start = (bf16[64,1152]{1,0:T(8,128)(2,1)S(1)}, bf16[64,1152]{1,0:T(8,128)(2,1)S(1)}, u32[]{:S(2)}, u32[]{:S(2)}) collective-permute-start(bf16[64,1152]{1,0:T(8,128)(2,1)S(1)} %shard_map.55.refs_0_), channel_id=1, source_target_pairs={{0,1},{1,0},{2,3},{3,2},{4,5},{5,4},{6,7},{7,6},{8,9},{9,8},{10,11... | collective-permute-start | bytes 442376 | tf_op jit(solution)/shard_map/ppermute | solution.py:22
  1.4 2.6 %collective-permute-start.1 = (bf16[64,1152]{1,0:T(8,128)(2,1)S(1)}, bf16[64,1152]{1,0:T(8,128)(2,1)S(1)}, u32[]{:S(2)}, u32[]{:S(2)}) collective-permute-start(bf16[64,1152]{1,0:T(8,128)(2,1)S(1)} %shard_map.55.refs_0_), channel_id=1, source_target_pairs={{0,4},{1,5},{2,6},{3,7},{4,12},{5,13},{6,14},{7,15},{8,0},{9,1},{1... | collective-permute-start | bytes 442376 | tf_op jit(solution)/shard_map/ppermute | solution.py:31
  4.1 0.0 collective-permute-done.refs_1_
  4.1 2.4 %collective-permute-start.2 = (bf16[64,1152]{1,0:T(8,128)(2,1)S(1)}, bf16[64,1152]{1,0:T(8,128)(2,1)S(1)}, u32[]{:S(2)}, u32[]{:S(2)}) collective-permute-start(bf16[64,1152]{1,0:T(8,128)(2,1)S(1)} %shard_map.56.token_ref), channel_id=1, source_target_pairs={{0,8},{1,9},{2,10},{3,11},{4,0},{5,1},{6,2},{7,3},{8,12},{9,13},{1... | collective-permute-start | bytes 442376 | tf_op jit(solution)/shard_map/ppermute | solution.py:31
  6.5 1.5 %collective-permute-start.5 = (bf16[64,1152]{1,0:T(8,128)(2,1)S(1)}, bf16[64,1152]{1,0:T(8,128)(2,1)S(1)}, u32[]{:S(2)}, u32[]{:S(2)}) collective-permute-start(bf16[64,1152]{1,0:T(8,128)(2,1)S(1)} %shard_map.56.token_ref), channel_id=1, source_target_pairs={{0,2},{1,3},{2,0},{3,1},{4,6},{5,7},{6,4},{7,5},{8,10},{9,11},{10,... | collective-permute-start | bytes 442376 | tf_op jit(solution)/shard_map/ppermute | solution.py:22
  8.0 0.3 collective-permute-start.6
  8.3 1.6 %shard_map.57.target_ref = bf16[1024,1024]{1,0:T(8,128)(2,1)S(1)} custom-call(bf16[1024,1024]{1,0:T(8,128)(2,1)} %array_ref.1, bf16[64,1152]{1,0:T(8,128)(2,1)S(1)} %shard_map.56.token_ref), custom_call_target="tpu_custom_call" | custom-call | flops 1 | bytes 1 | tf_op jit(solution)/shard_map/pallas_call | solution.py:108
  9.9 0.0 collective-permute-done.1.refs_0_.refs_2_
  9.9 2.8 %collective-permute-done.2.refs_1_.refs_3_ = bf16[64,1152]{1,0:T(8,128)(2,1)S(1)} collective-permute-done((bf16[64,1152]{1,0:T(8,128)(2,1)S(1)}, bf16[64,1152]{1,0:T(8,128)(2,1)S(1)}, u32[]{:S(2)}, u32[]{:S(2)}) %collective-permute-start.2) | collective-permute-done | bytes 147488 | tf_op jit(solution)/shard_map/ppermute | solution.py:31
  12.8 2.2 %collective-permute-start.3 = (bf16[64,1152]{1,0:T(8,128)(2,1)S(1)}, bf16[64,1152]{1,0:T(8,128)(2,1)S(1)}, u32[]{:S(2)}, u32[]{:S(2)}) collective-permute-start(bf16[64,1152]{1,0:T(8,128)(2,1)S(1)} %broadcast_select_fusion), channel_id=1, source_target_pairs={{0,4},{1,5},{2,6},{3,7},{4,0},{5,1},{6,2},{7,3},{8,12},{9,13},{10,... | collective-permute-start | bytes 442376 | tf_op jit(solution)/shard_map/ppermute | solution.py:22
  15.0 1.5 %collective-permute-start.4 = (bf16[64,1152]{1,0:T(8,128)(2,1)S(1)}, bf16[64,1152]{1,0:T(8,128)(2,1)S(1)}, u32[]{:S(2)}, u32[]{:S(2)}) collective-permute-start(bf16[64,1152]{1,0:T(8,128)(2,1)S(1)} %broadcast_select_fusion), channel_id=1, source_target_pairs={{0,2},{1,3},{2,0},{3,1},{4,6},{5,7},{6,4},{7,5},{8,10},{9,11},{10,... | collective-permute-start | bytes 442376 | tf_op jit(solution)/shard_map/ppermute | solution.py:22
  16.5 0.0 collective-permute-start.9
  16.5 0.0 collective-permute-done.5.refs_2_.refs_4_
  16.5 0.4 collective-permute-done.6.refs_3_.refs_5_
  17.0 0.1 collective-permute-start.7
  17.1 1.9 %shard_map.59 = (f32[1024,128]{1,0:T(8,128)S(1)}, f32[1024,128]{1,0:T(8,128)S(1)}, f32[1024,128]{1,0:T(8,128)S(1)}) custom-call(bf16[1024,1024]{1,0:T(8,128)(2,1)S(1)} %shard_map.57.target_ref, bf16[64,1152]{1,0:T(8,128)(2,1)S(1)} %shard_map.55.refs_0_, bf16[64,1152]{1,0:T(8,128)(2,1)S(1)} %collective-permute-done.refs_1_, ...), custom_call_target="tpu_custom_call" | custom-call | flops 20000000000 | bytes 1 | tf_op jit(solution)/shard_map/pallas_call | solution.py:171
  18.9 0.1 collective-permute-done.7.refs_0_
  19.0 1.6 %shard_map.60 = (f32[1024,128]{1,0:T(8,128)S(1)}, f32[1024,128]{1,0:T(8,128)S(1)}, f32[1024,128]{1,0:T(8,128)S(1)}) custom-call(bf16[1024,1024]{1,0:T(8,128)(2,1)S(1)} %shard_map.57.target_ref, bf16[256,1152]{1,0:T(8,128)(2,1)S(1)} %collective-permute-done.7.refs_0_, f32[1024,128]{1,0:T(8,128)S(1)} %get-tuple-element.16.refs_1_, ...), custom_call_target="tpu_custom_call" | custom-call | flops 20000000000 | bytes 1 | tf_op jit(solution)/shard_map/pallas_call | solution.py:171
  20.6 0.0 collective-permute-done.3.refs_0_
  20.6 1.6 %collective-permute-done.4.refs_1_ = bf16[64,1152]{1,0:T(8,128)(2,1)S(1)} collective-permute-done((bf16[64,1152]{1,0:T(8,128)(2,1)S(1)}, bf16[64,1152]{1,0:T(8,128)(2,1)S(1)}, u32[]{:S(2)}, u32[]{:S(2)}) %collective-permute-start.4) | collective-permute-done | bytes 147488 | tf_op jit(solution)/shard_map/ppermute | solution.py:22
  22.2 0.0 copy-start
  22.2 0.0 copy-start.1
  22.2 0.1 collective-permute-start.8
  22.3 1.0 %collective-permute-done.9.refs_2_ = bf16[64,1152]{1,0:T(8,128)(2,1)S(1)} collective-permute-done((bf16[64,1152]{1,0:T(8,128)(2,1)S(1)}, bf16[64,1152]{1,0:T(8,128)(2,1)S(1)}, u32[]{:S(2)}, u32[]{:S(2)}) %collective-permute-start.9) | collective-permute-done | bytes 147488 | tf_op jit(solution)/shard_map/ppermute | solution.py:22
  23.3 0.0 collective-permute-start.10
  23.3 1.1 %shard_map.62 = (f32[1024,128]{1,0:T(8,128)S(1)}, f32[1024,128]{1,0:T(8,128)S(1)}, f32[1024,128]{1,0:T(8,128)S(1)}) custom-call(bf16[1024,1024]{1,0:T(8,128)(2,1)S(1)} %shard_map.57.target_ref, bf16[64,1152]{1,0:T(8,128)(2,1)S(1)} %collective-permute-done.3.refs_0_, bf16[64,1152]{1,0:T(8,128)(2,1)S(1)} %collective-permute-done.4.refs_1_, ...), custom_call_target="tpu_custom_call" | custom-call | flops 1 | bytes 1 | tf_op jit(solution)/shard_map/pallas_call | solution.py:171
  24.4 0.2 collective-permute-done.10.refs_1_
  24.7 0.0 collective-permute-done.8.refs_0_
  24.7 0.0 copy-done
  24.7 0.0 copy-done.1
  24.7 1.2 %shard_map.63 = (f32[1024,128]{1,0:T(8,128)S(1)}, f32[1,128]{1,0:T(1,128)S(1)}) custom-call(bf16[1024,1024]{1,0:T(8,128)(2,1)S(1)} %shard_map.57.target_ref, bf16[128,1152]{1,0:T(8,128)(2,1)S(1)} %collective-permute-done.8.refs_0_, bf16[64,1152]{1,0:T(8,128)(2,1)S(1)} %collective-permute-done.10.refs_1_, f32[1024,128]{1,0:T(8,128)S(1)} %get-tuple-element.22.refs_2_, ...), custom_call_target="tpu_custom_call" | custom-call | flops 1 | bytes 1 | tf_op jit(solution)/shard_map/pallas_call | solution.py:171
  25.9 0.4 collective-permute-start.11
  26.3 0.8 %collective-permute-done.11 = f32[1,128]{1,0:T(1,128)S(1)} collective-permute-done((f32[1,128]{1,0:T(1,128)S(1)}, f32[1,128]{1,0:T(1,128)S(1)}, u32[]{:S(2)}, u32[]{:S(2)}) %collective-permute-start.11) | collective-permute-done | bytes 544 | tf_op jit(solution)/shard_map/ppermute | solution.py:22
  27.1 1.9 %collective-permute-start.12 = (f32[1,128]{1,0:T(1,128)S(1)}, f32[1,128]{1,0:T(1,128)S(1)}, u32[]{:S(2)}, u32[]{:S(2)}) collective-permute-start(f32[1,128]{1,0:T(1,128)S(1)} %add.32), channel_id=1, source_target_pairs={{0,2},{1,3},{2,0},{3,1},{4,6},{5,7},{6,4},{7,5},{8,10},{9,11},{10,... | collective-permute-start | bytes 1544 | tf_op jit(solution)/shard_map/ppermute | solution.py:22
  29.0 0.4 %collective-permute-start.13 = (f32[1,128]{1,0:T(1,128)S(1)}, f32[1,128]{1,0:T(1,128)S(1)}, u32[]{:S(2)}, u32[]{:S(2)}) collective-permute-start(f32[1,128]{1,0:T(1,128)S(1)} %add.32), channel_id=1, source_target_pairs={{0,4},{1,5},{2,6},{3,7},{4,0},{5,1},{6,2},{7,3},{8,12},{9,13},{10,... | collective-permute-start | bytes 1544 | tf_op jit(solution)/shard_map/ppermute | solution.py:22
  29.4 1.1 %collective-permute-start.14 = (f32[1,128]{1,0:T(1,128)S(1)}, f32[1,128]{1,0:T(1,128)S(1)}, u32[]{:S(2)}, u32[]{:S(2)}) collective-permute-start(f32[1,128]{1,0:T(1,128)S(1)} %add.32), channel_id=1, source_target_pairs={{0,6},{1,7},{2,4},{3,5},{4,2},{5,3},{6,0},{7,1},{8,14},{9,15},{10,... | collective-permute-start | bytes 1544 | tf_op jit(solution)/shard_map/ppermute | solution.py:22
  30.6 0.1 collective-permute-done.12
  30.6 1.9 %collective-permute-done.13 = f32[1,128]{1,0:T(1,128)S(1)} collective-permute-done((f32[1,128]{1,0:T(1,128)S(1)}, f32[1,128]{1,0:T(1,128)S(1)}, u32[]{:S(2)}, u32[]{:S(2)}) %collective-permute-start.13) | collective-permute-done | bytes 544 | tf_op jit(solution)/shard_map/ppermute | solution.py:22
  32.5 1.3 %collective-permute-done.14 = f32[1,128]{1,0:T(1,128)S(1)} collective-permute-done((f32[1,128]{1,0:T(1,128)S(1)}, f32[1,128]{1,0:T(1,128)S(1)}, u32[]{:S(2)}, u32[]{:S(2)}) %collective-permute-start.14) | collective-permute-done | bytes 544 | tf_op jit(solution)/shard_map/ppermute | solution.py:22
  33.9 2.2 %collective-permute-start.15 = (f32[1,128]{1,0:T(1,128)S(1)}, f32[1,128]{1,0:T(1,128)S(1)}, u32[]{:S(2)}, u32[]{:S(2)}) collective-permute-start(f32[1,128]{1,0:T(1,128)S(1)} %add_add_fusion), channel_id=1, source_target_pairs={{0,8},{1,9},{2,10},{3,11},{4,12},{5,13},{6,14},{7,15},{8,0},{9,1},... | collective-permute-start | bytes 1544 | tf_op jit(solution)/shard_map/ppermute | solution.py:22
  36.1 2.2 %collective-permute-done.15 = f32[1,128]{1,0:T(1,128)S(1)} collective-permute-done((f32[1,128]{1,0:T(1,128)S(1)}, f32[1,128]{1,0:T(1,128)S(1)}, u32[]{:S(2)}, u32[]{:S(2)}) %collective-permute-start.15) | collective-permute-done | bytes 544 | tf_op jit(solution)/shard_map/ppermute | solution.py:22
  38.3 0.8 %broadcast_divide_fusion = f32[1024,128]{1,0:T(8,128)} fusion(f32[1024,128]{1,0:T(8,128)S(1)} %get-tuple-element.25, f32[128]{0:T(128)S(1)} %sqrt_bitcast_fusion), kind=kLoop, calls=%fused_computation | loop fusion | flops 131072 | bytes 1049088 | tf_op jit(solution)/shard_map/div | solution.py:215
  (7 shorter events, 0.1 us)
Async XLA Ops:
  0.9 3.2 %collective-permute-start = (bf16[64,1152]{1,0:T(8,128)(2,1)S(1)}, bf16[64,1152]{1,0:T(8,128)(2,1)S(1)}, u32[]{:S(2)}, u32[]{:S(2)}) collective-permute-start(bf16[64,1152]{1,0:T(8,128)(2,1)S(1)} %shard_map.55.refs_0_), channel_id=1, source_target_pairs={{0,1},{1,0},{2,3},{3,2},{4,5},{5,4},{6,7},{7,6},{8,9},{9,8},{10,11... | collective-permute-start | bytes 442376 | tf_op jit(solution)/shard_map/ppermute | solution.py:22
  1.4 8.5 %collective-permute-start.1 = (bf16[64,1152]{1,0:T(8,128)(2,1)S(1)}, bf16[64,1152]{1,0:T(8,128)(2,1)S(1)}, u32[]{:S(2)}, u32[]{:S(2)}) collective-permute-start(bf16[64,1152]{1,0:T(8,128)(2,1)S(1)} %shard_map.55.refs_0_), channel_id=1, source_target_pairs={{0,4},{1,5},{2,6},{3,7},{4,12},{5,13},{6,14},{7,15},{8,0},{9,1},{1... | collective-permute-start | bytes 442376 | tf_op jit(solution)/shard_map/ppermute | solution.py:31
  4.1 8.7 %collective-permute-start.2 = (bf16[64,1152]{1,0:T(8,128)(2,1)S(1)}, bf16[64,1152]{1,0:T(8,128)(2,1)S(1)}, u32[]{:S(2)}, u32[]{:S(2)}) collective-permute-start(bf16[64,1152]{1,0:T(8,128)(2,1)S(1)} %shard_map.56.token_ref), channel_id=1, source_target_pairs={{0,8},{1,9},{2,10},{3,11},{4,0},{5,1},{6,2},{7,3},{8,12},{9,13},{1... | collective-permute-start | bytes 442376 | tf_op jit(solution)/shard_map/ppermute | solution.py:31
  6.5 10.1 %collective-permute-start.5 = (bf16[64,1152]{1,0:T(8,128)(2,1)S(1)}, bf16[64,1152]{1,0:T(8,128)(2,1)S(1)}, u32[]{:S(2)}, u32[]{:S(2)}) collective-permute-start(bf16[64,1152]{1,0:T(8,128)(2,1)S(1)} %shard_map.56.token_ref), channel_id=1, source_target_pairs={{0,2},{1,3},{2,0},{3,1},{4,6},{5,7},{6,4},{7,5},{8,10},{9,11},{10,... | collective-permute-start | bytes 442376 | tf_op jit(solution)/shard_map/ppermute | solution.py:22
  8.0 8.9 %collective-permute-start.6 = (bf16[64,1152]{1,0:T(8,128)(2,1)S(1)}, bf16[64,1152]{1,0:T(8,128)(2,1)S(1)}, u32[]{:S(2)}, u32[]{:S(2)}) collective-permute-start(bf16[64,1152]{1,0:T(8,128)(2,1)S(1)} %shard_map.56.token_ref), channel_id=1, source_target_pairs={{0,6},{1,7},{2,4},{3,5},{4,2},{5,3},{6,0},{7,1},{8,14},{9,15},{10,... | collective-permute-start | bytes 442376 | tf_op jit(solution)/shard_map/ppermute | solution.py:22
  12.8 7.8 %collective-permute-start.3 = (bf16[64,1152]{1,0:T(8,128)(2,1)S(1)}, bf16[64,1152]{1,0:T(8,128)(2,1)S(1)}, u32[]{:S(2)}, u32[]{:S(2)}) collective-permute-start(bf16[64,1152]{1,0:T(8,128)(2,1)S(1)} %broadcast_select_fusion), channel_id=1, source_target_pairs={{0,4},{1,5},{2,6},{3,7},{4,0},{5,1},{6,2},{7,3},{8,12},{9,13},{10,... | collective-permute-start | bytes 442376 | tf_op jit(solution)/shard_map/ppermute | solution.py:22
  15.0 7.2 %collective-permute-start.4 = (bf16[64,1152]{1,0:T(8,128)(2,1)S(1)}, bf16[64,1152]{1,0:T(8,128)(2,1)S(1)}, u32[]{:S(2)}, u32[]{:S(2)}) collective-permute-start(bf16[64,1152]{1,0:T(8,128)(2,1)S(1)} %broadcast_select_fusion), channel_id=1, source_target_pairs={{0,2},{1,3},{2,0},{3,1},{4,6},{5,7},{6,4},{7,5},{8,10},{9,11},{10,... | collective-permute-start | bytes 442376 | tf_op jit(solution)/shard_map/ppermute | solution.py:22
  16.5 6.8 %collective-permute-start.9 = (bf16[64,1152]{1,0:T(8,128)(2,1)S(1)}, bf16[64,1152]{1,0:T(8,128)(2,1)S(1)}, u32[]{:S(2)}, u32[]{:S(2)}) collective-permute-start(bf16[64,1152]{1,0:T(8,128)(2,1)S(1)} %broadcast_select_fusion), channel_id=1, source_target_pairs={{0,6},{1,7},{2,4},{3,5},{4,2},{5,3},{6,0},{7,1},{8,14},{9,15},{10,... | collective-permute-start | bytes 442376 | tf_op jit(solution)/shard_map/ppermute | solution.py:22
  17.0 2.1 %collective-permute-start.7 = (bf16[256,1152]{1,0:T(8,128)(2,1)S(1)}, bf16[256,1152]{1,0:T(8,128)(2,1)S(1)}, u32[]{:S(2)}, u32[]{:S(2)}) collective-permute-start(bf16[256,1152]{1,0:T(8,128)(2,1)S(1)} %shard_map.58), channel_id=1, source_target_pairs={{0,1},{1,0},{2,3},{3,2},{4,5},{5,4},{6,7},{7,6},{8,9},{9,8},{10,11... | collective-permute-start | bytes 1769480 | tf_op jit(solution)/shard_map/ppermute | solution.py:22
  22.2 2.5 %copy-start = (f32[1024,128]{1,0:T(8,128)S(1)}, f32[1024,128]{1,0:T(8,128)}, u32[]{:S(2)}) copy-start(f32[1024,128]{1,0:T(8,128)} %refs_5_.1) | copy-start | bytes 1572868
  22.2 2.5 %copy-start.1 = (f32[1024,128]{1,0:T(8,128)S(1)}, f32[1024,128]{1,0:T(8,128)}, u32[]{:S(2)}) copy-start(f32[1024,128]{1,0:T(8,128)} %refs_6_.1) | copy-start | bytes 1572868
  22.2 2.4 %collective-permute-start.8 = (bf16[128,1152]{1,0:T(8,128)(2,1)S(1)}, bf16[128,1152]{1,0:T(8,128)(2,1)S(1)}, u32[]{:S(2)}, u32[]{:S(2)}) collective-permute-start(bf16[128,1152]{1,0:T(8,128)(2,1)S(1)} %shard_map.61), channel_id=1, source_target_pairs={{0,1},{1,0},{2,3},{3,2},{4,5},{5,4},{6,7},{7,6},{8,9},{9,8},{10,11... | collective-permute-start | bytes 884744 | tf_op jit(solution)/shard_map/ppermute | solution.py:22
  23.3 1.4 %collective-permute-start.10 = (bf16[64,1152]{1,0:T(8,128)(2,1)S(1)}, bf16[64,1152]{1,0:T(8,128)(2,1)S(1)}, u32[]{:S(2)}, u32[]{:S(2)}) collective-permute-start(bf16[64,1152]{1,0:T(8,128)(2,1)S(1)} %collective-permute-done.9.refs_2_), channel_id=1, source_target_pairs={{0,1},{1,0},{2,3},{3,2},{4,5},{5,4},{6,7},{7,6},{8,9},{9,8},{10,11... | collective-permute-start | bytes 442376 | tf_op jit(solution)/shard_map/ppermute | solution.py:22
  25.9 1.2 %collective-permute-start.11 = (f32[1,128]{1,0:T(1,128)S(1)}, f32[1,128]{1,0:T(1,128)S(1)}, u32[]{:S(2)}, u32[]{:S(2)}) collective-permute-start(f32[1,128]{1,0:T(1,128)S(1)} %get-tuple-element.26), channel_id=1, source_target_pairs={{0,1},{1,0},{2,3},{3,2},{4,5},{5,4},{6,7},{7,6},{8,9},{9,8},{10,11... | collective-permute-start | bytes 1544 | tf_op jit(solution)/shard_map/ppermute | solution.py:22
  27.1 3.5 %collective-permute-start.12 = (f32[1,128]{1,0:T(1,128)S(1)}, f32[1,128]{1,0:T(1,128)S(1)}, u32[]{:S(2)}, u32[]{:S(2)}) collective-permute-start(f32[1,128]{1,0:T(1,128)S(1)} %add.32), channel_id=1, source_target_pairs={{0,2},{1,3},{2,0},{3,1},{4,6},{5,7},{6,4},{7,5},{8,10},{9,11},{10,... | collective-permute-start | bytes 1544 | tf_op jit(solution)/shard_map/ppermute | solution.py:22
  29.0 3.5 %collective-permute-start.13 = (f32[1,128]{1,0:T(1,128)S(1)}, f32[1,128]{1,0:T(1,128)S(1)}, u32[]{:S(2)}, u32[]{:S(2)}) collective-permute-start(f32[1,128]{1,0:T(1,128)S(1)} %add.32), channel_id=1, source_target_pairs={{0,4},{1,5},{2,6},{3,7},{4,0},{5,1},{6,2},{7,3},{8,12},{9,13},{10,... | collective-permute-start | bytes 1544 | tf_op jit(solution)/shard_map/ppermute | solution.py:22
  29.4 4.4 %collective-permute-start.14 = (f32[1,128]{1,0:T(1,128)S(1)}, f32[1,128]{1,0:T(1,128)S(1)}, u32[]{:S(2)}, u32[]{:S(2)}) collective-permute-start(f32[1,128]{1,0:T(1,128)S(1)} %add.32), channel_id=1, source_target_pairs={{0,6},{1,7},{2,4},{3,5},{4,2},{5,3},{6,0},{7,1},{8,14},{9,15},{10,... | collective-permute-start | bytes 1544 | tf_op jit(solution)/shard_map/ppermute | solution.py:22
  33.9 4.4 %collective-permute-start.15 = (f32[1,128]{1,0:T(1,128)S(1)}, f32[1,128]{1,0:T(1,128)S(1)}, u32[]{:S(2)}, u32[]{:S(2)}) collective-permute-start(f32[1,128]{1,0:T(1,128)S(1)} %add_add_fusion), channel_id=1, source_target_pairs={{0,8},{1,9},{2,10},{3,11},{4,12},{5,13},{6,14},{7,15},{8,0},{9,1},... | collective-permute-start | bytes 1544 | tf_op jit(solution)/shard_map/ppermute | solution.py:22

commit v6 on v5

--- a/solution.py
+++ b/solution.py
@@ -20,6 +20,11 @@
 def swap(x, bits):
     n = lax.axis_size("tgt")
     return lax.ppermute(x, "tgt", [(i, i ^ bits) for i in range(n)])
+
+
+def swap_by_core(x, first, second):
+    n = lax.axis_size("tgt")
+    return lax.ppermute(x, "tgt", [(i, i ^ (second if i % 2 else first)) for i in range(n)])
 
 
 def cross(x, low, high, ends_first):
@@ -195,7 +200,7 @@
     target = load(target, later)
     place = lax.axis_index("tgt")
     far = jnp.where((place // 4 + place // bit) % 2 == 0, one, two)
-    beyond = [swap(far, k) for k in (4, 2, 6)]
+    beyond = [swap_by_core(far, a, b) for a, b in ((2, 4), (4, 2), (6, 6))]
     state = step(target, [near, near_other] + around, [], [], scale, 20, True)
     early = swap(joined(around), 1)
     state = step(target, [early], state, [], scale, 20, True)

time: 39.3 us -> 39.3 us (level)
  starting transfers between devices: 17.4 us -> 18.1 us
  waiting for transfers between devices: 12.5 us -> 11.8 us
    ppermute x0 -> x3, starting transfers between devices: none -> 3.74 us  [swap_by_core(): lax.ppermute(x, 'tgt', [(i, i ^ (second if i % 2 else first)) for i in ra...]
    ppermute x14 -> x11, starting transfers between devices: 12.4 us -> 9.36 us  [swap(): return lax.ppermute(x, 'tgt', [(i, i ^ bits) for i in range(n)])]
    ppermute x14 -> x11, waiting for transfers between devices: 9.63 us -> 7.19 us  [swap(): return lax.ppermute(x, 'tgt', [(i, i ^ bits) for i in range(n)])]
    ppermute x0 -> x3, waiting for transfers between devices: none -> 1.72 us  [swap_by_core(): lax.ppermute(x, 'tgt', [(i, i ^ (second if i % 2 else first)) for i in ra...]
where the time goes in v6:
time: 39.3 us; the launch traced here: 39.2 us
  starting transfers between devices  18.1 us (46%)
  waiting for transfers between devices  11.8 us (30%)
  Pallas kernels  8.34 us (21%)
  other arithmetic  0.88 us (2%)
    ppermute x11, starting transfers between devices, swap(): return lax.ppermute(x, 'tgt', [(i, i ^ bits) for i in range(n)])  9.36 us
    ppermute x11, waiting for transfers between devices, swap(): return lax.ppermute(x, 'tgt', [(i, i ^ bits) for i in range(n)])  7.19 us
    pallas_call x4, Pallas kernels, step(): pl.pallas_call(functools.partial(step_kernel, scale, len(pieces), not sta...  5.77 us
    ppermute x2, starting transfers between devices, cross(): return lax.ppermute(x, 'tgt', pairs)  5 us
    ppermute x3, starting transfers between devices, swap_by_core(): lax.ppermute(x, 'tgt', [(i, i ^ (second if i % 2 else first)) for i in ra...  3.74 us
    ppermute x2, waiting for transfers between devices, cross(): return lax.ppermute(x, 'tgt', pairs)  2.84 us
    ppermute x3, waiting for transfers between devices, swap_by_core(): lax.ppermute(x, 'tgt', [(i, i ^ (second if i % 2 else first)) for i in ra...  1.72 us
    pallas_call x1, Pallas kernels, load(): pl.pallas_call(load_kernel, out_shape=jax.ShapeDtypeStruct(array.shape, a...  1.57 us
  transfers between devices with their start and end apart: 16, of which 11 were waited for; matrix products, arithmetic and copies ran while one was open for 0% of the time, Pallas kernels for 16%

profile of v6, /device:TPU:0, one launch (start us, length us, event | category | flops | bytes accessed | tf_op | source)
XLA Modules:
  0.0 39.2 jit_solution(13973519552393293481)
XLA Ops:
  0.0 0.9 %shard_map.55.refs_0_ = bf16[64,1152]{1,0:T(8,128)(2,1)S(1)} custom-call(bf16[64,1024]{1,0:T(8,128)(2,1)} %feats_ref.1, bf16[64,128]{1,0:T(8,128)(2,1)} %vecs_ref.1), custom_call_target="tpu_custom_call" | custom-call | tf_op jit(solution)/shard_map/pallas_call | solution.py:64
  0.9 0.5 %collective-permute-start = (bf16[64,1152]{1,0:T(8,128)(2,1)S(1)}, bf16[64,1152]{1,0:T(8,128)(2,1)S(1)}, u32[]{:S(2)}, u32[]{:S(2)}) collective-permute-start(bf16[64,1152]{1,0:T(8,128)(2,1)S(1)} %shard_map.55.refs_0_), channel_id=1, source_target_pairs={{0,1},{1,0},{2,3},{3,2},{4,5},{5,4},{6,7},{7,6},{8,9},{9,8},{10,11... | collective-permute-start | bytes 442376 | tf_op jit(solution)/shard_map/ppermute | solution.py:22
  1.4 2.6 %collective-permute-start.1 = (bf16[64,1152]{1,0:T(8,128)(2,1)S(1)}, bf16[64,1152]{1,0:T(8,128)(2,1)S(1)}, u32[]{:S(2)}, u32[]{:S(2)}) collective-permute-start(bf16[64,1152]{1,0:T(8,128)(2,1)S(1)} %shard_map.55.refs_0_), channel_id=1, source_target_pairs={{0,4},{1,5},{2,6},{3,7},{4,12},{5,13},{6,14},{7,15},{8,0},{9,1},{1... | collective-permute-start | bytes 442376 | tf_op jit(solution)/shard_map/ppermute | solution.py:36
  4.1 0.0 collective-permute-done.refs_1_
  4.1 2.4 %collective-permute-start.2 = (bf16[64,1152]{1,0:T(8,128)(2,1)S(1)}, bf16[64,1152]{1,0:T(8,128)(2,1)S(1)}, u32[]{:S(2)}, u32[]{:S(2)}) collective-permute-start(bf16[64,1152]{1,0:T(8,128)(2,1)S(1)} %shard_map.56.token_ref), channel_id=1, source_target_pairs={{0,8},{1,9},{2,10},{3,11},{4,0},{5,1},{6,2},{7,3},{8,12},{9,13},{1... | collective-permute-start | bytes 442376 | tf_op jit(solution)/shard_map/ppermute | solution.py:36
  6.5 1.5 %collective-permute-start.5 = (bf16[64,1152]{1,0:T(8,128)(2,1)S(1)}, bf16[64,1152]{1,0:T(8,128)(2,1)S(1)}, u32[]{:S(2)}, u32[]{:S(2)}) collective-permute-start(bf16[64,1152]{1,0:T(8,128)(2,1)S(1)} %shard_map.56.token_ref), channel_id=1, source_target_pairs={{0,2},{1,3},{2,0},{3,1},{4,6},{5,7},{6,4},{7,5},{8,10},{9,11},{10,... | collective-permute-start | bytes 442376 | tf_op jit(solution)/shard_map/ppermute | solution.py:22
  8.0 0.3 collective-permute-start.6
  8.3 1.6 %shard_map.57.target_ref = bf16[1024,1024]{1,0:T(8,128)(2,1)S(1)} custom-call(bf16[1024,1024]{1,0:T(8,128)(2,1)} %array_ref.1, bf16[64,1152]{1,0:T(8,128)(2,1)S(1)} %shard_map.56.token_ref), custom_call_target="tpu_custom_call" | custom-call | flops 1 | bytes 1 | tf_op jit(solution)/shard_map/pallas_call | solution.py:113
  9.9 0.0 collective-permute-done.1.refs_0_.refs_2_
  9.9 2.8 %collective-permute-done.2.refs_1_.refs_3_ = bf16[64,1152]{1,0:T(8,128)(2,1)S(1)} collective-permute-done((bf16[64,1152]{1,0:T(8,128)(2,1)S(1)}, bf16[64,1152]{1,0:T(8,128)(2,1)S(1)}, u32[]{:S(2)}, u32[]{:S(2)}) %collective-permute-start.2) | collective-permute-done | bytes 147488 | tf_op jit(solution)/shard_map/ppermute | solution.py:36
  12.8 1.6 %collective-permute-start.3 = (bf16[64,1152]{1,0:T(8,128)(2,1)S(1)}, bf16[64,1152]{1,0:T(8,128)(2,1)S(1)}, u32[]{:S(2)}, u32[]{:S(2)}) collective-permute-start(bf16[64,1152]{1,0:T(8,128)(2,1)S(1)} %broadcast_select_fusion), channel_id=1, source_target_pairs={{0,2},{1,5},{2,0},{3,7},{4,6},{5,1},{6,4},{7,3},{8,10},{9,13},{10,... | collective-permute-start | bytes 442376 | tf_op jit(solution)/shard_map/ppermute | solution.py:27
  14.4 2.1 %collective-permute-start.4 = (bf16[64,1152]{1,0:T(8,128)(2,1)S(1)}, bf16[64,1152]{1,0:T(8,128)(2,1)S(1)}, u32[]{:S(2)}, u32[]{:S(2)}) collective-permute-start(bf16[64,1152]{1,0:T(8,128)(2,1)S(1)} %broadcast_select_fusion), channel_id=1, source_target_pairs={{0,4},{1,3},{2,6},{3,1},{4,0},{5,7},{6,2},{7,5},{8,12},{9,11},{10,... | collective-permute-start | bytes 442376 | tf_op jit(solution)/shard_map/ppermute | solution.py:27
  16.5 0.0 collective-permute-start.9
  16.5 0.0 collective-permute-done.5.refs_2_.refs_4_
  16.5 0.4 %collective-permute-done.6.refs_3_.refs_5_ = bf16[64,1152]{1,0:T(8,128)(2,1)S(1)} collective-permute-done((bf16[64,1152]{1,0:T(8,128)(2,1)S(1)}, bf16[64,1152]{1,0:T(8,128)(2,1)S(1)}, u32[]{:S(2)}, u32[]{:S(2)}) %collective-permute-start.6) | collective-permute-done | bytes 147488 | tf_op jit(solution)/shard_map/ppermute | solution.py:22
  17.0 0.1 collective-permute-start.7
  17.1 1.9 %shard_map.59 = (f32[1024,128]{1,0:T(8,128)S(1)}, f32[1024,128]{1,0:T(8,128)S(1)}, f32[1024,128]{1,0:T(8,128)S(1)}) custom-call(bf16[1024,1024]{1,0:T(8,128)(2,1)S(1)} %shard_map.57.target_ref, bf16[64,1152]{1,0:T(8,128)(2,1)S(1)} %shard_map.55.refs_0_, bf16[64,1152]{1,0:T(8,128)(2,1)S(1)} %collective-permute-done.refs_1_, ...), custom_call_target="tpu_custom_call" | custom-call | flops 20000000000 | bytes 1 | tf_op jit(solution)/shard_map/pallas_call | solution.py:176
  18.9 0.1 collective-permute-done.7.refs_0_
  19.0 1.6 %shard_map.60 = (f32[1024,128]{1,0:T(8,128)S(1)}, f32[1024,128]{1,0:T(8,128)S(1)}, f32[1024,128]{1,0:T(8,128)S(1)}) custom-call(bf16[1024,1024]{1,0:T(8,128)(2,1)S(1)} %shard_map.57.target_ref, bf16[256,1152]{1,0:T(8,128)(2,1)S(1)} %collective-permute-done.7.refs_0_, f32[1024,128]{1,0:T(8,128)S(1)} %get-tuple-element.16.refs_1_, ...), custom_call_target="tpu_custom_call" | custom-call | flops 20000000000 | bytes 1 | tf_op jit(solution)/shard_map/pallas_call | solution.py:176
  20.6 0.6 %collective-permute-done.3.refs_0_ = bf16[64,1152]{1,0:T(8,128)(2,1)S(1)} collective-permute-done((bf16[64,1152]{1,0:T(8,128)(2,1)S(1)}, bf16[64,1152]{1,0:T(8,128)(2,1)S(1)}, u32[]{:S(2)}, u32[]{:S(2)}) %collective-permute-start.3) | collective-permute-done | bytes 147488 | tf_op jit(solution)/shard_map/ppermute | solution.py:27
  21.2 0.0 collective-permute-done.4.refs_1_
  21.2 0.0 copy-start
  21.3 0.0 copy-start.1
  21.3 0.8 %collective-permute-start.8 = (bf16[128,1152]{1,0:T(8,128)(2,1)S(1)}, bf16[128,1152]{1,0:T(8,128)(2,1)S(1)}, u32[]{:S(2)}, u32[]{:S(2)}) collective-permute-start(bf16[128,1152]{1,0:T(8,128)(2,1)S(1)} %shard_map.61), channel_id=1, source_target_pairs={{0,1},{1,0},{2,3},{3,2},{4,5},{5,4},{6,7},{7,6},{8,9},{9,8},{10,11... | collective-permute-start | bytes 884744 | tf_op jit(solution)/shard_map/ppermute | solution.py:22
  22.1 1.1 %collective-permute-done.9.refs_2_ = bf16[64,1152]{1,0:T(8,128)(2,1)S(1)} collective-permute-done((bf16[64,1152]{1,0:T(8,128)(2,1)S(1)}, bf16[64,1152]{1,0:T(8,128)(2,1)S(1)}, u32[]{:S(2)}, u32[]{:S(2)}) %collective-permute-start.9) | collective-permute-done | bytes 147488 | tf_op jit(solution)/shard_map/ppermute | solution.py:27
  23.2 0.0 collective-permute-start.10
  23.2 1.1 %shard_map.62 = (f32[1024,128]{1,0:T(8,128)S(1)}, f32[1024,128]{1,0:T(8,128)S(1)}, f32[1024,128]{1,0:T(8,128)S(1)}) custom-call(bf16[1024,1024]{1,0:T(8,128)(2,1)S(1)} %shard_map.57.target_ref, bf16[64,1152]{1,0:T(8,128)(2,1)S(1)} %collective-permute-done.3.refs_0_, bf16[64,1152]{1,0:T(8,128)(2,1)S(1)} %collective-permute-done.4.refs_1_, ...), custom_call_target="tpu_custom_call" | custom-call | flops 1 | bytes 1 | tf_op jit(solution)/shard_map/pallas_call | solution.py:176
  24.3 0.2 collective-permute-done.10.refs_1_
  24.6 0.0 collective-permute-done.8.refs_0_
  24.6 0.0 copy-done
  24.6 0.0 copy-done.1
  24.6 1.2 %shard_map.63 = (f32[1024,128]{1,0:T(8,128)S(1)}, f32[1,128]{1,0:T(1,128)S(1)}) custom-call(bf16[1024,1024]{1,0:T(8,128)(2,1)S(1)} %shard_map.57.target_ref, bf16[128,1152]{1,0:T(8,128)(2,1)S(1)} %collective-permute-done.8.refs_0_, bf16[64,1152]{1,0:T(8,128)(2,1)S(1)} %collective-permute-done.10.refs_1_, f32[1024,128]{1,0:T(8,128)S(1)} %get-tuple-element.22.refs_2_, ...), custom_call_target="tpu_custom_call" | custom-call | flops 1 | bytes 1 | tf_op jit(solution)/shard_map/pallas_call | solution.py:176
  25.8 0.4 collective-permute-start.11
  26.2 0.8 %collective-permute-done.11 = f32[1,128]{1,0:T(1,128)S(1)} collective-permute-done((f32[1,128]{1,0:T(1,128)S(1)}, f32[1,128]{1,0:T(1,128)S(1)}, u32[]{:S(2)}, u32[]{:S(2)}) %collective-permute-start.11) | collective-permute-done | bytes 544 | tf_op jit(solution)/shard_map/ppermute | solution.py:22
  27.0 1.6 %collective-permute-start.12 = (f32[1,128]{1,0:T(1,128)S(1)}, f32[1,128]{1,0:T(1,128)S(1)}, u32[]{:S(2)}, u32[]{:S(2)}) collective-permute-start(f32[1,128]{1,0:T(1,128)S(1)} %add.32), channel_id=1, source_target_pairs={{0,2},{1,3},{2,0},{3,1},{4,6},{5,7},{6,4},{7,5},{8,10},{9,11},{10,... | collective-permute-start | bytes 1544 | tf_op jit(solution)/shard_map/ppermute | solution.py:22
  28.6 0.9 %collective-permute-start.13 = (f32[1,128]{1,0:T(1,128)S(1)}, f32[1,128]{1,0:T(1,128)S(1)}, u32[]{:S(2)}, u32[]{:S(2)}) collective-permute-start(f32[1,128]{1,0:T(1,128)S(1)} %add.32), channel_id=1, source_target_pairs={{0,4},{1,5},{2,6},{3,7},{4,0},{5,1},{6,2},{7,3},{8,12},{9,13},{10,... | collective-permute-start | bytes 1544 | tf_op jit(solution)/shard_map/ppermute | solution.py:22
  29.4 1.0 %collective-permute-start.14 = (f32[1,128]{1,0:T(1,128)S(1)}, f32[1,128]{1,0:T(1,128)S(1)}, u32[]{:S(2)}, u32[]{:S(2)}) collective-permute-start(f32[1,128]{1,0:T(1,128)S(1)} %add.32), channel_id=1, source_target_pairs={{0,6},{1,7},{2,4},{3,5},{4,2},{5,3},{6,0},{7,1},{8,14},{9,15},{10,... | collective-permute-start | bytes 1544 | tf_op jit(solution)/shard_map/ppermute | solution.py:22
  30.5 0.1 collective-permute-done.12
  30.5 1.6 %collective-permute-done.13 = f32[1,128]{1,0:T(1,128)S(1)} collective-permute-done((f32[1,128]{1,0:T(1,128)S(1)}, f32[1,128]{1,0:T(1,128)S(1)}, u32[]{:S(2)}, u32[]{:S(2)}) %collective-permute-start.13) | collective-permute-done | bytes 544 | tf_op jit(solution)/shard_map/ppermute | solution.py:22
  32.1 1.8 %collective-permute-done.14 = f32[1,128]{1,0:T(1,128)S(1)} collective-permute-done((f32[1,128]{1,0:T(1,128)S(1)}, f32[1,128]{1,0:T(1,128)S(1)}, u32[]{:S(2)}, u32[]{:S(2)}) %collective-permute-start.14) | collective-permute-done | bytes 544 | tf_op jit(solution)/shard_map/ppermute | solution.py:22
  33.9 2.2 %collective-permute-start.15 = (f32[1,128]{1,0:T(1,128)S(1)}, f32[1,128]{1,0:T(1,128)S(1)}, u32[]{:S(2)}, u32[]{:S(2)}) collective-permute-start(f32[1,128]{1,0:T(1,128)S(1)} %add_add_fusion), channel_id=1, source_target_pairs={{0,8},{1,9},{2,10},{3,11},{4,12},{5,13},{6,14},{7,15},{8,0},{9,1},... | collective-permute-start | bytes 1544 | tf_op jit(solution)/shard_map/ppermute | solution.py:22
  36.1 2.2 %collective-permute-done.15 = f32[1,128]{1,0:T(1,128)S(1)} collective-permute-done((f32[1,128]{1,0:T(1,128)S(1)}, f32[1,128]{1,0:T(1,128)S(1)}, u32[]{:S(2)}, u32[]{:S(2)}) %collective-permute-start.15) | collective-permute-done | bytes 544 | tf_op jit(solution)/shard_map/ppermute | solution.py:22
  38.3 0.8 %broadcast_divide_fusion = f32[1024,128]{1,0:T(8,128)} fusion(f32[1024,128]{1,0:T(8,128)S(1)} %get-tuple-element.25, f32[128]{0:T(128)S(1)} %sqrt_bitcast_fusion), kind=kLoop, calls=%fused_computation | loop fusion | flops 131072 | bytes 1049088 | tf_op jit(solution)/shard_map/div | solution.py:220
  (7 shorter events, 0.1 us)
Async XLA Ops:
  0.9 3.2 %collective-permute-start = (bf16[64,1152]{1,0:T(8,128)(2,1)S(1)}, bf16[64,1152]{1,0:T(8,128)(2,1)S(1)}, u32[]{:S(2)}, u32[]{:S(2)}) collective-permute-start(bf16[64,1152]{1,0:T(8,128)(2,1)S(1)} %shard_map.55.refs_0_), channel_id=1, source_target_pairs={{0,1},{1,0},{2,3},{3,2},{4,5},{5,4},{6,7},{7,6},{8,9},{9,8},{10,11... | collective-permute-start | bytes 442376 | tf_op jit(solution)/shard_map/ppermute | solution.py:22
  1.4 8.5 %collective-permute-start.1 = (bf16[64,1152]{1,0:T(8,128)(2,1)S(1)}, bf16[64,1152]{1,0:T(8,128)(2,1)S(1)}, u32[]{:S(2)}, u32[]{:S(2)}) collective-permute-start(bf16[64,1152]{1,0:T(8,128)(2,1)S(1)} %shard_map.55.refs_0_), channel_id=1, source_target_pairs={{0,4},{1,5},{2,6},{3,7},{4,12},{5,13},{6,14},{7,15},{8,0},{9,1},{1... | collective-permute-start | bytes 442376 | tf_op jit(solution)/shard_map/ppermute | solution.py:36
  4.1 8.7 %collective-permute-start.2 = (bf16[64,1152]{1,0:T(8,128)(2,1)S(1)}, bf16[64,1152]{1,0:T(8,128)(2,1)S(1)}, u32[]{:S(2)}, u32[]{:S(2)}) collective-permute-start(bf16[64,1152]{1,0:T(8,128)(2,1)S(1)} %shard_map.56.token_ref), channel_id=1, source_target_pairs={{0,8},{1,9},{2,10},{3,11},{4,0},{5,1},{6,2},{7,3},{8,12},{9,13},{1... | collective-permute-start | bytes 442376 | tf_op jit(solution)/shard_map/ppermute | solution.py:36
  6.5 10.0 %collective-permute-start.5 = (bf16[64,1152]{1,0:T(8,128)(2,1)S(1)}, bf16[64,1152]{1,0:T(8,128)(2,1)S(1)}, u32[]{:S(2)}, u32[]{:S(2)}) collective-permute-start(bf16[64,1152]{1,0:T(8,128)(2,1)S(1)} %shard_map.56.token_ref), channel_id=1, source_target_pairs={{0,2},{1,3},{2,0},{3,1},{4,6},{5,7},{6,4},{7,5},{8,10},{9,11},{10,... | collective-permute-start | bytes 442376 | tf_op jit(solution)/shard_map/ppermute | solution.py:22
  8.0 8.9 %collective-permute-start.6 = (bf16[64,1152]{1,0:T(8,128)(2,1)S(1)}, bf16[64,1152]{1,0:T(8,128)(2,1)S(1)}, u32[]{:S(2)}, u32[]{:S(2)}) collective-permute-start(bf16[64,1152]{1,0:T(8,128)(2,1)S(1)} %shard_map.56.token_ref), channel_id=1, source_target_pairs={{0,6},{1,7},{2,4},{3,5},{4,2},{5,3},{6,0},{7,1},{8,14},{9,15},{10,... | collective-permute-start | bytes 442376 | tf_op jit(solution)/shard_map/ppermute | solution.py:22
  12.8 8.4 %collective-permute-start.3 = (bf16[64,1152]{1,0:T(8,128)(2,1)S(1)}, bf16[64,1152]{1,0:T(8,128)(2,1)S(1)}, u32[]{:S(2)}, u32[]{:S(2)}) collective-permute-start(bf16[64,1152]{1,0:T(8,128)(2,1)S(1)} %broadcast_select_fusion), channel_id=1, source_target_pairs={{0,2},{1,5},{2,0},{3,7},{4,6},{5,1},{6,4},{7,3},{8,10},{9,13},{10,... | collective-permute-start | bytes 442376 | tf_op jit(solution)/shard_map/ppermute | solution.py:27
  14.4 6.8 %collective-permute-start.4 = (bf16[64,1152]{1,0:T(8,128)(2,1)S(1)}, bf16[64,1152]{1,0:T(8,128)(2,1)S(1)}, u32[]{:S(2)}, u32[]{:S(2)}) collective-permute-start(bf16[64,1152]{1,0:T(8,128)(2,1)S(1)} %broadcast_select_fusion), channel_id=1, source_target_pairs={{0,4},{1,3},{2,6},{3,1},{4,0},{5,7},{6,2},{7,5},{8,12},{9,11},{10,... | collective-permute-start | bytes 442376 | tf_op jit(solution)/shard_map/ppermute | solution.py:27
  16.5 6.7 %collective-permute-start.9 = (bf16[64,1152]{1,0:T(8,128)(2,1)S(1)}, bf16[64,1152]{1,0:T(8,128)(2,1)S(1)}, u32[]{:S(2)}, u32[]{:S(2)}) collective-permute-start(bf16[64,1152]{1,0:T(8,128)(2,1)S(1)} %broadcast_select_fusion), channel_id=1, source_target_pairs={{0,6},{1,7},{2,4},{3,5},{4,2},{5,3},{6,0},{7,1},{8,14},{9,15},{10,... | collective-permute-start | bytes 442376 | tf_op jit(solution)/shard_map/ppermute | solution.py:27
  17.0 2.1 %collective-permute-start.7 = (bf16[256,1152]{1,0:T(8,128)(2,1)S(1)}, bf16[256,1152]{1,0:T(8,128)(2,1)S(1)}, u32[]{:S(2)}, u32[]{:S(2)}) collective-permute-start(bf16[256,1152]{1,0:T(8,128)(2,1)S(1)} %shard_map.58), channel_id=1, source_target_pairs={{0,1},{1,0},{2,3},{3,2},{4,5},{5,4},{6,7},{7,6},{8,9},{9,8},{10,11... | collective-permute-start | bytes 1769480 | tf_op jit(solution)/shard_map/ppermute | solution.py:22
  21.2 3.3 %copy-start = (f32[1024,128]{1,0:T(8,128)S(1)}, f32[1024,128]{1,0:T(8,128)}, u32[]{:S(2)}) copy-start(f32[1024,128]{1,0:T(8,128)} %refs_5_.1) | copy-start | bytes 1572868
  21.3 3.3 %copy-start.1 = (f32[1024,128]{1,0:T(8,128)S(1)}, f32[1024,128]{1,0:T(8,128)}, u32[]{:S(2)}) copy-start(f32[1024,128]{1,0:T(8,128)} %refs_6_.1) | copy-start | bytes 1572868
  21.3 3.3 %collective-permute-start.8 = (bf16[128,1152]{1,0:T(8,128)(2,1)S(1)}, bf16[128,1152]{1,0:T(8,128)(2,1)S(1)}, u32[]{:S(2)}, u32[]{:S(2)}) collective-permute-start(bf16[128,1152]{1,0:T(8,128)(2,1)S(1)} %shard_map.61), channel_id=1, source_target_pairs={{0,1},{1,0},{2,3},{3,2},{4,5},{5,4},{6,7},{7,6},{8,9},{9,8},{10,11... | collective-permute-start | bytes 884744 | tf_op jit(solution)/shard_map/ppermute | solution.py:22
  23.2 1.4 %collective-permute-start.10 = (bf16[64,1152]{1,0:T(8,128)(2,1)S(1)}, bf16[64,1152]{1,0:T(8,128)(2,1)S(1)}, u32[]{:S(2)}, u32[]{:S(2)}) collective-permute-start(bf16[64,1152]{1,0:T(8,128)(2,1)S(1)} %collective-permute-done.9.refs_2_), channel_id=1, source_target_pairs={{0,1},{1,0},{2,3},{3,2},{4,5},{5,4},{6,7},{7,6},{8,9},{9,8},{10,11... | collective-permute-start | bytes 442376 | tf_op jit(solution)/shard_map/ppermute | solution.py:22
  25.8 1.2 %collective-permute-start.11 = (f32[1,128]{1,0:T(1,128)S(1)}, f32[1,128]{1,0:T(1,128)S(1)}, u32[]{:S(2)}, u32[]{:S(2)}) collective-permute-start(f32[1,128]{1,0:T(1,128)S(1)} %get-tuple-element.26), channel_id=1, source_target_pairs={{0,1},{1,0},{2,3},{3,2},{4,5},{5,4},{6,7},{7,6},{8,9},{9,8},{10,11... | collective-permute-start | bytes 1544 | tf_op jit(solution)/shard_map/ppermute | solution.py:22
  27.0 3.5 %collective-permute-start.12 = (f32[1,128]{1,0:T(1,128)S(1)}, f32[1,128]{1,0:T(1,128)S(1)}, u32[]{:S(2)}, u32[]{:S(2)}) collective-permute-start(f32[1,128]{1,0:T(1,128)S(1)} %add.32), channel_id=1, source_target_pairs={{0,2},{1,3},{2,0},{3,1},{4,6},{5,7},{6,4},{7,5},{8,10},{9,11},{10,... | collective-permute-start | bytes 1544 | tf_op jit(solution)/shard_map/ppermute | solution.py:22
  28.6 3.5 %collective-permute-start.13 = (f32[1,128]{1,0:T(1,128)S(1)}, f32[1,128]{1,0:T(1,128)S(1)}, u32[]{:S(2)}, u32[]{:S(2)}) collective-permute-start(f32[1,128]{1,0:T(1,128)S(1)} %add.32), channel_id=1, source_target_pairs={{0,4},{1,5},{2,6},{3,7},{4,0},{5,1},{6,2},{7,3},{8,12},{9,13},{10,... | collective-permute-start | bytes 1544 | tf_op jit(solution)/shard_map/ppermute | solution.py:22
  29.4 4.4 %collective-permute-start.14 = (f32[1,128]{1,0:T(1,128)S(1)}, f32[1,128]{1,0:T(1,128)S(1)}, u32[]{:S(2)}, u32[]{:S(2)}) collective-permute-start(f32[1,128]{1,0:T(1,128)S(1)} %add.32), channel_id=1, source_target_pairs={{0,6},{1,7},{2,4},{3,5},{4,2},{5,3},{6,0},{7,1},{8,14},{9,15},{10,... | collective-permute-start | bytes 1544 | tf_op jit(solution)/shard_map/ppermute | solution.py:22
  33.9 4.4 %collective-permute-start.15 = (f32[1,128]{1,0:T(1,128)S(1)}, f32[1,128]{1,0:T(1,128)S(1)}, u32[]{:S(2)}, u32[]{:S(2)}) collective-permute-start(f32[1,128]{1,0:T(1,128)S(1)} %add_add_fusion), channel_id=1, source_target_pairs={{0,8},{1,9},{2,10},{3,11},{4,12},{5,13},{6,14},{7,15},{8,0},{9,1},... | collective-permute-start | bytes 1544 | tf_op jit(solution)/shard_map/ppermute | solution.py:22

commit v7 on v6

--- a/solution.py
+++ b/solution.py
@@ -41,7 +41,10 @@
     if n & (n - 1) or n < 16:
         return lax.psum(x, "tgt")
     x = x + swap(x, 1)
-    x = x + sum(swap(x, k) for k in (2, 4, 6))
+    one = swap_by_core(x, 4, 6)
+    two = swap_by_core(x, 2, 4)
+    x = jnp.where(lax.axis_index("tgt") % 2 == 0, x + one + two, one)
+    x = x + swap(x, 1)
     bit = 8
     while bit < n:
         x = x + swap(x, bit)

time: 39.3 us -> 38.4 us (0.977)
  waiting for transfers between devices: 11.8 us -> 10.8 us
    ppermute x11 -> x9, waiting for transfers between devices: 7.19 us -> 4.23 us  [swap(): return lax.ppermute(x, 'tgt', [(i, i ^ bits) for i in range(n)])]
    ppermute x11 -> x9, starting transfers between devices: 9.36 us -> 6.89 us  [swap(): return lax.ppermute(x, 'tgt', [(i, i ^ bits) for i in range(n)])]
    ppermute x3 -> x5, starting transfers between devices: 3.74 us -> 6.18 us  [swap_by_core(): lax.ppermute(x, 'tgt', [(i, i ^ (second if i % 2 else first)) for i in ra...]
    ppermute x3 -> x5, waiting for transfers between devices: 1.72 us -> 3.76 us  [swap_by_core(): lax.ppermute(x, 'tgt', [(i, i ^ (second if i % 2 else first)) for i in ra...]
where the time goes in v7:
time: 38.4 us; the launch traced here: 38.2 us
  starting transfers between devices  18.1 us (47%)
  waiting for transfers between devices  10.8 us (28%)
  Pallas kernels  8.34 us (22%)
  other arithmetic  0.88 us (2%)
    ppermute x9, starting transfers between devices, swap(): return lax.ppermute(x, 'tgt', [(i, i ^ bits) for i in range(n)])  6.89 us
    ppermute x5, starting transfers between devices, swap_by_core(): lax.ppermute(x, 'tgt', [(i, i ^ (second if i % 2 else first)) for i in ra...  6.18 us
    pallas_call x4, Pallas kernels, step(): pl.pallas_call(functools.partial(step_kernel, scale, len(pieces), not sta...  5.77 us
    ppermute x2, starting transfers between devices, cross(): return lax.ppermute(x, 'tgt', pairs)  5 us
    ppermute x9, waiting for transfers between devices, swap(): return lax.ppermute(x, 'tgt', [(i, i ^ bits) for i in range(n)])  4.23 us
    ppermute x5, waiting for transfers between devices, swap_by_core(): lax.ppermute(x, 'tgt', [(i, i ^ (second if i % 2 else first)) for i in ra...  3.76 us
    ppermute x2, waiting for transfers between devices, cross(): return lax.ppermute(x, 'tgt', pairs)  2.84 us
    pallas_call x1, Pallas kernels, load(): pl.pallas_call(load_kernel, out_shape=jax.ShapeDtypeStruct(array.shape, a...  1.57 us
  transfers between devices with their start and end apart: 16, of which 11 were waited for; matrix products, arithmetic and copies ran while one was open for 0% of the time, Pallas kernels for 16%

profile of v7, /device:TPU:0, one launch (start us, length us, event | category | flops | bytes accessed | tf_op | source)
XLA Modules:
  0.0 38.2 jit_solution(7423066404344732412)
XLA Ops:
  0.0 0.9 %shard_map.55.refs_0_ = bf16[64,1152]{1,0:T(8,128)(2,1)S(1)} custom-call(bf16[64,1024]{1,0:T(8,128)(2,1)} %feats_ref.1, bf16[64,128]{1,0:T(8,128)(2,1)} %vecs_ref.1), custom_call_target="tpu_custom_call" | custom-call | tf_op jit(solution)/shard_map/pallas_call | solution.py:67
  0.9 0.5 %collective-permute-start = (bf16[64,1152]{1,0:T(8,128)(2,1)S(1)}, bf16[64,1152]{1,0:T(8,128)(2,1)S(1)}, u32[]{:S(2)}, u32[]{:S(2)}) collective-permute-start(bf16[64,1152]{1,0:T(8,128)(2,1)S(1)} %shard_map.55.refs_0_), channel_id=1, source_target_pairs={{0,1},{1,0},{2,3},{3,2},{4,5},{5,4},{6,7},{7,6},{8,9},{9,8},{10,11... | collective-permute-start | bytes 442376 | tf_op jit(solution)/shard_map/ppermute | solution.py:22
  1.4 2.6 %collective-permute-start.1 = (bf16[64,1152]{1,0:T(8,128)(2,1)S(1)}, bf16[64,1152]{1,0:T(8,128)(2,1)S(1)}, u32[]{:S(2)}, u32[]{:S(2)}) collective-permute-start(bf16[64,1152]{1,0:T(8,128)(2,1)S(1)} %shard_map.55.refs_0_), channel_id=1, source_target_pairs={{0,4},{1,5},{2,6},{3,7},{4,12},{5,13},{6,14},{7,15},{8,0},{9,1},{1... | collective-permute-start | bytes 442376 | tf_op jit(solution)/shard_map/ppermute | solution.py:36
  4.1 0.0 collective-permute-done.refs_1_
  4.1 2.4 %collective-permute-start.2 = (bf16[64,1152]{1,0:T(8,128)(2,1)S(1)}, bf16[64,1152]{1,0:T(8,128)(2,1)S(1)}, u32[]{:S(2)}, u32[]{:S(2)}) collective-permute-start(bf16[64,1152]{1,0:T(8,128)(2,1)S(1)} %shard_map.56.token_ref), channel_id=1, source_target_pairs={{0,8},{1,9},{2,10},{3,11},{4,0},{5,1},{6,2},{7,3},{8,12},{9,13},{1... | collective-permute-start | bytes 442376 | tf_op jit(solution)/shard_map/ppermute | solution.py:36
  6.5 1.5 %collective-permute-start.5 = (bf16[64,1152]{1,0:T(8,128)(2,1)S(1)}, bf16[64,1152]{1,0:T(8,128)(2,1)S(1)}, u32[]{:S(2)}, u32[]{:S(2)}) collective-permute-start(bf16[64,1152]{1,0:T(8,128)(2,1)S(1)} %shard_map.56.token_ref), channel_id=1, source_target_pairs={{0,2},{1,3},{2,0},{3,1},{4,6},{5,7},{6,4},{7,5},{8,10},{9,11},{10,... | collective-permute-start | bytes 442376 | tf_op jit(solution)/shard_map/ppermute | solution.py:22
  8.0 0.3 collective-permute-start.6
  8.3 1.6 %shard_map.57.target_ref = bf16[1024,1024]{1,0:T(8,128)(2,1)S(1)} custom-call(bf16[1024,1024]{1,0:T(8,128)(2,1)} %array_ref.1, bf16[64,1152]{1,0:T(8,128)(2,1)S(1)} %shard_map.56.token_ref), custom_call_target="tpu_custom_call" | custom-call | flops 1 | bytes 1 | tf_op jit(solution)/shard_map/pallas_call | solution.py:116
  9.9 0.0 collective-permute-done.1.refs_0_.refs_2_
  9.9 2.8 %collective-permute-done.2.refs_1_.refs_3_ = bf16[64,1152]{1,0:T(8,128)(2,1)S(1)} collective-permute-done((bf16[64,1152]{1,0:T(8,128)(2,1)S(1)}, bf16[64,1152]{1,0:T(8,128)(2,1)S(1)}, u32[]{:S(2)}, u32[]{:S(2)}) %collective-permute-start.2) | collective-permute-done | bytes 147488 | tf_op jit(solution)/shard_map/ppermute | solution.py:36
  12.8 1.6 %collective-permute-start.3 = (bf16[64,1152]{1,0:T(8,128)(2,1)S(1)}, bf16[64,1152]{1,0:T(8,128)(2,1)S(1)}, u32[]{:S(2)}, u32[]{:S(2)}) collective-permute-start(bf16[64,1152]{1,0:T(8,128)(2,1)S(1)} %broadcast_select_fusion), channel_id=1, source_target_pairs={{0,2},{1,5},{2,0},{3,7},{4,6},{5,1},{6,4},{7,3},{8,10},{9,13},{10,... | collective-permute-start | bytes 442376 | tf_op jit(solution)/shard_map/ppermute | solution.py:27
  14.4 2.1 %collective-permute-start.4 = (bf16[64,1152]{1,0:T(8,128)(2,1)S(1)}, bf16[64,1152]{1,0:T(8,128)(2,1)S(1)}, u32[]{:S(2)}, u32[]{:S(2)}) collective-permute-start(bf16[64,1152]{1,0:T(8,128)(2,1)S(1)} %broadcast_select_fusion), channel_id=1, source_target_pairs={{0,4},{1,3},{2,6},{3,1},{4,0},{5,7},{6,2},{7,5},{8,12},{9,11},{10,... | collective-permute-start | bytes 442376 | tf_op jit(solution)/shard_map/ppermute | solution.py:27
  16.5 0.0 collective-permute-start.9
  16.5 0.0 collective-permute-done.5.refs_2_.refs_4_
  16.5 0.4 %collective-permute-done.6.refs_3_.refs_5_ = bf16[64,1152]{1,0:T(8,128)(2,1)S(1)} collective-permute-done((bf16[64,1152]{1,0:T(8,128)(2,1)S(1)}, bf16[64,1152]{1,0:T(8,128)(2,1)S(1)}, u32[]{:S(2)}, u32[]{:S(2)}) %collective-permute-start.6) | collective-permute-done | bytes 147488 | tf_op jit(solution)/shard_map/ppermute | solution.py:22
  17.0 0.1 collective-permute-start.7
  17.1 1.9 %shard_map.59 = (f32[1024,128]{1,0:T(8,128)S(1)}, f32[1024,128]{1,0:T(8,128)S(1)}, f32[1024,128]{1,0:T(8,128)S(1)}) custom-call(bf16[1024,1024]{1,0:T(8,128)(2,1)S(1)} %shard_map.57.target_ref, bf16[64,1152]{1,0:T(8,128)(2,1)S(1)} %shard_map.55.refs_0_, bf16[64,1152]{1,0:T(8,128)(2,1)S(1)} %collective-permute-done.refs_1_, ...), custom_call_target="tpu_custom_call" | custom-call | flops 20000000000 | bytes 1 | tf_op jit(solution)/shard_map/pallas_call | solution.py:179
  18.9 0.1 collective-permute-done.7.refs_0_
  19.0 1.6 %shard_map.60 = (f32[1024,128]{1,0:T(8,128)S(1)}, f32[1024,128]{1,0:T(8,128)S(1)}, f32[1024,128]{1,0:T(8,128)S(1)}) custom-call(bf16[1024,1024]{1,0:T(8,128)(2,1)S(1)} %shard_map.57.target_ref, bf16[256,1152]{1,0:T(8,128)(2,1)S(1)} %collective-permute-done.7.refs_0_, f32[1024,128]{1,0:T(8,128)S(1)} %get-tuple-element.16.refs_1_, ...), custom_call_target="tpu_custom_call" | custom-call | flops 20000000000 | bytes 1 | tf_op jit(solution)/shard_map/pallas_call | solution.py:179
  20.6 0.6 %collective-permute-done.3.refs_0_ = bf16[64,1152]{1,0:T(8,128)(2,1)S(1)} collective-permute-done((bf16[64,1152]{1,0:T(8,128)(2,1)S(1)}, bf16[64,1152]{1,0:T(8,128)(2,1)S(1)}, u32[]{:S(2)}, u32[]{:S(2)}) %collective-permute-start.3) | collective-permute-done | bytes 147488 | tf_op jit(solution)/shard_map/ppermute | solution.py:27
  21.2 0.0 collective-permute-done.4.refs_1_
  21.2 0.0 copy-start
  21.3 0.0 copy-start.1
  21.3 0.8 %collective-permute-start.8 = (bf16[128,1152]{1,0:T(8,128)(2,1)S(1)}, bf16[128,1152]{1,0:T(8,128)(2,1)S(1)}, u32[]{:S(2)}, u32[]{:S(2)}) collective-permute-start(bf16[128,1152]{1,0:T(8,128)(2,1)S(1)} %shard_map.61), channel_id=1, source_target_pairs={{0,1},{1,0},{2,3},{3,2},{4,5},{5,4},{6,7},{7,6},{8,9},{9,8},{10,11... | collective-permute-start | bytes 884744 | tf_op jit(solution)/shard_map/ppermute | solution.py:22
  22.1 1.1 %collective-permute-done.9.refs_2_ = bf16[64,1152]{1,0:T(8,128)(2,1)S(1)} collective-permute-done((bf16[64,1152]{1,0:T(8,128)(2,1)S(1)}, bf16[64,1152]{1,0:T(8,128)(2,1)S(1)}, u32[]{:S(2)}, u32[]{:S(2)}) %collective-permute-start.9) | collective-permute-done | bytes 147488 | tf_op jit(solution)/shard_map/ppermute | solution.py:27
  23.2 0.0 collective-permute-start.10
  23.2 1.1 %shard_map.62 = (f32[1024,128]{1,0:T(8,128)S(1)}, f32[1024,128]{1,0:T(8,128)S(1)}, f32[1024,128]{1,0:T(8,128)S(1)}) custom-call(bf16[1024,1024]{1,0:T(8,128)(2,1)S(1)} %shard_map.57.target_ref, bf16[64,1152]{1,0:T(8,128)(2,1)S(1)} %collective-permute-done.3.refs_0_, bf16[64,1152]{1,0:T(8,128)(2,1)S(1)} %collective-permute-done.4.refs_1_, ...), custom_call_target="tpu_custom_call" | custom-call | flops 1 | bytes 1 | tf_op jit(solution)/shard_map/pallas_call | solution.py:179
  24.3 0.2 collective-permute-done.10.refs_1_
  24.6 0.0 collective-permute-done.8.refs_0_
  24.6 0.0 copy-done
  24.6 0.0 copy-done.1
  24.6 1.2 %shard_map.63 = (f32[1024,128]{1,0:T(8,128)S(1)}, f32[1,128]{1,0:T(1,128)S(1)}) custom-call(bf16[1024,1024]{1,0:T(8,128)(2,1)S(1)} %shard_map.57.target_ref, bf16[128,1152]{1,0:T(8,128)(2,1)S(1)} %collective-permute-done.8.refs_0_, bf16[64,1152]{1,0:T(8,128)(2,1)S(1)} %collective-permute-done.10.refs_1_, f32[1024,128]{1,0:T(8,128)S(1)} %get-tuple-element.22.refs_2_, ...), custom_call_target="tpu_custom_call" | custom-call | flops 1 | bytes 1 | tf_op jit(solution)/shard_map/pallas_call | solution.py:179
  25.8 0.4 collective-permute-start.11
  26.2 0.8 %collective-permute-done.11 = f32[1,128]{1,0:T(1,128)S(1)} collective-permute-done((f32[1,128]{1,0:T(1,128)S(1)}, f32[1,128]{1,0:T(1,128)S(1)}, u32[]{:S(2)}, u32[]{:S(2)}) %collective-permute-start.11) | collective-permute-done | bytes 544 | tf_op jit(solution)/shard_map/ppermute | solution.py:22
  27.0 0.9 %collective-permute-start.12 = (f32[1,128]{1,0:T(1,128)S(1)}, f32[1,128]{1,0:T(1,128)S(1)}, u32[]{:S(2)}, u32[]{:S(2)}) collective-permute-start(f32[1,128]{1,0:T(1,128)S(1)} %add.36), channel_id=1, source_target_pairs={{0,4},{1,7},{2,6},{3,5},{4,0},{5,3},{6,2},{7,1},{8,12},{9,15},{10,... | collective-permute-start | bytes 1544 | tf_op jit(solution)/shard_map/ppermute | solution.py:27
  27.9 1.5 %collective-permute-start.13 = (f32[1,128]{1,0:T(1,128)S(1)}, f32[1,128]{1,0:T(1,128)S(1)}, u32[]{:S(2)}, u32[]{:S(2)}) collective-permute-start(f32[1,128]{1,0:T(1,128)S(1)} %add.36), channel_id=1, source_target_pairs={{0,2},{1,5},{2,0},{3,7},{4,6},{5,1},{6,4},{7,3},{8,10},{9,13},{10,... | collective-permute-start | bytes 1544 | tf_op jit(solution)/shard_map/ppermute | solution.py:27
  29.4 1.1 %collective-permute-done.12 = f32[1,128]{1,0:T(1,128)S(1)} collective-permute-done((f32[1,128]{1,0:T(1,128)S(1)}, f32[1,128]{1,0:T(1,128)S(1)}, u32[]{:S(2)}, u32[]{:S(2)}) %collective-permute-start.12) | collective-permute-done | bytes 544 | tf_op jit(solution)/shard_map/ppermute | solution.py:27
  30.5 0.9 %collective-permute-done.13 = f32[1,128]{1,0:T(1,128)S(1)} collective-permute-done((f32[1,128]{1,0:T(1,128)S(1)}, f32[1,128]{1,0:T(1,128)S(1)}, u32[]{:S(2)}, u32[]{:S(2)}) %collective-permute-start.13) | collective-permute-done | bytes 544 | tf_op jit(solution)/shard_map/ppermute | solution.py:27
  31.5 0.0 collective-permute-start.14
  31.5 1.1 %collective-permute-done.14 = f32[1,128]{1,0:T(1,128)S(1)} collective-permute-done((f32[1,128]{1,0:T(1,128)S(1)}, f32[1,128]{1,0:T(1,128)S(1)}, u32[]{:S(2)}, u32[]{:S(2)}) %collective-permute-start.14) | collective-permute-done | bytes 544 | tf_op jit(solution)/shard_map/ppermute | solution.py:22
  32.6 3.2 %collective-permute-start.15 = (f32[1,128]{1,0:T(1,128)S(1)}, f32[1,128]{1,0:T(1,128)S(1)}, u32[]{:S(2)}, u32[]{:S(2)}) collective-permute-start(f32[1,128]{1,0:T(1,128)S(1)} %add.39), channel_id=1, source_target_pairs={{0,8},{1,9},{2,10},{3,11},{4,12},{5,13},{6,14},{7,15},{8,0},{9,1},... | collective-permute-start | bytes 1544 | tf_op jit(solution)/shard_map/ppermute | solution.py:22
  35.9 1.5 %collective-permute-done.15 = f32[1,128]{1,0:T(1,128)S(1)} collective-permute-done((f32[1,128]{1,0:T(1,128)S(1)}, f32[1,128]{1,0:T(1,128)S(1)}, u32[]{:S(2)}, u32[]{:S(2)}) %collective-permute-start.15) | collective-permute-done | bytes 544 | tf_op jit(solution)/shard_map/ppermute | solution.py:22
  37.4 0.8 %broadcast_divide_fusion = f32[1024,128]{1,0:T(8,128)} fusion(f32[1024,128]{1,0:T(8,128)S(1)} %get-tuple-element.25, f32[128]{0:T(128)S(1)} %sqrt_bitcast_fusion), kind=kLoop, calls=%fused_computation | loop fusion | flops 131072 | bytes 1049088 | tf_op jit(solution)/shard_map/div | solution.py:223
  (8 shorter events, 0.1 us)
Async XLA Ops:
  0.9 3.2 %collective-permute-start = (bf16[64,1152]{1,0:T(8,128)(2,1)S(1)}, bf16[64,1152]{1,0:T(8,128)(2,1)S(1)}, u32[]{:S(2)}, u32[]{:S(2)}) collective-permute-start(bf16[64,1152]{1,0:T(8,128)(2,1)S(1)} %shard_map.55.refs_0_), channel_id=1, source_target_pairs={{0,1},{1,0},{2,3},{3,2},{4,5},{5,4},{6,7},{7,6},{8,9},{9,8},{10,11... | collective-permute-start | bytes 442376 | tf_op jit(solution)/shard_map/ppermute | solution.py:22
  1.4 8.5 %collective-permute-start.1 = (bf16[64,1152]{1,0:T(8,128)(2,1)S(1)}, bf16[64,1152]{1,0:T(8,128)(2,1)S(1)}, u32[]{:S(2)}, u32[]{:S(2)}) collective-permute-start(bf16[64,1152]{1,0:T(8,128)(2,1)S(1)} %shard_map.55.refs_0_), channel_id=1, source_target_pairs={{0,4},{1,5},{2,6},{3,7},{4,12},{5,13},{6,14},{7,15},{8,0},{9,1},{1... | collective-permute-start | bytes 442376 | tf_op jit(solution)/shard_map/ppermute | solution.py:36
  4.1 8.7 %collective-permute-start.2 = (bf16[64,1152]{1,0:T(8,128)(2,1)S(1)}, bf16[64,1152]{1,0:T(8,128)(2,1)S(1)}, u32[]{:S(2)}, u32[]{:S(2)}) collective-permute-start(bf16[64,1152]{1,0:T(8,128)(2,1)S(1)} %shard_map.56.token_ref), channel_id=1, source_target_pairs={{0,8},{1,9},{2,10},{3,11},{4,0},{5,1},{6,2},{7,3},{8,12},{9,13},{1... | collective-permute-start | bytes 442376 | tf_op jit(solution)/shard_map/ppermute | solution.py:36
  6.5 10.0 %collective-permute-start.5 = (bf16[64,1152]{1,0:T(8,128)(2,1)S(1)}, bf16[64,1152]{1,0:T(8,128)(2,1)S(1)}, u32[]{:S(2)}, u32[]{:S(2)}) collective-permute-start(bf16[64,1152]{1,0:T(8,128)(2,1)S(1)} %shard_map.56.token_ref), channel_id=1, source_target_pairs={{0,2},{1,3},{2,0},{3,1},{4,6},{5,7},{6,4},{7,5},{8,10},{9,11},{10,... | collective-permute-start | bytes 442376 | tf_op jit(solution)/shard_map/ppermute | solution.py:22
  8.0 8.9 %collective-permute-start.6 = (bf16[64,1152]{1,0:T(8,128)(2,1)S(1)}, bf16[64,1152]{1,0:T(8,128)(2,1)S(1)}, u32[]{:S(2)}, u32[]{:S(2)}) collective-permute-start(bf16[64,1152]{1,0:T(8,128)(2,1)S(1)} %shard_map.56.token_ref), channel_id=1, source_target_pairs={{0,6},{1,7},{2,4},{3,5},{4,2},{5,3},{6,0},{7,1},{8,14},{9,15},{10,... | collective-permute-start | bytes 442376 | tf_op jit(solution)/shard_map/ppermute | solution.py:22
  12.8 8.4 %collective-permute-start.3 = (bf16[64,1152]{1,0:T(8,128)(2,1)S(1)}, bf16[64,1152]{1,0:T(8,128)(2,1)S(1)}, u32[]{:S(2)}, u32[]{:S(2)}) collective-permute-start(bf16[64,1152]{1,0:T(8,128)(2,1)S(1)} %broadcast_select_fusion), channel_id=1, source_target_pairs={{0,2},{1,5},{2,0},{3,7},{4,6},{5,1},{6,4},{7,3},{8,10},{9,13},{10,... | collective-permute-start | bytes 442376 | tf_op jit(solution)/shard_map/ppermute | solution.py:27
  14.4 6.8 %collective-permute-start.4 = (bf16[64,1152]{1,0:T(8,128)(2,1)S(1)}, bf16[64,1152]{1,0:T(8,128)(2,1)S(1)}, u32[]{:S(2)}, u32[]{:S(2)}) collective-permute-start(bf16[64,1152]{1,0:T(8,128)(2,1)S(1)} %broadcast_select_fusion), channel_id=1, source_target_pairs={{0,4},{1,3},{2,6},{3,1},{4,0},{5,7},{6,2},{7,5},{8,12},{9,11},{10,... | collective-permute-start | bytes 442376 | tf_op jit(solution)/shard_map/ppermute | solution.py:27
  16.5 6.7 %collective-permute-start.9 = (bf16[64,1152]{1,0:T(8,128)(2,1)S(1)}, bf16[64,1152]{1,0:T(8,128)(2,1)S(1)}, u32[]{:S(2)}, u32[]{:S(2)}) collective-permute-start(bf16[64,1152]{1,0:T(8,128)(2,1)S(1)} %broadcast_select_fusion), channel_id=1, source_target_pairs={{0,6},{1,7},{2,4},{3,5},{4,2},{5,3},{6,0},{7,1},{8,14},{9,15},{10,... | collective-permute-start | bytes 442376 | tf_op jit(solution)/shard_map/ppermute | solution.py:27
  17.0 2.1 %collective-permute-start.7 = (bf16[256,1152]{1,0:T(8,128)(2,1)S(1)}, bf16[256,1152]{1,0:T(8,128)(2,1)S(1)}, u32[]{:S(2)}, u32[]{:S(2)}) collective-permute-start(bf16[256,1152]{1,0:T(8,128)(2,1)S(1)} %shard_map.58), channel_id=1, source_target_pairs={{0,1},{1,0},{2,3},{3,2},{4,5},{5,4},{6,7},{7,6},{8,9},{9,8},{10,11... | collective-permute-start | bytes 1769480 | tf_op jit(solution)/shard_map/ppermute | solution.py:22
  21.2 3.3 %copy-start = (f32[1024,128]{1,0:T(8,128)S(1)}, f32[1024,128]{1,0:T(8,128)}, u32[]{:S(2)}) copy-start(f32[1024,128]{1,0:T(8,128)} %refs_5_.1) | copy-start | bytes 1572868
  21.3 3.3 %copy-start.1 = (f32[1024,128]{1,0:T(8,128)S(1)}, f32[1024,128]{1,0:T(8,128)}, u32[]{:S(2)}) copy-start(f32[1024,128]{1,0:T(8,128)} %refs_6_.1) | copy-start | bytes 1572868
  21.3 3.3 %collective-permute-start.8 = (bf16[128,1152]{1,0:T(8,128)(2,1)S(1)}, bf16[128,1152]{1,0:T(8,128)(2,1)S(1)}, u32[]{:S(2)}, u32[]{:S(2)}) collective-permute-start(bf16[128,1152]{1,0:T(8,128)(2,1)S(1)} %shard_map.61), channel_id=1, source_target_pairs={{0,1},{1,0},{2,3},{3,2},{4,5},{5,4},{6,7},{7,6},{8,9},{9,8},{10,11... | collective-permute-start | bytes 884744 | tf_op jit(solution)/shard_map/ppermute | solution.py:22
  23.2 1.4 %collective-permute-start.10 = (bf16[64,1152]{1,0:T(8,128)(2,1)S(1)}, bf16[64,1152]{1,0:T(8,128)(2,1)S(1)}, u32[]{:S(2)}, u32[]{:S(2)}) collective-permute-start(bf16[64,1152]{1,0:T(8,128)(2,1)S(1)} %collective-permute-done.9.refs_2_), channel_id=1, source_target_pairs={{0,1},{1,0},{2,3},{3,2},{4,5},{5,4},{6,7},{7,6},{8,9},{9,8},{10,11... | collective-permute-start | bytes 442376 | tf_op jit(solution)/shard_map/ppermute | solution.py:22
  25.8 1.2 %collective-permute-start.11 = (f32[1,128]{1,0:T(1,128)S(1)}, f32[1,128]{1,0:T(1,128)S(1)}, u32[]{:S(2)}, u32[]{:S(2)}) collective-permute-start(f32[1,128]{1,0:T(1,128)S(1)} %get-tuple-element.26), channel_id=1, source_target_pairs={{0,1},{1,0},{2,3},{3,2},{4,5},{5,4},{6,7},{7,6},{8,9},{9,8},{10,11... | collective-permute-start | bytes 1544 | tf_op jit(solution)/shard_map/ppermute | solution.py:22
  27.0 3.5 %collective-permute-start.12 = (f32[1,128]{1,0:T(1,128)S(1)}, f32[1,128]{1,0:T(1,128)S(1)}, u32[]{:S(2)}, u32[]{:S(2)}) collective-permute-start(f32[1,128]{1,0:T(1,128)S(1)} %add.36), channel_id=1, source_target_pairs={{0,4},{1,7},{2,6},{3,5},{4,0},{5,3},{6,2},{7,1},{8,12},{9,15},{10,... | collective-permute-start | bytes 1544 | tf_op jit(solution)/shard_map/ppermute | solution.py:27
  27.9 3.5 %collective-permute-start.13 = (f32[1,128]{1,0:T(1,128)S(1)}, f32[1,128]{1,0:T(1,128)S(1)}, u32[]{:S(2)}, u32[]{:S(2)}) collective-permute-start(f32[1,128]{1,0:T(1,128)S(1)} %add.36), channel_id=1, source_target_pairs={{0,2},{1,5},{2,0},{3,7},{4,6},{5,1},{6,4},{7,3},{8,10},{9,13},{10,... | collective-permute-start | bytes 1544 | tf_op jit(solution)/shard_map/ppermute | solution.py:27
  31.5 1.1 %collective-permute-start.14 = (f32[1,128]{1,0:T(1,128)S(1)}, f32[1,128]{1,0:T(1,128)S(1)}, u32[]{:S(2)}, u32[]{:S(2)}) collective-permute-start(f32[1,128]{1,0:T(1,128)S(1)} %broadcast_select_fusion.1), channel_id=1, source_target_pairs={{0,1},{1,0},{2,3},{3,2},{4,5},{5,4},{6,7},{7,6},{8,9},{9,8},{10,11... | collective-permute-start | bytes 1544 | tf_op jit(solution)/shard_map/ppermute | solution.py:22
  32.6 4.8 %collective-permute-start.15 = (f32[1,128]{1,0:T(1,128)S(1)}, f32[1,128]{1,0:T(1,128)S(1)}, u32[]{:S(2)}, u32[]{:S(2)}) collective-permute-start(f32[1,128]{1,0:T(1,128)S(1)} %add.39), channel_id=1, source_target_pairs={{0,8},{1,9},{2,10},{3,11},{4,12},{5,13},{6,14},{7,15},{8,0},{9,1},... | collective-permute-start | bytes 1544 | tf_op jit(solution)/shard_map/ppermute | solution.py:22

commit v8 on v7

--- a/solution.py
+++ b/solution.py
@@ -98,7 +98,7 @@
     return joined([x], *tokens)
 
 
-def load_kernel(array_ref, token_ref, out_ref, sem):
+def load_kernel(array_ref, token_ref, current_ref, previous_ref, out_ref, rest_ref, sem):
     del token_ref
     parts = sem.shape[0]
     rows = array_ref.shape[0] // parts
@@ -108,20 +108,21 @@
     ]
     for copy in copies:
         copy.start()
+    rest_ref[...] = 2.0 / 0.05 * 0.01 * current_ref[...] + previous_ref[...]
     for copy in copies:
         copy.wait()
 
 
-def load(array, token):
+def load(array, token, current, previous):
     return pl.pallas_call(
         load_kernel,
-        out_shape=jax.ShapeDtypeStruct(array.shape, array.dtype),
-        in_specs=[IN_HBM, pl.BlockSpec(memory_space=pl.ANY)],
-        out_specs=VMEM,
+        out_shape=[jax.ShapeDtypeStruct(array.shape, array.dtype), jax.ShapeDtypeStruct(current.shape, current.dtype)],
+        in_specs=[IN_HBM, pl.BlockSpec(memory_space=pl.ANY), VMEM, VMEM],
+        out_specs=[VMEM] * 2,
         scratch_shapes=[pltpu.SemaphoreType.DMA((8 if array.shape[0] % 128 == 0 else 1,))],
-        compiler_params=pltpu.CompilerParams(vmem_limit_bytes=4 * 2**20),
+        compiler_params=pltpu.CompilerParams(vmem_limit_bytes=8 * 2**20),
         cost_estimate=SMALL,
-    )(hbm(array), token)
+    )(hbm(array), token, current, previous)
 
 
 def scores_of(target, feats):
@@ -166,8 +167,8 @@
         denom_ref[...] = added
         numer_ref[...] = product
         return
-    current_ref, previous_ref, next_ref, column_ref = refs
-    step = 2.0 / 0.05 * (product / added - 0.01 * current_ref[...]) - previous_ref[...]
+    rest_ref, next_ref, column_ref = refs
+    step = 2.0 / 0.05 * (product / added) - rest_ref[...]
     next_ref[...] = step
     column_ref[...] = jnp.sum(step * step, axis=0, keepdims=True)
 
@@ -186,11 +187,12 @@
     )(target, *pieces, *state, *ends)
 
 
-def gather(shard, target, scale):
+def gather(shard, target, current, previous, scale):
     n = lax.axis_size("tgt")
     if n & (n - 1) or n < 16:
         everything = lax.all_gather(shard, "tgt", axis=0, tiled=True)
-        return target, [everything], []
+        target, rest = load(target, shard, current, previous)
+        return target, rest, [everything], []
     near, bit = shard, n // 2
     while bit > 8:
         near = jnp.concatenate([near, swap(near, bit)], axis=0)
@@ -200,7 +202,7 @@
     later = tie(near, near_other)
     two = cross(later, 4, bit, False)
     around = [one, two] + [swap(later, k) for k in (2, 6)]
-    target = load(target, later)
+    target, rest = load(target, later, current, previous)
     place = lax.axis_index("tgt")
     far = jnp.where((place // 4 + place // bit) % 2 == 0, one, two)
     beyond = [swap_by_core(far, a, b) for a, b in ((2, 4), (4, 2), (6, 6))]
@@ -209,15 +211,15 @@
     state = step(target, [early], state, [], scale, 20, True)
     others = [swap(joined(beyond[:2], state[0]), 1), swap(beyond[2], 1)]
     state = step(target, beyond, state, [], scale, 0)
-    return target, others, state
+    return target, rest, others, state
 
 
 def on_device(target_features, source_features, vectors, current, previous):
     rows, width = target_features.shape
     gamma = 0.25 / math.sqrt(width)
     scale = 2.0 * gamma * math.log2(math.e)
-    target, pieces, state = gather(pack(source_features, vectors), target_features, scale)
-    next_iter, column = step(target, pieces, state, [current, previous], scale)
+    target, rest, pieces, state = gather(pack(source_features, vectors), target_features, current, previous, scale)
+    next_iter, column = step(target, pieces, state, [rest], scale)
     column_sq = total(column)
     total_rows = rows * lax.axis_size("tgt")
     return next_iter / jnp.sqrt(column_sq / total_rows + 1e-06)

time: 38.4 us -> 38.4 us (level)
  local copies, waits for them, and re-layouts: 0.01 us -> 2.08 us
  waiting for transfers between devices: 10.8 us -> 8.81 us
    ppermute x2, waiting for transfers between devices: 2.84 us -> 0.75 us  [cross(): return lax.ppermute(x, 'tgt', pairs)]
    unnamed x4, local copies, waits for them, and re-layouts: 0.01 us -> 2.08 us
where the time goes in v8:
time: 38.4 us; the launch traced here: 38.2 us
  starting transfers between devices  18 us (47%)
  waiting for transfers between devices  8.81 us (23%)
  Pallas kernels  8.32 us (22%)
  local copies, waits for them, and re-layouts  2.08 us (5%)
  other arithmetic  0.88 us (2%)
    ppermute x9, starting transfers between devices, swap(): return lax.ppermute(x, 'tgt', [(i, i ^ bits) for i in range(n)])  6.87 us
    ppermute x5, starting transfers between devices, swap_by_core(): lax.ppermute(x, 'tgt', [(i, i ^ (second if i % 2 else first)) for i in ra...  6.15 us
    pallas_call x4, Pallas kernels, step(): pl.pallas_call(functools.partial(step_kernel, scale, len(pieces), not sta...  5.75 us
    ppermute x2, starting transfers between devices, cross(): return lax.ppermute(x, 'tgt', pairs)  5 us
    ppermute x9, waiting for transfers between devices, swap(): return lax.ppermute(x, 'tgt', [(i, i ^ bits) for i in range(n)])  4.25 us
    ppermute x5, waiting for transfers between devices, swap_by_core(): lax.ppermute(x, 'tgt', [(i, i ^ (second if i % 2 else first)) for i in ra...  3.81 us
    unnamed x4, local copies, waits for them, and re-layouts  2.08 us
    pallas_call x1, Pallas kernels, load(): pl.pallas_call(load_kernel, out_shape=[jax.ShapeDtypeStruct(array.shape,...  1.57 us
  transfers between devices with their start and end apart: 16, of which 11 were waited for; matrix products, arithmetic and copies ran while one was open for 0% of the time, Pallas kernels for 16%

profile of v8, /device:TPU:0, one launch (start us, length us, event | category | flops | bytes accessed | tf_op | source)
XLA Modules:
  0.0 38.2 jit_solution(16962605725096915845)
XLA Ops:
  0.0 0.9 %shard_map.55.refs_0_ = bf16[64,1152]{1,0:T(8,128)(2,1)S(1)} custom-call(bf16[64,1024]{1,0:T(8,128)(2,1)} %feats_ref.1, bf16[64,128]{1,0:T(8,128)(2,1)} %vecs_ref.1), custom_call_target="tpu_custom_call" | custom-call | tf_op jit(solution)/shard_map/pallas_call | solution.py:67
  0.9 0.5 %collective-permute-start = (bf16[64,1152]{1,0:T(8,128)(2,1)S(1)}, bf16[64,1152]{1,0:T(8,128)(2,1)S(1)}, u32[]{:S(2)}, u32[]{:S(2)}) collective-permute-start(bf16[64,1152]{1,0:T(8,128)(2,1)S(1)} %shard_map.55.refs_0_), channel_id=1, source_target_pairs={{0,1},{1,0},{2,3},{3,2},{4,5},{5,4},{6,7},{7,6},{8,9},{9,8},{10,11... | collective-permute-start | bytes 442376 | tf_op jit(solution)/shard_map/ppermute | solution.py:22
  1.4 2.6 %collective-permute-start.1 = (bf16[64,1152]{1,0:T(8,128)(2,1)S(1)}, bf16[64,1152]{1,0:T(8,128)(2,1)S(1)}, u32[]{:S(2)}, u32[]{:S(2)}) collective-permute-start(bf16[64,1152]{1,0:T(8,128)(2,1)S(1)} %shard_map.55.refs_0_), channel_id=1, source_target_pairs={{0,4},{1,5},{2,6},{3,7},{4,12},{5,13},{6,14},{7,15},{8,0},{9,1},{1... | collective-permute-start | bytes 442376 | tf_op jit(solution)/shard_map/ppermute | solution.py:36
  4.1 0.0 collective-permute-done.refs_1_
  4.1 2.4 %collective-permute-start.2 = (bf16[64,1152]{1,0:T(8,128)(2,1)S(1)}, bf16[64,1152]{1,0:T(8,128)(2,1)S(1)}, u32[]{:S(2)}, u32[]{:S(2)}) collective-permute-start(bf16[64,1152]{1,0:T(8,128)(2,1)S(1)} %shard_map.56.token_ref), channel_id=1, source_target_pairs={{0,8},{1,9},{2,10},{3,11},{4,0},{5,1},{6,2},{7,3},{8,12},{9,13},{1... | collective-permute-start | bytes 442376 | tf_op jit(solution)/shard_map/ppermute | solution.py:36
  6.5 1.5 %collective-permute-start.5 = (bf16[64,1152]{1,0:T(8,128)(2,1)S(1)}, bf16[64,1152]{1,0:T(8,128)(2,1)S(1)}, u32[]{:S(2)}, u32[]{:S(2)}) collective-permute-start(bf16[64,1152]{1,0:T(8,128)(2,1)S(1)} %shard_map.56.token_ref), channel_id=1, source_target_pairs={{0,2},{1,3},{2,0},{3,1},{4,6},{5,7},{6,4},{7,5},{8,10},{9,11},{10,... | collective-permute-start | bytes 442376 | tf_op jit(solution)/shard_map/ppermute | solution.py:22
  8.0 0.3 collective-permute-start.6
  8.3 0.0 copy-start
  8.3 1.0 %copy-done = f32[1024,128]{1,0:T(8,128)S(1)} copy-done((f32[1024,128]{1,0:T(8,128)S(1)}, f32[1024,128]{1,0:T(8,128)}, u32[]{:S(2)}) %copy-start) | copy-done | bytes 524312
  9.4 0.0 copy-start.1
  9.4 1.0 %copy-done.1 = f32[1024,128]{1,0:T(8,128)S(1)} copy-done((f32[1024,128]{1,0:T(8,128)S(1)}, f32[1024,128]{1,0:T(8,128)}, u32[]{:S(2)}) %copy-start.1) | copy-done | bytes 524312
  10.4 1.6 %shard_map.57 = (bf16[1024,1024]{1,0:T(8,128)(2,1)S(1)}, f32[1024,128]{1,0:T(8,128)S(1)}) custom-call(bf16[1024,1024]{1,0:T(8,128)(2,1)} %array_ref.1, bf16[64,1152]{1,0:T(8,128)(2,1)S(1)} %shard_map.56.token_ref, f32[1024,128]{1,0:T(8,128)S(1)} %copy-done, f32[1024,128]{1,0:T(8,128)S(1)} %copy-done.1), custom_call_target="tpu_custom_call" | custom-call | flops 1 | bytes 1 | tf_op jit(solution)/shard_map/pallas_call | solution.py:117
  12.0 0.0 collective-permute-done.1.refs_0_.refs_2_
  12.0 0.8 %collective-permute-done.2.refs_1_.refs_3_ = bf16[64,1152]{1,0:T(8,128)(2,1)S(1)} collective-permute-done((bf16[64,1152]{1,0:T(8,128)(2,1)S(1)}, bf16[64,1152]{1,0:T(8,128)(2,1)S(1)}, u32[]{:S(2)}, u32[]{:S(2)}) %collective-permute-start.2) | collective-permute-done | bytes 147488 | tf_op jit(solution)/shard_map/ppermute | solution.py:36
  12.8 1.6 %collective-permute-start.3 = (bf16[64,1152]{1,0:T(8,128)(2,1)S(1)}, bf16[64,1152]{1,0:T(8,128)(2,1)S(1)}, u32[]{:S(2)}, u32[]{:S(2)}) collective-permute-start(bf16[64,1152]{1,0:T(8,128)(2,1)S(1)} %broadcast_select_fusion), channel_id=1, source_target_pairs={{0,2},{1,5},{2,0},{3,7},{4,6},{5,1},{6,4},{7,3},{8,10},{9,13},{10,... | collective-permute-start | bytes 442376 | tf_op jit(solution)/shard_map/ppermute | solution.py:27
  14.4 2.1 %collective-permute-start.4 = (bf16[64,1152]{1,0:T(8,128)(2,1)S(1)}, bf16[64,1152]{1,0:T(8,128)(2,1)S(1)}, u32[]{:S(2)}, u32[]{:S(2)}) collective-permute-start(bf16[64,1152]{1,0:T(8,128)(2,1)S(1)} %broadcast_select_fusion), channel_id=1, source_target_pairs={{0,4},{1,3},{2,6},{3,1},{4,0},{5,7},{6,2},{7,5},{8,12},{9,11},{10,... | collective-permute-start | bytes 442376 | tf_op jit(solution)/shard_map/ppermute | solution.py:27
  16.5 0.0 collective-permute-start.9
  16.5 0.0 collective-permute-done.5.refs_2_.refs_4_
  16.5 0.4 %collective-permute-done.6.refs_3_.refs_5_ = bf16[64,1152]{1,0:T(8,128)(2,1)S(1)} collective-permute-done((bf16[64,1152]{1,0:T(8,128)(2,1)S(1)}, bf16[64,1152]{1,0:T(8,128)(2,1)S(1)}, u32[]{:S(2)}, u32[]{:S(2)}) %collective-permute-start.6) | collective-permute-done | bytes 147488 | tf_op jit(solution)/shard_map/ppermute | solution.py:22
  17.0 0.1 collective-permute-start.7
  17.1 1.9 %shard_map.59 = (f32[1024,128]{1,0:T(8,128)S(1)}, f32[1024,128]{1,0:T(8,128)S(1)}, f32[1024,128]{1,0:T(8,128)S(1)}) custom-call(bf16[1024,1024]{1,0:T(8,128)(2,1)S(1)} %get-tuple-element.18.target_ref, bf16[64,1152]{1,0:T(8,128)(2,1)S(1)} %shard_map.55.refs_0_, bf16[64,1152]{1,0:T(8,128)(2,1)S(1)} %collective-permute-done.refs_1_, ...), custom_call_target="tpu_custom_call" | custom-call | flops 20000000000 | bytes 1 | tf_op jit(solution)/shard_map/pallas_call | solution.py:180
  18.9 0.1 collective-permute-done.7.refs_0_
  19.0 1.6 %shard_map.60 = (f32[1024,128]{1,0:T(8,128)S(1)}, f32[1024,128]{1,0:T(8,128)S(1)}, f32[1024,128]{1,0:T(8,128)S(1)}) custom-call(bf16[1024,1024]{1,0:T(8,128)(2,1)S(1)} %get-tuple-element.18.target_ref, bf16[256,1152]{1,0:T(8,128)(2,1)S(1)} %collective-permute-done.7.refs_0_, f32[1024,128]{1,0:T(8,128)S(1)} %get-tuple-element.19.refs_1_, ...), custom_call_target="tpu_custom_call" | custom-call | flops 20000000000 | bytes 1 | tf_op jit(solution)/shard_map/pallas_call | solution.py:180
  20.6 0.6 %collective-permute-done.3.refs_0_ = bf16[64,1152]{1,0:T(8,128)(2,1)S(1)} collective-permute-done((bf16[64,1152]{1,0:T(8,128)(2,1)S(1)}, bf16[64,1152]{1,0:T(8,128)(2,1)S(1)}, u32[]{:S(2)}, u32[]{:S(2)}) %collective-permute-start.3) | collective-permute-done | bytes 147488 | tf_op jit(solution)/shard_map/ppermute | solution.py:27
  21.2 0.0 collective-permute-done.4.refs_1_
  21.2 0.8 %collective-permute-start.8 = (bf16[128,1152]{1,0:T(8,128)(2,1)S(1)}, bf16[128,1152]{1,0:T(8,128)(2,1)S(1)}, u32[]{:S(2)}, u32[]{:S(2)}) collective-permute-start(bf16[128,1152]{1,0:T(8,128)(2,1)S(1)} %shard_map.61), channel_id=1, source_target_pairs={{0,1},{1,0},{2,3},{3,2},{4,5},{5,4},{6,7},{7,6},{8,9},{9,8},{10,11... | collective-permute-start | bytes 884744 | tf_op jit(solution)/shard_map/ppermute | solution.py:22
  22.1 1.1 %collective-permute-done.9.refs_2_ = bf16[64,1152]{1,0:T(8,128)(2,1)S(1)} collective-permute-done((bf16[64,1152]{1,0:T(8,128)(2,1)S(1)}, bf16[64,1152]{1,0:T(8,128)(2,1)S(1)}, u32[]{:S(2)}, u32[]{:S(2)}) %collective-permute-start.9) | collective-permute-done | bytes 147488 | tf_op jit(solution)/shard_map/ppermute | solution.py:27
  23.2 0.0 collective-permute-start.10
  23.2 1.1 %shard_map.62 = (f32[1024,128]{1,0:T(8,128)S(1)}, f32[1024,128]{1,0:T(8,128)S(1)}, f32[1024,128]{1,0:T(8,128)S(1)}) custom-call(bf16[1024,1024]{1,0:T(8,128)(2,1)S(1)} %get-tuple-element.18.target_ref, bf16[64,1152]{1,0:T(8,128)(2,1)S(1)} %collective-permute-done.3.refs_0_, bf16[64,1152]{1,0:T(8,128)(2,1)S(1)} %collective-permute-done.4.refs_1_, ...), custom_call_target="tpu_custom_call" | custom-call | flops 1 | bytes 1 | tf_op jit(solution)/shard_map/pallas_call | solution.py:180
  24.3 0.2 collective-permute-done.10.refs_1_
  24.6 0.0 collective-permute-done.8.refs_0_
  24.6 1.2 %shard_map.63 = (f32[1024,128]{1,0:T(8,128)S(1)}, f32[1,128]{1,0:T(1,128)S(1)}) custom-call(bf16[1024,1024]{1,0:T(8,128)(2,1)S(1)} %get-tuple-element.18.target_ref, bf16[128,1152]{1,0:T(8,128)(2,1)S(1)} %collective-permute-done.8.refs_0_, bf16[64,1152]{1,0:T(8,128)(2,1)S(1)} %collective-permute-done.10.refs_1_, f32[1024,128]{1,0:T(8,128)S(1)} %get-tuple-element.25.refs_2_, ...), custom_call_target="tpu_custom_call" | custom-call | flops 1 | bytes 1 | tf_op jit(solution)/shard_map/pallas_call | solution.py:180
  25.8 0.3 collective-permute-start.11
  26.1 0.8 %collective-permute-done.11 = f32[1,128]{1,0:T(1,128)S(1)} collective-permute-done((f32[1,128]{1,0:T(1,128)S(1)}, f32[1,128]{1,0:T(1,128)S(1)}, u32[]{:S(2)}, u32[]{:S(2)}) %collective-permute-start.11) | collective-permute-done | bytes 544 | tf_op jit(solution)/shard_map/ppermute | solution.py:22
  27.0 0.9 %collective-permute-start.12 = (f32[1,128]{1,0:T(1,128)S(1)}, f32[1,128]{1,0:T(1,128)S(1)}, u32[]{:S(2)}, u32[]{:S(2)}) collective-permute-start(f32[1,128]{1,0:T(1,128)S(1)} %add.36), channel_id=1, source_target_pairs={{0,4},{1,7},{2,6},{3,5},{4,0},{5,3},{6,2},{7,1},{8,12},{9,15},{10,... | collective-permute-start | bytes 1544 | tf_op jit(solution)/shard_map/ppermute | solution.py:27
  27.9 1.5 %collective-permute-start.13 = (f32[1,128]{1,0:T(1,128)S(1)}, f32[1,128]{1,0:T(1,128)S(1)}, u32[]{:S(2)}, u32[]{:S(2)}) collective-permute-start(f32[1,128]{1,0:T(1,128)S(1)} %add.36), channel_id=1, source_target_pairs={{0,2},{1,5},{2,0},{3,7},{4,6},{5,1},{6,4},{7,3},{8,10},{9,13},{10,... | collective-permute-start | bytes 1544 | tf_op jit(solution)/shard_map/ppermute | solution.py:27
  29.4 1.1 %collective-permute-done.12 = f32[1,128]{1,0:T(1,128)S(1)} collective-permute-done((f32[1,128]{1,0:T(1,128)S(1)}, f32[1,128]{1,0:T(1,128)S(1)}, u32[]{:S(2)}, u32[]{:S(2)}) %collective-permute-start.12) | collective-permute-done | bytes 544 | tf_op jit(solution)/shard_map/ppermute | solution.py:27
  30.5 0.9 %collective-permute-done.13 = f32[1,128]{1,0:T(1,128)S(1)} collective-permute-done((f32[1,128]{1,0:T(1,128)S(1)}, f32[1,128]{1,0:T(1,128)S(1)}, u32[]{:S(2)}, u32[]{:S(2)}) %collective-permute-start.13) | collective-permute-done | bytes 544 | tf_op jit(solution)/shard_map/ppermute | solution.py:27
  31.5 0.0 collective-permute-start.14
  31.5 1.1 %collective-permute-done.14 = f32[1,128]{1,0:T(1,128)S(1)} collective-permute-done((f32[1,128]{1,0:T(1,128)S(1)}, f32[1,128]{1,0:T(1,128)S(1)}, u32[]{:S(2)}, u32[]{:S(2)}) %collective-permute-start.14) | collective-permute-done | bytes 544 | tf_op jit(solution)/shard_map/ppermute | solution.py:22
  32.6 3.2 %collective-permute-start.15 = (f32[1,128]{1,0:T(1,128)S(1)}, f32[1,128]{1,0:T(1,128)S(1)}, u32[]{:S(2)}, u32[]{:S(2)}) collective-permute-start(f32[1,128]{1,0:T(1,128)S(1)} %add.39), channel_id=1, source_target_pairs={{0,8},{1,9},{2,10},{3,11},{4,12},{5,13},{6,14},{7,15},{8,0},{9,1},... | collective-permute-start | bytes 1544 | tf_op jit(solution)/shard_map/ppermute | solution.py:22
  35.8 1.5 %collective-permute-done.15 = f32[1,128]{1,0:T(1,128)S(1)} collective-permute-done((f32[1,128]{1,0:T(1,128)S(1)}, f32[1,128]{1,0:T(1,128)S(1)}, u32[]{:S(2)}, u32[]{:S(2)}) %collective-permute-start.15) | collective-permute-done | bytes 544 | tf_op jit(solution)/shard_map/ppermute | solution.py:22
  37.4 0.8 %broadcast_divide_fusion = f32[1024,128]{1,0:T(8,128)} fusion(f32[1024,128]{1,0:T(8,128)S(1)} %get-tuple-element.29, f32[128]{0:T(128)S(1)} %sqrt_bitcast_fusion), kind=kLoop, calls=%fused_computation | loop fusion | flops 131072 | bytes 1049088 | tf_op jit(solution)/shard_map/div | solution.py:225
  (8 shorter events, 0.1 us)
Async XLA Ops:
  0.9 3.2 %collective-permute-start = (bf16[64,1152]{1,0:T(8,128)(2,1)S(1)}, bf16[64,1152]{1,0:T(8,128)(2,1)S(1)}, u32[]{:S(2)}, u32[]{:S(2)}) collective-permute-start(bf16[64,1152]{1,0:T(8,128)(2,1)S(1)} %shard_map.55.refs_0_), channel_id=1, source_target_pairs={{0,1},{1,0},{2,3},{3,2},{4,5},{5,4},{6,7},{7,6},{8,9},{9,8},{10,11... | collective-permute-start | bytes 442376 | tf_op jit(solution)/shard_map/ppermute | solution.py:22
  1.4 10.5 %collective-permute-start.1 = (bf16[64,1152]{1,0:T(8,128)(2,1)S(1)}, bf16[64,1152]{1,0:T(8,128)(2,1)S(1)}, u32[]{:S(2)}, u32[]{:S(2)}) collective-permute-start(bf16[64,1152]{1,0:T(8,128)(2,1)S(1)} %shard_map.55.refs_0_), channel_id=1, source_target_pairs={{0,4},{1,5},{2,6},{3,7},{4,12},{5,13},{6,14},{7,15},{8,0},{9,1},{1... | collective-permute-start | bytes 442376 | tf_op jit(solution)/shard_map/ppermute | solution.py:36
  4.1 8.7 %collective-permute-start.2 = (bf16[64,1152]{1,0:T(8,128)(2,1)S(1)}, bf16[64,1152]{1,0:T(8,128)(2,1)S(1)}, u32[]{:S(2)}, u32[]{:S(2)}) collective-permute-start(bf16[64,1152]{1,0:T(8,128)(2,1)S(1)} %shard_map.56.token_ref), channel_id=1, source_target_pairs={{0,8},{1,9},{2,10},{3,11},{4,0},{5,1},{6,2},{7,3},{8,12},{9,13},{1... | collective-permute-start | bytes 442376 | tf_op jit(solution)/shard_map/ppermute | solution.py:36
  6.5 10.0 %collective-permute-start.5 = (bf16[64,1152]{1,0:T(8,128)(2,1)S(1)}, bf16[64,1152]{1,0:T(8,128)(2,1)S(1)}, u32[]{:S(2)}, u32[]{:S(2)}) collective-permute-start(bf16[64,1152]{1,0:T(8,128)(2,1)S(1)} %shard_map.56.token_ref), channel_id=1, source_target_pairs={{0,2},{1,3},{2,0},{3,1},{4,6},{5,7},{6,4},{7,5},{8,10},{9,11},{10,... | collective-permute-start | bytes 442376 | tf_op jit(solution)/shard_map/ppermute | solution.py:22
  8.0 8.9 %collective-permute-start.6 = (bf16[64,1152]{1,0:T(8,128)(2,1)S(1)}, bf16[64,1152]{1,0:T(8,128)(2,1)S(1)}, u32[]{:S(2)}, u32[]{:S(2)}) collective-permute-start(bf16[64,1152]{1,0:T(8,128)(2,1)S(1)} %shard_map.56.token_ref), channel_id=1, source_target_pairs={{0,6},{1,7},{2,4},{3,5},{4,2},{5,3},{6,0},{7,1},{8,14},{9,15},{10,... | collective-permute-start | bytes 442376 | tf_op jit(solution)/shard_map/ppermute | solution.py:22
  8.3 1.0 %copy-start = (f32[1024,128]{1,0:T(8,128)S(1)}, f32[1024,128]{1,0:T(8,128)}, u32[]{:S(2)}) copy-start(f32[1024,128]{1,0:T(8,128)} %current_ref.1) | copy-start | bytes 1572868
  9.4 1.0 %copy-start.1 = (f32[1024,128]{1,0:T(8,128)S(1)}, f32[1024,128]{1,0:T(8,128)}, u32[]{:S(2)}) copy-start(f32[1024,128]{1,0:T(8,128)} %previous_ref.1) | copy-start | bytes 1572868
  12.8 8.4 %collective-permute-start.3 = (bf16[64,1152]{1,0:T(8,128)(2,1)S(1)}, bf16[64,1152]{1,0:T(8,128)(2,1)S(1)}, u32[]{:S(2)}, u32[]{:S(2)}) collective-permute-start(bf16[64,1152]{1,0:T(8,128)(2,1)S(1)} %broadcast_select_fusion), channel_id=1, source_target_pairs={{0,2},{1,5},{2,0},{3,7},{4,6},{5,1},{6,4},{7,3},{8,10},{9,13},{10,... | collective-permute-start | bytes 442376 | tf_op jit(solution)/shard_map/ppermute | solution.py:27
  14.4 6.8 %collective-permute-start.4 = (bf16[64,1152]{1,0:T(8,128)(2,1)S(1)}, bf16[64,1152]{1,0:T(8,128)(2,1)S(1)}, u32[]{:S(2)}, u32[]{:S(2)}) collective-permute-start(bf16[64,1152]{1,0:T(8,128)(2,1)S(1)} %broadcast_select_fusion), channel_id=1, source_target_pairs={{0,4},{1,3},{2,6},{3,1},{4,0},{5,7},{6,2},{7,5},{8,12},{9,11},{10,... | collective-permute-start | bytes 442376 | tf_op jit(solution)/shard_map/ppermute | solution.py:27
  16.5 6.7 %collective-permute-start.9 = (bf16[64,1152]{1,0:T(8,128)(2,1)S(1)}, bf16[64,1152]{1,0:T(8,128)(2,1)S(1)}, u32[]{:S(2)}, u32[]{:S(2)}) collective-permute-start(bf16[64,1152]{1,0:T(8,128)(2,1)S(1)} %broadcast_select_fusion), channel_id=1, source_target_pairs={{0,6},{1,7},{2,4},{3,5},{4,2},{5,3},{6,0},{7,1},{8,14},{9,15},{10,... | collective-permute-start | bytes 442376 | tf_op jit(solution)/shard_map/ppermute | solution.py:27
  17.0 2.1 %collective-permute-start.7 = (bf16[256,1152]{1,0:T(8,128)(2,1)S(1)}, bf16[256,1152]{1,0:T(8,128)(2,1)S(1)}, u32[]{:S(2)}, u32[]{:S(2)}) collective-permute-start(bf16[256,1152]{1,0:T(8,128)(2,1)S(1)} %shard_map.58), channel_id=1, source_target_pairs={{0,1},{1,0},{2,3},{3,2},{4,5},{5,4},{6,7},{7,6},{8,9},{9,8},{10,11... | collective-permute-start | bytes 1769480 | tf_op jit(solution)/shard_map/ppermute | solution.py:22
  21.2 3.3 %collective-permute-start.8 = (bf16[128,1152]{1,0:T(8,128)(2,1)S(1)}, bf16[128,1152]{1,0:T(8,128)(2,1)S(1)}, u32[]{:S(2)}, u32[]{:S(2)}) collective-permute-start(bf16[128,1152]{1,0:T(8,128)(2,1)S(1)} %shard_map.61), channel_id=1, source_target_pairs={{0,1},{1,0},{2,3},{3,2},{4,5},{5,4},{6,7},{7,6},{8,9},{9,8},{10,11... | collective-permute-start | bytes 884744 | tf_op jit(solution)/shard_map/ppermute | solution.py:22
  23.2 1.4 %collective-permute-start.10 = (bf16[64,1152]{1,0:T(8,128)(2,1)S(1)}, bf16[64,1152]{1,0:T(8,128)(2,1)S(1)}, u32[]{:S(2)}, u32[]{:S(2)}) collective-permute-start(bf16[64,1152]{1,0:T(8,128)(2,1)S(1)} %collective-permute-done.9.refs_2_), channel_id=1, source_target_pairs={{0,1},{1,0},{2,3},{3,2},{4,5},{5,4},{6,7},{7,6},{8,9},{9,8},{10,11... | collective-permute-start | bytes 442376 | tf_op jit(solution)/shard_map/ppermute | solution.py:22
  25.8 1.2 %collective-permute-start.11 = (f32[1,128]{1,0:T(1,128)S(1)}, f32[1,128]{1,0:T(1,128)S(1)}, u32[]{:S(2)}, u32[]{:S(2)}) collective-permute-start(f32[1,128]{1,0:T(1,128)S(1)} %get-tuple-element.30), channel_id=1, source_target_pairs={{0,1},{1,0},{2,3},{3,2},{4,5},{5,4},{6,7},{7,6},{8,9},{9,8},{10,11... | collective-permute-start | bytes 1544 | tf_op jit(solution)/shard_map/ppermute | solution.py:22
  27.0 3.5 %collective-permute-start.12 = (f32[1,128]{1,0:T(1,128)S(1)}, f32[1,128]{1,0:T(1,128)S(1)}, u32[]{:S(2)}, u32[]{:S(2)}) collective-permute-start(f32[1,128]{1,0:T(1,128)S(1)} %add.36), channel_id=1, source_target_pairs={{0,4},{1,7},{2,6},{3,5},{4,0},{5,3},{6,2},{7,1},{8,12},{9,15},{10,... | collective-permute-start | bytes 1544 | tf_op jit(solution)/shard_map/ppermute | solution.py:27
  27.9 3.5 %collective-permute-start.13 = (f32[1,128]{1,0:T(1,128)S(1)}, f32[1,128]{1,0:T(1,128)S(1)}, u32[]{:S(2)}, u32[]{:S(2)}) collective-permute-start(f32[1,128]{1,0:T(1,128)S(1)} %add.36), channel_id=1, source_target_pairs={{0,2},{1,5},{2,0},{3,7},{4,6},{5,1},{6,4},{7,3},{8,10},{9,13},{10,... | collective-permute-start | bytes 1544 | tf_op jit(solution)/shard_map/ppermute | solution.py:27
  31.5 1.1 %collective-permute-start.14 = (f32[1,128]{1,0:T(1,128)S(1)}, f32[1,128]{1,0:T(1,128)S(1)}, u32[]{:S(2)}, u32[]{:S(2)}) collective-permute-start(f32[1,128]{1,0:T(1,128)S(1)} %broadcast_select_fusion.1), channel_id=1, source_target_pairs={{0,1},{1,0},{2,3},{3,2},{4,5},{5,4},{6,7},{7,6},{8,9},{9,8},{10,11... | collective-permute-start | bytes 1544 | tf_op jit(solution)/shard_map/ppermute | solution.py:22
  32.6 4.8 %collective-permute-start.15 = (f32[1,128]{1,0:T(1,128)S(1)}, f32[1,128]{1,0:T(1,128)S(1)}, u32[]{:S(2)}, u32[]{:S(2)}) collective-permute-start(f32[1,128]{1,0:T(1,128)S(1)} %add.39), channel_id=1, source_target_pairs={{0,8},{1,9},{2,10},{3,11},{4,12},{5,13},{6,14},{7,15},{8,0},{9,1},... | collective-permute-start | bytes 1544 | tf_op jit(solution)/shard_map/ppermute | solution.py:22

commit v9 on v6

--- a/solution.py
+++ b/solution.py
@@ -41,8 +41,12 @@
     if n & (n - 1) or n < 16:
         return lax.psum(x, "tgt")
     x = x + swap(x, 1)
-    x = x + sum(swap(x, k) for k in (2, 4, 6))
-    bit = 8
+    x = x + swap(x, 2)
+    g0 = swap_by_core(x, 8, 12)
+    g1 = swap_by_core(x, 4, 8)
+    x = jnp.where(lax.axis_index("tgt") % 2 == 0, x + g0 + g1, g0)
+    x = x + swap(x, 1)
+    bit = 16
     while bit < n:
         x = x + swap(x, bit)
         bit *= 2

time: 39.3 us -> 38.4 us (0.977)
  waiting for transfers between devices: 11.8 us -> 10.7 us
    ppermute x3 -> x5, starting transfers between devices: 3.74 us -> 7.92 us  [swap_by_core(): lax.ppermute(x, 'tgt', [(i, i ^ (second if i % 2 else first)) for i in ra...]
    ppermute x11 -> x9, starting transfers between devices: 9.36 us -> 5.3 us  [swap(): return lax.ppermute(x, 'tgt', [(i, i ^ bits) for i in range(n)])]
    ppermute x11 -> x9, waiting for transfers between devices: 7.19 us -> 4.6 us  [swap(): return lax.ppermute(x, 'tgt', [(i, i ^ bits) for i in range(n)])]
    ppermute x3 -> x5, waiting for transfers between devices: 1.72 us -> 3.24 us  [swap_by_core(): lax.ppermute(x, 'tgt', [(i, i ^ (second if i % 2 else first)) for i in ra...]
where the time goes in v9:
time: 38.4 us; the launch traced here: 38.2 us
  starting transfers between devices  18.2 us (47%)
  waiting for transfers between devices  10.7 us (28%)
  Pallas kernels  8.34 us (22%)
  other arithmetic  0.88 us (2%)
    ppermute x5, starting transfers between devices, swap_by_core(): lax.ppermute(x, 'tgt', [(i, i ^ (second if i % 2 else first)) for i in ra...  7.92 us
    pallas_call x4, Pallas kernels, step(): pl.pallas_call(functools.partial(step_kernel, scale, len(pieces), not sta...  5.77 us
    ppermute x9, starting transfers between devices, swap(): return lax.ppermute(x, 'tgt', [(i, i ^ bits) for i in range(n)])  5.3 us
    ppermute x2, starting transfers between devices, cross(): return lax.ppermute(x, 'tgt', pairs)  5 us
    ppermute x9, waiting for transfers between devices, swap(): return lax.ppermute(x, 'tgt', [(i, i ^ bits) for i in range(n)])  4.6 us
    ppermute x5, waiting for transfers between devices, swap_by_core(): lax.ppermute(x, 'tgt', [(i, i ^ (second if i % 2 else first)) for i in ra...  3.24 us
    ppermute x2, waiting for transfers between devices, cross(): return lax.ppermute(x, 'tgt', pairs)  2.84 us
    pallas_call x1, Pallas kernels, load(): pl.pallas_call(load_kernel, out_shape=jax.ShapeDtypeStruct(array.shape, a...  1.57 us
  transfers between devices with their start and end apart: 16, of which 11 were waited for; matrix products, arithmetic and copies ran while one was open for 0% of the time, Pallas kernels for 16%

profile of v9, /device:TPU:0, one launch (start us, length us, event | category | flops | bytes accessed | tf_op | source)
XLA Modules:
  0.0 38.2 jit_solution(12916555097838599336)
XLA Ops:
  0.0 0.9 %shard_map.55.refs_0_ = bf16[64,1152]{1,0:T(8,128)(2,1)S(1)} custom-call(bf16[64,1024]{1,0:T(8,128)(2,1)} %feats_ref.1, bf16[64,128]{1,0:T(8,128)(2,1)} %vecs_ref.1), custom_call_target="tpu_custom_call" | custom-call | tf_op jit(solution)/shard_map/pallas_call | solution.py:68
  0.9 0.5 %collective-permute-start = (bf16[64,1152]{1,0:T(8,128)(2,1)S(1)}, bf16[64,1152]{1,0:T(8,128)(2,1)S(1)}, u32[]{:S(2)}, u32[]{:S(2)}) collective-permute-start(bf16[64,1152]{1,0:T(8,128)(2,1)S(1)} %shard_map.55.refs_0_), channel_id=1, source_target_pairs={{0,1},{1,0},{2,3},{3,2},{4,5},{5,4},{6,7},{7,6},{8,9},{9,8},{10,11... | collective-permute-start | bytes 442376 | tf_op jit(solution)/shard_map/ppermute | solution.py:22
  1.4 2.6 %collective-permute-start.1 = (bf16[64,1152]{1,0:T(8,128)(2,1)S(1)}, bf16[64,1152]{1,0:T(8,128)(2,1)S(1)}, u32[]{:S(2)}, u32[]{:S(2)}) collective-permute-start(bf16[64,1152]{1,0:T(8,128)(2,1)S(1)} %shard_map.55.refs_0_), channel_id=1, source_target_pairs={{0,4},{1,5},{2,6},{3,7},{4,12},{5,13},{6,14},{7,15},{8,0},{9,1},{1... | collective-permute-start | bytes 442376 | tf_op jit(solution)/shard_map/ppermute | solution.py:36
  4.1 0.0 collective-permute-done.refs_1_
  4.1 2.4 %collective-permute-start.2 = (bf16[64,1152]{1,0:T(8,128)(2,1)S(1)}, bf16[64,1152]{1,0:T(8,128)(2,1)S(1)}, u32[]{:S(2)}, u32[]{:S(2)}) collective-permute-start(bf16[64,1152]{1,0:T(8,128)(2,1)S(1)} %shard_map.56.token_ref), channel_id=1, source_target_pairs={{0,8},{1,9},{2,10},{3,11},{4,0},{5,1},{6,2},{7,3},{8,12},{9,13},{1... | collective-permute-start | bytes 442376 | tf_op jit(solution)/shard_map/ppermute | solution.py:36
  6.5 1.5 %collective-permute-start.5 = (bf16[64,1152]{1,0:T(8,128)(2,1)S(1)}, bf16[64,1152]{1,0:T(8,128)(2,1)S(1)}, u32[]{:S(2)}, u32[]{:S(2)}) collective-permute-start(bf16[64,1152]{1,0:T(8,128)(2,1)S(1)} %shard_map.56.token_ref), channel_id=1, source_target_pairs={{0,2},{1,3},{2,0},{3,1},{4,6},{5,7},{6,4},{7,5},{8,10},{9,11},{10,... | collective-permute-start | bytes 442376 | tf_op jit(solution)/shard_map/ppermute | solution.py:22
  8.0 0.3 collective-permute-start.6
  8.3 1.6 %shard_map.57.target_ref = bf16[1024,1024]{1,0:T(8,128)(2,1)S(1)} custom-call(bf16[1024,1024]{1,0:T(8,128)(2,1)} %array_ref.1, bf16[64,1152]{1,0:T(8,128)(2,1)S(1)} %shard_map.56.token_ref), custom_call_target="tpu_custom_call" | custom-call | flops 1 | bytes 1 | tf_op jit(solution)/shard_map/pallas_call | solution.py:117
  9.9 0.0 collective-permute-done.1.refs_0_.refs_2_
  9.9 2.8 %collective-permute-done.2.refs_1_.refs_3_ = bf16[64,1152]{1,0:T(8,128)(2,1)S(1)} collective-permute-done((bf16[64,1152]{1,0:T(8,128)(2,1)S(1)}, bf16[64,1152]{1,0:T(8,128)(2,1)S(1)}, u32[]{:S(2)}, u32[]{:S(2)}) %collective-permute-start.2) | collective-permute-done | bytes 147488 | tf_op jit(solution)/shard_map/ppermute | solution.py:36
  12.8 1.6 %collective-permute-start.3 = (bf16[64,1152]{1,0:T(8,128)(2,1)S(1)}, bf16[64,1152]{1,0:T(8,128)(2,1)S(1)}, u32[]{:S(2)}, u32[]{:S(2)}) collective-permute-start(bf16[64,1152]{1,0:T(8,128)(2,1)S(1)} %broadcast_select_fusion), channel_id=1, source_target_pairs={{0,2},{1,5},{2,0},{3,7},{4,6},{5,1},{6,4},{7,3},{8,10},{9,13},{10,... | collective-permute-start | bytes 442376 | tf_op jit(solution)/shard_map/ppermute | solution.py:27
  14.4 2.1 %collective-permute-start.4 = (bf16[64,1152]{1,0:T(8,128)(2,1)S(1)}, bf16[64,1152]{1,0:T(8,128)(2,1)S(1)}, u32[]{:S(2)}, u32[]{:S(2)}) collective-permute-start(bf16[64,1152]{1,0:T(8,128)(2,1)S(1)} %broadcast_select_fusion), channel_id=1, source_target_pairs={{0,4},{1,3},{2,6},{3,1},{4,0},{5,7},{6,2},{7,5},{8,12},{9,11},{10,... | collective-permute-start | bytes 442376 | tf_op jit(solution)/shard_map/ppermute | solution.py:27
  16.5 0.0 collective-permute-start.9
  16.5 0.0 collective-permute-done.5.refs_2_.refs_4_
  16.5 0.4 %collective-permute-done.6.refs_3_.refs_5_ = bf16[64,1152]{1,0:T(8,128)(2,1)S(1)} collective-permute-done((bf16[64,1152]{1,0:T(8,128)(2,1)S(1)}, bf16[64,1152]{1,0:T(8,128)(2,1)S(1)}, u32[]{:S(2)}, u32[]{:S(2)}) %collective-permute-start.6) | collective-permute-done | bytes 147488 | tf_op jit(solution)/shard_map/ppermute | solution.py:22
  17.0 0.1 collective-permute-start.7
  17.1 1.9 %shard_map.59 = (f32[1024,128]{1,0:T(8,128)S(1)}, f32[1024,128]{1,0:T(8,128)S(1)}, f32[1024,128]{1,0:T(8,128)S(1)}) custom-call(bf16[1024,1024]{1,0:T(8,128)(2,1)S(1)} %shard_map.57.target_ref, bf16[64,1152]{1,0:T(8,128)(2,1)S(1)} %shard_map.55.refs_0_, bf16[64,1152]{1,0:T(8,128)(2,1)S(1)} %collective-permute-done.refs_1_, ...), custom_call_target="tpu_custom_call" | custom-call | flops 20000000000 | bytes 1 | tf_op jit(solution)/shard_map/pallas_call | solution.py:180
  18.9 0.1 collective-permute-done.7.refs_0_
  19.0 1.6 %shard_map.60 = (f32[1024,128]{1,0:T(8,128)S(1)}, f32[1024,128]{1,0:T(8,128)S(1)}, f32[1024,128]{1,0:T(8,128)S(1)}) custom-call(bf16[1024,1024]{1,0:T(8,128)(2,1)S(1)} %shard_map.57.target_ref, bf16[256,1152]{1,0:T(8,128)(2,1)S(1)} %collective-permute-done.7.refs_0_, f32[1024,128]{1,0:T(8,128)S(1)} %get-tuple-element.16.refs_1_, ...), custom_call_target="tpu_custom_call" | custom-call | flops 20000000000 | bytes 1 | tf_op jit(solution)/shard_map/pallas_call | solution.py:180
  20.6 0.6 %collective-permute-done.3.refs_0_ = bf16[64,1152]{1,0:T(8,128)(2,1)S(1)} collective-permute-done((bf16[64,1152]{1,0:T(8,128)(2,1)S(1)}, bf16[64,1152]{1,0:T(8,128)(2,1)S(1)}, u32[]{:S(2)}, u32[]{:S(2)}) %collective-permute-start.3) | collective-permute-done | bytes 147488 | tf_op jit(solution)/shard_map/ppermute | solution.py:27
  21.2 0.0 collective-permute-done.4.refs_1_
  21.2 0.0 copy-start
  21.3 0.0 copy-start.1
  21.3 0.8 %collective-permute-start.8 = (bf16[128,1152]{1,0:T(8,128)(2,1)S(1)}, bf16[128,1152]{1,0:T(8,128)(2,1)S(1)}, u32[]{:S(2)}, u32[]{:S(2)}) collective-permute-start(bf16[128,1152]{1,0:T(8,128)(2,1)S(1)} %shard_map.61), channel_id=1, source_target_pairs={{0,1},{1,0},{2,3},{3,2},{4,5},{5,4},{6,7},{7,6},{8,9},{9,8},{10,11... | collective-permute-start | bytes 884744 | tf_op jit(solution)/shard_map/ppermute | solution.py:22
  22.1 1.1 %collective-permute-done.9.refs_2_ = bf16[64,1152]{1,0:T(8,128)(2,1)S(1)} collective-permute-done((bf16[64,1152]{1,0:T(8,128)(2,1)S(1)}, bf16[64,1152]{1,0:T(8,128)(2,1)S(1)}, u32[]{:S(2)}, u32[]{:S(2)}) %collective-permute-start.9) | collective-permute-done | bytes 147488 | tf_op jit(solution)/shard_map/ppermute | solution.py:27
  23.2 0.0 collective-permute-start.10
  23.2 1.1 %shard_map.62 = (f32[1024,128]{1,0:T(8,128)S(1)}, f32[1024,128]{1,0:T(8,128)S(1)}, f32[1024,128]{1,0:T(8,128)S(1)}) custom-call(bf16[1024,1024]{1,0:T(8,128)(2,1)S(1)} %shard_map.57.target_ref, bf16[64,1152]{1,0:T(8,128)(2,1)S(1)} %collective-permute-done.3.refs_0_, bf16[64,1152]{1,0:T(8,128)(2,1)S(1)} %collective-permute-done.4.refs_1_, ...), custom_call_target="tpu_custom_call" | custom-call | flops 1 | bytes 1 | tf_op jit(solution)/shard_map/pallas_call | solution.py:180
  24.3 0.2 collective-permute-done.10.refs_1_
  24.6 0.0 collective-permute-done.8.refs_0_
  24.6 0.0 copy-done
  24.6 0.0 copy-done.1
  24.6 1.2 %shard_map.63 = (f32[1024,128]{1,0:T(8,128)S(1)}, f32[1,128]{1,0:T(1,128)S(1)}) custom-call(bf16[1024,1024]{1,0:T(8,128)(2,1)S(1)} %shard_map.57.target_ref, bf16[128,1152]{1,0:T(8,128)(2,1)S(1)} %collective-permute-done.8.refs_0_, bf16[64,1152]{1,0:T(8,128)(2,1)S(1)} %collective-permute-done.10.refs_1_, f32[1024,128]{1,0:T(8,128)S(1)} %get-tuple-element.22.refs_2_, ...), custom_call_target="tpu_custom_call" | custom-call | flops 1 | bytes 1 | tf_op jit(solution)/shard_map/pallas_call | solution.py:180
  25.8 0.4 collective-permute-start.11
  26.2 0.8 %collective-permute-done.11 = f32[1,128]{1,0:T(1,128)S(1)} collective-permute-done((f32[1,128]{1,0:T(1,128)S(1)}, f32[1,128]{1,0:T(1,128)S(1)}, u32[]{:S(2)}, u32[]{:S(2)}) %collective-permute-start.11) | collective-permute-done | bytes 544 | tf_op jit(solution)/shard_map/ppermute | solution.py:22
  27.0 1.6 %collective-permute-start.12 = (f32[1,128]{1,0:T(1,128)S(1)}, f32[1,128]{1,0:T(1,128)S(1)}, u32[]{:S(2)}, u32[]{:S(2)}) collective-permute-start(f32[1,128]{1,0:T(1,128)S(1)} %add.36), channel_id=1, source_target_pairs={{0,2},{1,3},{2,0},{3,1},{4,6},{5,7},{6,4},{7,5},{8,10},{9,11},{10,... | collective-permute-start | bytes 1544 | tf_op jit(solution)/shard_map/ppermute | solution.py:22
  28.6 2.0 %collective-permute-done.12 = f32[1,128]{1,0:T(1,128)S(1)} collective-permute-done((f32[1,128]{1,0:T(1,128)S(1)}, f32[1,128]{1,0:T(1,128)S(1)}, u32[]{:S(2)}, u32[]{:S(2)}) %collective-permute-start.12) | collective-permute-done | bytes 544 | tf_op jit(solution)/shard_map/ppermute | solution.py:22
  30.6 1.7 %collective-permute-start.13 = (f32[1,128]{1,0:T(1,128)S(1)}, f32[1,128]{1,0:T(1,128)S(1)}, u32[]{:S(2)}, u32[]{:S(2)}) collective-permute-start(f32[1,128]{1,0:T(1,128)S(1)} %add.37), channel_id=1, source_target_pairs={{0,8},{1,13},{2,10},{3,15},{4,12},{5,9},{6,14},{7,11},{8,0},{9,5},... | collective-permute-start | bytes 1544 | tf_op jit(solution)/shard_map/ppermute | solution.py:27
  32.2 2.5 %collective-permute-start.14 = (f32[1,128]{1,0:T(1,128)S(1)}, f32[1,128]{1,0:T(1,128)S(1)}, u32[]{:S(2)}, u32[]{:S(2)}) collective-permute-start(f32[1,128]{1,0:T(1,128)S(1)} %add.37), channel_id=1, source_target_pairs={{0,4},{1,9},{2,6},{3,11},{4,0},{5,13},{6,2},{7,15},{8,12},{9,1},{1... | collective-permute-start | bytes 1544 | tf_op jit(solution)/shard_map/ppermute | solution.py:27
  34.7 0.3 collective-permute-done.13
  35.0 1.3 %collective-permute-done.14 = f32[1,128]{1,0:T(1,128)S(1)} collective-permute-done((f32[1,128]{1,0:T(1,128)S(1)}, f32[1,128]{1,0:T(1,128)S(1)}, u32[]{:S(2)}, u32[]{:S(2)}) %collective-permute-start.14) | collective-permute-done | bytes 544 | tf_op jit(solution)/shard_map/ppermute | solution.py:27
  36.3 0.1 collective-permute-start.15
  36.3 1.0 %collective-permute-done.15 = f32[1,128]{1,0:T(1,128)S(1)} collective-permute-done((f32[1,128]{1,0:T(1,128)S(1)}, f32[1,128]{1,0:T(1,128)S(1)}, u32[]{:S(2)}, u32[]{:S(2)}) %collective-permute-start.15) | collective-permute-done | bytes 544 | tf_op jit(solution)/shard_map/ppermute | solution.py:22
  37.4 0.8 %broadcast_divide_fusion = f32[1024,128]{1,0:T(8,128)} fusion(f32[1024,128]{1,0:T(8,128)S(1)} %get-tuple-element.25, f32[128]{0:T(128)S(1)} %sqrt_bitcast_fusion), kind=kLoop, calls=%fused_computation | loop fusion | flops 131072 | bytes 1049088 | tf_op jit(solution)/shard_map/div | solution.py:224
  (8 shorter events, 0.1 us)
Async XLA Ops:
  0.9 3.2 %collective-permute-start = (bf16[64,1152]{1,0:T(8,128)(2,1)S(1)}, bf16[64,1152]{1,0:T(8,128)(2,1)S(1)}, u32[]{:S(2)}, u32[]{:S(2)}) collective-permute-start(bf16[64,1152]{1,0:T(8,128)(2,1)S(1)} %shard_map.55.refs_0_), channel_id=1, source_target_pairs={{0,1},{1,0},{2,3},{3,2},{4,5},{5,4},{6,7},{7,6},{8,9},{9,8},{10,11... | collective-permute-start | bytes 442376 | tf_op jit(solution)/shard_map/ppermute | solution.py:22
  1.4 8.5 %collective-permute-start.1 = (bf16[64,1152]{1,0:T(8,128)(2,1)S(1)}, bf16[64,1152]{1,0:T(8,128)(2,1)S(1)}, u32[]{:S(2)}, u32[]{:S(2)}) collective-permute-start(bf16[64,1152]{1,0:T(8,128)(2,1)S(1)} %shard_map.55.refs_0_), channel_id=1, source_target_pairs={{0,4},{1,5},{2,6},{3,7},{4,12},{5,13},{6,14},{7,15},{8,0},{9,1},{1... | collective-permute-start | bytes 442376 | tf_op jit(solution)/shard_map/ppermute | solution.py:36
  4.1 8.7 %collective-permute-start.2 = (bf16[64,1152]{1,0:T(8,128)(2,1)S(1)}, bf16[64,1152]{1,0:T(8,128)(2,1)S(1)}, u32[]{:S(2)}, u32[]{:S(2)}) collective-permute-start(bf16[64,1152]{1,0:T(8,128)(2,1)S(1)} %shard_map.56.token_ref), channel_id=1, source_target_pairs={{0,8},{1,9},{2,10},{3,11},{4,0},{5,1},{6,2},{7,3},{8,12},{9,13},{1... | collective-permute-start | bytes 442376 | tf_op jit(solution)/shard_map/ppermute | solution.py:36
  6.5 10.0 %collective-permute-start.5 = (bf16[64,1152]{1,0:T(8,128)(2,1)S(1)}, bf16[64,1152]{1,0:T(8,128)(2,1)S(1)}, u32[]{:S(2)}, u32[]{:S(2)}) collective-permute-start(bf16[64,1152]{1,0:T(8,128)(2,1)S(1)} %shard_map.56.token_ref), channel_id=1, source_target_pairs={{0,2},{1,3},{2,0},{3,1},{4,6},{5,7},{6,4},{7,5},{8,10},{9,11},{10,... | collective-permute-start | bytes 442376 | tf_op jit(solution)/shard_map/ppermute | solution.py:22
  8.0 8.9 %collective-permute-start.6 = (bf16[64,1152]{1,0:T(8,128)(2,1)S(1)}, bf16[64,1152]{1,0:T(8,128)(2,1)S(1)}, u32[]{:S(2)}, u32[]{:S(2)}) collective-permute-start(bf16[64,1152]{1,0:T(8,128)(2,1)S(1)} %shard_map.56.token_ref), channel_id=1, source_target_pairs={{0,6},{1,7},{2,4},{3,5},{4,2},{5,3},{6,0},{7,1},{8,14},{9,15},{10,... | collective-permute-start | bytes 442376 | tf_op jit(solution)/shard_map/ppermute | solution.py:22
  12.8 8.4 %collective-permute-start.3 = (bf16[64,1152]{1,0:T(8,128)(2,1)S(1)}, bf16[64,1152]{1,0:T(8,128)(2,1)S(1)}, u32[]{:S(2)}, u32[]{:S(2)}) collective-permute-start(bf16[64,1152]{1,0:T(8,128)(2,1)S(1)} %broadcast_select_fusion), channel_id=1, source_target_pairs={{0,2},{1,5},{2,0},{3,7},{4,6},{5,1},{6,4},{7,3},{8,10},{9,13},{10,... | collective-permute-start | bytes 442376 | tf_op jit(solution)/shard_map/ppermute | solution.py:27
  14.4 6.8 %collective-permute-start.4 = (bf16[64,1152]{1,0:T(8,128)(2,1)S(1)}, bf16[64,1152]{1,0:T(8,128)(2,1)S(1)}, u32[]{:S(2)}, u32[]{:S(2)}) collective-permute-start(bf16[64,1152]{1,0:T(8,128)(2,1)S(1)} %broadcast_select_fusion), channel_id=1, source_target_pairs={{0,4},{1,3},{2,6},{3,1},{4,0},{5,7},{6,2},{7,5},{8,12},{9,11},{10,... | collective-permute-start | bytes 442376 | tf_op jit(solution)/shard_map/ppermute | solution.py:27
  16.5 6.7 %collective-permute-start.9 = (bf16[64,1152]{1,0:T(8,128)(2,1)S(1)}, bf16[64,1152]{1,0:T(8,128)(2,1)S(1)}, u32[]{:S(2)}, u32[]{:S(2)}) collective-permute-start(bf16[64,1152]{1,0:T(8,128)(2,1)S(1)} %broadcast_select_fusion), channel_id=1, source_target_pairs={{0,6},{1,7},{2,4},{3,5},{4,2},{5,3},{6,0},{7,1},{8,14},{9,15},{10,... | collective-permute-start | bytes 442376 | tf_op jit(solution)/shard_map/ppermute | solution.py:27
  17.0 2.1 %collective-permute-start.7 = (bf16[256,1152]{1,0:T(8,128)(2,1)S(1)}, bf16[256,1152]{1,0:T(8,128)(2,1)S(1)}, u32[]{:S(2)}, u32[]{:S(2)}) collective-permute-start(bf16[256,1152]{1,0:T(8,128)(2,1)S(1)} %shard_map.58), channel_id=1, source_target_pairs={{0,1},{1,0},{2,3},{3,2},{4,5},{5,4},{6,7},{7,6},{8,9},{9,8},{10,11... | collective-permute-start | bytes 1769480 | tf_op jit(solution)/shard_map/ppermute | solution.py:22
  21.2 3.3 %copy-start = (f32[1024,128]{1,0:T(8,128)S(1)}, f32[1024,128]{1,0:T(8,128)}, u32[]{:S(2)}) copy-start(f32[1024,128]{1,0:T(8,128)} %refs_5_.1) | copy-start | bytes 1572868
  21.3 3.3 %copy-start.1 = (f32[1024,128]{1,0:T(8,128)S(1)}, f32[1024,128]{1,0:T(8,128)}, u32[]{:S(2)}) copy-start(f32[1024,128]{1,0:T(8,128)} %refs_6_.1) | copy-start | bytes 1572868
  21.3 3.3 %collective-permute-start.8 = (bf16[128,1152]{1,0:T(8,128)(2,1)S(1)}, bf16[128,1152]{1,0:T(8,128)(2,1)S(1)}, u32[]{:S(2)}, u32[]{:S(2)}) collective-permute-start(bf16[128,1152]{1,0:T(8,128)(2,1)S(1)} %shard_map.61), channel_id=1, source_target_pairs={{0,1},{1,0},{2,3},{3,2},{4,5},{5,4},{6,7},{7,6},{8,9},{9,8},{10,11... | collective-permute-start | bytes 884744 | tf_op jit(solution)/shard_map/ppermute | solution.py:22
  23.2 1.4 %collective-permute-start.10 = (bf16[64,1152]{1,0:T(8,128)(2,1)S(1)}, bf16[64,1152]{1,0:T(8,128)(2,1)S(1)}, u32[]{:S(2)}, u32[]{:S(2)}) collective-permute-start(bf16[64,1152]{1,0:T(8,128)(2,1)S(1)} %collective-permute-done.9.refs_2_), channel_id=1, source_target_pairs={{0,1},{1,0},{2,3},{3,2},{4,5},{5,4},{6,7},{7,6},{8,9},{9,8},{10,11... | collective-permute-start | bytes 442376 | tf_op jit(solution)/shard_map/ppermute | solution.py:22
  25.8 1.2 %collective-permute-start.11 = (f32[1,128]{1,0:T(1,128)S(1)}, f32[1,128]{1,0:T(1,128)S(1)}, u32[]{:S(2)}, u32[]{:S(2)}) collective-permute-start(f32[1,128]{1,0:T(1,128)S(1)} %get-tuple-element.26), channel_id=1, source_target_pairs={{0,1},{1,0},{2,3},{3,2},{4,5},{5,4},{6,7},{7,6},{8,9},{9,8},{10,11... | collective-permute-start | bytes 1544 | tf_op jit(solution)/shard_map/ppermute | solution.py:22
  27.0 3.5 %collective-permute-start.12 = (f32[1,128]{1,0:T(1,128)S(1)}, f32[1,128]{1,0:T(1,128)S(1)}, u32[]{:S(2)}, u32[]{:S(2)}) collective-permute-start(f32[1,128]{1,0:T(1,128)S(1)} %add.36), channel_id=1, source_target_pairs={{0,2},{1,3},{2,0},{3,1},{4,6},{5,7},{6,4},{7,5},{8,10},{9,11},{10,... | collective-permute-start | bytes 1544 | tf_op jit(solution)/shard_map/ppermute | solution.py:22
  30.6 4.4 %collective-permute-start.13 = (f32[1,128]{1,0:T(1,128)S(1)}, f32[1,128]{1,0:T(1,128)S(1)}, u32[]{:S(2)}, u32[]{:S(2)}) collective-permute-start(f32[1,128]{1,0:T(1,128)S(1)} %add.37), channel_id=1, source_target_pairs={{0,8},{1,13},{2,10},{3,15},{4,12},{5,9},{6,14},{7,11},{8,0},{9,5},... | collective-permute-start | bytes 1544 | tf_op jit(solution)/shard_map/ppermute | solution.py:27
  32.2 4.0 %collective-permute-start.14 = (f32[1,128]{1,0:T(1,128)S(1)}, f32[1,128]{1,0:T(1,128)S(1)}, u32[]{:S(2)}, u32[]{:S(2)}) collective-permute-start(f32[1,128]{1,0:T(1,128)S(1)} %add.37), channel_id=1, source_target_pairs={{0,4},{1,9},{2,6},{3,11},{4,0},{5,13},{6,2},{7,15},{8,12},{9,1},{1... | collective-permute-start | bytes 1544 | tf_op jit(solution)/shard_map/ppermute | solution.py:27
  36.3 1.1 %collective-permute-start.15 = (f32[1,128]{1,0:T(1,128)S(1)}, f32[1,128]{1,0:T(1,128)S(1)}, u32[]{:S(2)}, u32[]{:S(2)}) collective-permute-start(f32[1,128]{1,0:T(1,128)S(1)} %broadcast_select_fusion.1), channel_id=1, source_target_pairs={{0,1},{1,0},{2,3},{3,2},{4,5},{5,4},{6,7},{7,6},{8,9},{9,8},{10,11... | collective-permute-start | bytes 1544 | tf_op jit(solution)/shard_map/ppermute | solution.py:22

commit v10 on v7

--- a/solution.py
+++ b/solution.py
@@ -203,7 +203,7 @@
     target = load(target, later)
     place = lax.axis_index("tgt")
     far = jnp.where((place // 4 + place // bit) % 2 == 0, one, two)
-    beyond = [swap_by_core(far, a, b) for a, b in ((2, 4), (4, 2), (6, 6))]
+    beyond = [swap_by_core(far, a, b) for a, b in ((6, 4), (4, 2), (2, 6))]
     state = step(target, [near, near_other] + around, [], [], scale, 20, True)
     early = swap(joined(around), 1)
     state = step(target, [early], state, [], scale, 20, True)

time: 38.4 us -> 38.4 us (level)
  starting transfers between devices: 18.1 us -> 17 us
  waiting for transfers between devices: 10.8 us -> 11.9 us
    ppermute x5, waiting for transfers between devices: 3.76 us -> 4.91 us  [swap_by_core(): lax.ppermute(x, 'tgt', [(i, i ^ (second if i % 2 else first)) for i in ra...]
    ppermute x9, starting transfers between devices: 6.89 us -> 6.14 us  [swap(): return lax.ppermute(x, 'tgt', [(i, i ^ bits) for i in range(n)])]
  transfers between devices with their start and end apart: 16 -> 16, of which waited for: 11 -> 12; matrix products, arithmetic and copies ran while one was open for 0% -> 0% of each run, Pallas kernels for 16% -> 16%
where the time goes in v10:
time: 38.4 us; the launch traced here: 38.2 us
  starting transfers between devices  17 us (44%)
  waiting for transfers between devices  11.9 us (31%)
  Pallas kernels  8.34 us (22%)
  other arithmetic  0.88 us (2%)
    ppermute x9, starting transfers between devices, swap(): return lax.ppermute(x, 'tgt', [(i, i ^ bits) for i in range(n)])  6.14 us
    ppermute x5, starting transfers between devices, swap_by_core(): lax.ppermute(x, 'tgt', [(i, i ^ (second if i % 2 else first)) for i in ra...  5.85 us
    pallas_call x4, Pallas kernels, step(): pl.pallas_call(functools.partial(step_kernel, scale, len(pieces), not sta...  5.77 us
    ppermute x2, starting transfers between devices, cross(): return lax.ppermute(x, 'tgt', pairs)  5 us
    ppermute x5, waiting for transfers between devices, swap_by_core(): lax.ppermute(x, 'tgt', [(i, i ^ (second if i % 2 else first)) for i in ra...  4.91 us
    ppermute x9, waiting for transfers between devices, swap(): return lax.ppermute(x, 'tgt', [(i, i ^ bits) for i in range(n)])  4.14 us
    ppermute x2, waiting for transfers between devices, cross(): return lax.ppermute(x, 'tgt', pairs)  2.84 us
    pallas_call x1, Pallas kernels, load(): pl.pallas_call(load_kernel, out_shape=jax.ShapeDtypeStruct(array.shape, a...  1.57 us
  transfers between devices with their start and end apart: 16, of which 12 were waited for; matrix products, arithmetic and copies ran while one was open for 0% of the time, Pallas kernels for 16%

profile of v10, /device:TPU:0, one launch (start us, length us, event | category | flops | bytes accessed | tf_op | source)
XLA Modules:
  0.0 38.2 jit_solution(6188736628242411626)
XLA Ops:
  0.0 0.9 %shard_map.55.refs_0_ = bf16[64,1152]{1,0:T(8,128)(2,1)S(1)} custom-call(bf16[64,1024]{1,0:T(8,128)(2,1)} %feats_ref.1, bf16[64,128]{1,0:T(8,128)(2,1)} %vecs_ref.1), custom_call_target="tpu_custom_call" | custom-call | tf_op jit(solution)/shard_map/pallas_call | solution.py:67
  0.9 0.5 %collective-permute-start = (bf16[64,1152]{1,0:T(8,128)(2,1)S(1)}, bf16[64,1152]{1,0:T(8,128)(2,1)S(1)}, u32[]{:S(2)}, u32[]{:S(2)}) collective-permute-start(bf16[64,1152]{1,0:T(8,128)(2,1)S(1)} %shard_map.55.refs_0_), channel_id=1, source_target_pairs={{0,1},{1,0},{2,3},{3,2},{4,5},{5,4},{6,7},{7,6},{8,9},{9,8},{10,11... | collective-permute-start | bytes 442376 | tf_op jit(solution)/shard_map/ppermute | solution.py:22
  1.4 2.6 %collective-permute-start.1 = (bf16[64,1152]{1,0:T(8,128)(2,1)S(1)}, bf16[64,1152]{1,0:T(8,128)(2,1)S(1)}, u32[]{:S(2)}, u32[]{:S(2)}) collective-permute-start(bf16[64,1152]{1,0:T(8,128)(2,1)S(1)} %shard_map.55.refs_0_), channel_id=1, source_target_pairs={{0,4},{1,5},{2,6},{3,7},{4,12},{5,13},{6,14},{7,15},{8,0},{9,1},{1... | collective-permute-start | bytes 442376 | tf_op jit(solution)/shard_map/ppermute | solution.py:36
  4.1 0.0 collective-permute-done.refs_1_
  4.1 2.4 %collective-permute-start.2 = (bf16[64,1152]{1,0:T(8,128)(2,1)S(1)}, bf16[64,1152]{1,0:T(8,128)(2,1)S(1)}, u32[]{:S(2)}, u32[]{:S(2)}) collective-permute-start(bf16[64,1152]{1,0:T(8,128)(2,1)S(1)} %shard_map.56.token_ref), channel_id=1, source_target_pairs={{0,8},{1,9},{2,10},{3,11},{4,0},{5,1},{6,2},{7,3},{8,12},{9,13},{1... | collective-permute-start | bytes 442376 | tf_op jit(solution)/shard_map/ppermute | solution.py:36
  6.5 1.5 %collective-permute-start.5 = (bf16[64,1152]{1,0:T(8,128)(2,1)S(1)}, bf16[64,1152]{1,0:T(8,128)(2,1)S(1)}, u32[]{:S(2)}, u32[]{:S(2)}) collective-permute-start(bf16[64,1152]{1,0:T(8,128)(2,1)S(1)} %shard_map.56.token_ref), channel_id=1, source_target_pairs={{0,2},{1,3},{2,0},{3,1},{4,6},{5,7},{6,4},{7,5},{8,10},{9,11},{10,... | collective-permute-start | bytes 442376 | tf_op jit(solution)/shard_map/ppermute | solution.py:22
  8.0 0.3 collective-permute-start.6
  8.3 1.6 %shard_map.57.target_ref = bf16[1024,1024]{1,0:T(8,128)(2,1)S(1)} custom-call(bf16[1024,1024]{1,0:T(8,128)(2,1)} %array_ref.1, bf16[64,1152]{1,0:T(8,128)(2,1)S(1)} %shard_map.56.token_ref), custom_call_target="tpu_custom_call" | custom-call | flops 1 | bytes 1 | tf_op jit(solution)/shard_map/pallas_call | solution.py:116
  9.9 0.0 collective-permute-done.1.refs_0_.refs_2_
  9.9 2.8 %collective-permute-done.2.refs_1_.refs_3_ = bf16[64,1152]{1,0:T(8,128)(2,1)S(1)} collective-permute-done((bf16[64,1152]{1,0:T(8,128)(2,1)S(1)}, bf16[64,1152]{1,0:T(8,128)(2,1)S(1)}, u32[]{:S(2)}, u32[]{:S(2)}) %collective-permute-start.2) | collective-permute-done | bytes 147488 | tf_op jit(solution)/shard_map/ppermute | solution.py:36
  12.8 3.2 %collective-permute-start.3 = (bf16[64,1152]{1,0:T(8,128)(2,1)S(1)}, bf16[64,1152]{1,0:T(8,128)(2,1)S(1)}, u32[]{:S(2)}, u32[]{:S(2)}) collective-permute-start(bf16[64,1152]{1,0:T(8,128)(2,1)S(1)} %broadcast_select_fusion), channel_id=1, source_target_pairs={{0,6},{1,5},{2,4},{3,7},{4,2},{5,1},{6,0},{7,3},{8,14},{9,13},{10,... | collective-permute-start | bytes 442376 | tf_op jit(solution)/shard_map/ppermute | solution.py:27
  16.0 0.0 collective-permute-start.4
  16.0 0.6 %collective-permute-start.9 = (bf16[64,1152]{1,0:T(8,128)(2,1)S(1)}, bf16[64,1152]{1,0:T(8,128)(2,1)S(1)}, u32[]{:S(2)}, u32[]{:S(2)}) collective-permute-start(bf16[64,1152]{1,0:T(8,128)(2,1)S(1)} %broadcast_select_fusion), channel_id=1, source_target_pairs={{0,2},{1,7},{2,0},{3,5},{4,6},{5,3},{6,4},{7,1},{8,10},{9,15},{10,... | collective-permute-start | bytes 442376 | tf_op jit(solution)/shard_map/ppermute | solution.py:27
  16.6 0.0 collective-permute-done.5.refs_2_.refs_4_
  16.6 0.3 collective-permute-done.6.refs_3_.refs_5_
  17.0 0.1 collective-permute-start.7
  17.1 1.9 %shard_map.59 = (f32[1024,128]{1,0:T(8,128)S(1)}, f32[1024,128]{1,0:T(8,128)S(1)}, f32[1024,128]{1,0:T(8,128)S(1)}) custom-call(bf16[1024,1024]{1,0:T(8,128)(2,1)S(1)} %shard_map.57.target_ref, bf16[64,1152]{1,0:T(8,128)(2,1)S(1)} %shard_map.55.refs_0_, bf16[64,1152]{1,0:T(8,128)(2,1)S(1)} %collective-permute-done.refs_1_, ...), custom_call_target="tpu_custom_call" | custom-call | flops 20000000000 | bytes 1 | tf_op jit(solution)/shard_map/pallas_call | solution.py:179
  18.9 0.1 collective-permute-done.7.refs_0_
  19.0 1.6 %shard_map.60 = (f32[1024,128]{1,0:T(8,128)S(1)}, f32[1024,128]{1,0:T(8,128)S(1)}, f32[1024,128]{1,0:T(8,128)S(1)}) custom-call(bf16[1024,1024]{1,0:T(8,128)(2,1)S(1)} %shard_map.57.target_ref, bf16[256,1152]{1,0:T(8,128)(2,1)S(1)} %collective-permute-done.7.refs_0_, f32[1024,128]{1,0:T(8,128)S(1)} %get-tuple-element.16.refs_1_, ...), custom_call_target="tpu_custom_call" | custom-call | flops 20000000000 | bytes 1 | tf_op jit(solution)/shard_map/pallas_call | solution.py:179
  20.6 0.2 collective-permute-done.3.refs_0_
  20.8 1.4 %collective-permute-done.4.refs_1_ = bf16[64,1152]{1,0:T(8,128)(2,1)S(1)} collective-permute-done((bf16[64,1152]{1,0:T(8,128)(2,1)S(1)}, bf16[64,1152]{1,0:T(8,128)(2,1)S(1)}, u32[]{:S(2)}, u32[]{:S(2)}) %collective-permute-start.4) | collective-permute-done | bytes 147488 | tf_op jit(solution)/shard_map/ppermute | solution.py:27
  22.3 0.0 copy-start
  22.3 0.0 copy-start.1
  22.3 0.1 collective-permute-start.8
  22.4 0.8 %collective-permute-done.9.refs_2_ = bf16[64,1152]{1,0:T(8,128)(2,1)S(1)} collective-permute-done((bf16[64,1152]{1,0:T(8,128)(2,1)S(1)}, bf16[64,1152]{1,0:T(8,128)(2,1)S(1)}, u32[]{:S(2)}, u32[]{:S(2)}) %collective-permute-start.9) | collective-permute-done | bytes 147488 | tf_op jit(solution)/shard_map/ppermute | solution.py:27
  23.2 0.0 collective-permute-start.10
  23.2 1.1 %shard_map.62 = (f32[1024,128]{1,0:T(8,128)S(1)}, f32[1024,128]{1,0:T(8,128)S(1)}, f32[1024,128]{1,0:T(8,128)S(1)}) custom-call(bf16[1024,1024]{1,0:T(8,128)(2,1)S(1)} %shard_map.57.target_ref, bf16[64,1152]{1,0:T(8,128)(2,1)S(1)} %collective-permute-done.3.refs_0_, bf16[64,1152]{1,0:T(8,128)(2,1)S(1)} %collective-permute-done.4.refs_1_, ...), custom_call_target="tpu_custom_call" | custom-call | flops 1 | bytes 1 | tf_op jit(solution)/shard_map/pallas_call | solution.py:179
  24.3 0.2 collective-permute-done.10.refs_1_
  24.6 0.0 collective-permute-done.8.refs_0_
  24.6 0.0 copy-done
  24.6 0.0 copy-done.1
  24.6 1.2 %shard_map.63 = (f32[1024,128]{1,0:T(8,128)S(1)}, f32[1,128]{1,0:T(1,128)S(1)}) custom-call(bf16[1024,1024]{1,0:T(8,128)(2,1)S(1)} %shard_map.57.target_ref, bf16[128,1152]{1,0:T(8,128)(2,1)S(1)} %collective-permute-done.8.refs_0_, bf16[64,1152]{1,0:T(8,128)(2,1)S(1)} %collective-permute-done.10.refs_1_, f32[1024,128]{1,0:T(8,128)S(1)} %get-tuple-element.22.refs_2_, ...), custom_call_target="tpu_custom_call" | custom-call | flops 1 | bytes 1 | tf_op jit(solution)/shard_map/pallas_call | solution.py:179
  25.8 0.4 collective-permute-start.11
  26.2 0.8 %collective-permute-done.11 = f32[1,128]{1,0:T(1,128)S(1)} collective-permute-done((f32[1,128]{1,0:T(1,128)S(1)}, f32[1,128]{1,0:T(1,128)S(1)}, u32[]{:S(2)}, u32[]{:S(2)}) %collective-permute-start.11) | collective-permute-done | bytes 544 | tf_op jit(solution)/shard_map/ppermute | solution.py:22
  27.0 0.9 %collective-permute-start.12 = (f32[1,128]{1,0:T(1,128)S(1)}, f32[1,128]{1,0:T(1,128)S(1)}, u32[]{:S(2)}, u32[]{:S(2)}) collective-permute-start(f32[1,128]{1,0:T(1,128)S(1)} %add.36), channel_id=1, source_target_pairs={{0,4},{1,7},{2,6},{3,5},{4,0},{5,3},{6,2},{7,1},{8,12},{9,15},{10,... | collective-permute-start | bytes 1544 | tf_op jit(solution)/shard_map/ppermute | solution.py:27
  27.9 1.1 %collective-permute-start.13 = (f32[1,128]{1,0:T(1,128)S(1)}, f32[1,128]{1,0:T(1,128)S(1)}, u32[]{:S(2)}, u32[]{:S(2)}) collective-permute-start(f32[1,128]{1,0:T(1,128)S(1)} %add.36), channel_id=1, source_target_pairs={{0,2},{1,5},{2,0},{3,7},{4,6},{5,1},{6,4},{7,3},{8,10},{9,13},{10,... | collective-permute-start | bytes 1544 | tf_op jit(solution)/shard_map/ppermute | solution.py:27
  29.0 1.5 %collective-permute-done.12 = f32[1,128]{1,0:T(1,128)S(1)} collective-permute-done((f32[1,128]{1,0:T(1,128)S(1)}, f32[1,128]{1,0:T(1,128)S(1)}, u32[]{:S(2)}, u32[]{:S(2)}) %collective-permute-start.12) | collective-permute-done | bytes 544 | tf_op jit(solution)/shard_map/ppermute | solution.py:27
  30.5 0.9 %collective-permute-done.13 = f32[1,128]{1,0:T(1,128)S(1)} collective-permute-done((f32[1,128]{1,0:T(1,128)S(1)}, f32[1,128]{1,0:T(1,128)S(1)}, u32[]{:S(2)}, u32[]{:S(2)}) %collective-permute-start.13) | collective-permute-done | bytes 544 | tf_op jit(solution)/shard_map/ppermute | solution.py:27
  31.5 0.0 collective-permute-start.14
  31.5 1.1 %collective-permute-done.14 = f32[1,128]{1,0:T(1,128)S(1)} collective-permute-done((f32[1,128]{1,0:T(1,128)S(1)}, f32[1,128]{1,0:T(1,128)S(1)}, u32[]{:S(2)}, u32[]{:S(2)}) %collective-permute-start.14) | collective-permute-done | bytes 544 | tf_op jit(solution)/shard_map/ppermute | solution.py:22
  32.6 3.2 %collective-permute-start.15 = (f32[1,128]{1,0:T(1,128)S(1)}, f32[1,128]{1,0:T(1,128)S(1)}, u32[]{:S(2)}, u32[]{:S(2)}) collective-permute-start(f32[1,128]{1,0:T(1,128)S(1)} %add.39), channel_id=1, source_target_pairs={{0,8},{1,9},{2,10},{3,11},{4,12},{5,13},{6,14},{7,15},{8,0},{9,1},... | collective-permute-start | bytes 1544 | tf_op jit(solution)/shard_map/ppermute | solution.py:22
  35.9 1.5 %collective-permute-done.15 = f32[1,128]{1,0:T(1,128)S(1)} collective-permute-done((f32[1,128]{1,0:T(1,128)S(1)}, f32[1,128]{1,0:T(1,128)S(1)}, u32[]{:S(2)}, u32[]{:S(2)}) %collective-permute-start.15) | collective-permute-done | bytes 544 | tf_op jit(solution)/shard_map/ppermute | solution.py:22
  37.4 0.8 %broadcast_divide_fusion = f32[1024,128]{1,0:T(8,128)} fusion(f32[1024,128]{1,0:T(8,128)S(1)} %get-tuple-element.25, f32[128]{0:T(128)S(1)} %sqrt_bitcast_fusion), kind=kLoop, calls=%fused_computation | loop fusion | flops 131072 | bytes 1049088 | tf_op jit(solution)/shard_map/div | solution.py:223
  (8 shorter events, 0.1 us)
Async XLA Ops:
  0.9 3.2 %collective-permute-start = (bf16[64,1152]{1,0:T(8,128)(2,1)S(1)}, bf16[64,1152]{1,0:T(8,128)(2,1)S(1)}, u32[]{:S(2)}, u32[]{:S(2)}) collective-permute-start(bf16[64,1152]{1,0:T(8,128)(2,1)S(1)} %shard_map.55.refs_0_), channel_id=1, source_target_pairs={{0,1},{1,0},{2,3},{3,2},{4,5},{5,4},{6,7},{7,6},{8,9},{9,8},{10,11... | collective-permute-start | bytes 442376 | tf_op jit(solution)/shard_map/ppermute | solution.py:22
  1.4 8.5 %collective-permute-start.1 = (bf16[64,1152]{1,0:T(8,128)(2,1)S(1)}, bf16[64,1152]{1,0:T(8,128)(2,1)S(1)}, u32[]{:S(2)}, u32[]{:S(2)}) collective-permute-start(bf16[64,1152]{1,0:T(8,128)(2,1)S(1)} %shard_map.55.refs_0_), channel_id=1, source_target_pairs={{0,4},{1,5},{2,6},{3,7},{4,12},{5,13},{6,14},{7,15},{8,0},{9,1},{1... | collective-permute-start | bytes 442376 | tf_op jit(solution)/shard_map/ppermute | solution.py:36
  4.1 8.7 %collective-permute-start.2 = (bf16[64,1152]{1,0:T(8,128)(2,1)S(1)}, bf16[64,1152]{1,0:T(8,128)(2,1)S(1)}, u32[]{:S(2)}, u32[]{:S(2)}) collective-permute-start(bf16[64,1152]{1,0:T(8,128)(2,1)S(1)} %shard_map.56.token_ref), channel_id=1, source_target_pairs={{0,8},{1,9},{2,10},{3,11},{4,0},{5,1},{6,2},{7,3},{8,12},{9,13},{1... | collective-permute-start | bytes 442376 | tf_op jit(solution)/shard_map/ppermute | solution.py:36
  6.5 10.1 %collective-permute-start.5 = (bf16[64,1152]{1,0:T(8,128)(2,1)S(1)}, bf16[64,1152]{1,0:T(8,128)(2,1)S(1)}, u32[]{:S(2)}, u32[]{:S(2)}) collective-permute-start(bf16[64,1152]{1,0:T(8,128)(2,1)S(1)} %shard_map.56.token_ref), channel_id=1, source_target_pairs={{0,2},{1,3},{2,0},{3,1},{4,6},{5,7},{6,4},{7,5},{8,10},{9,11},{10,... | collective-permute-start | bytes 442376 | tf_op jit(solution)/shard_map/ppermute | solution.py:22
  8.0 8.9 %collective-permute-start.6 = (bf16[64,1152]{1,0:T(8,128)(2,1)S(1)}, bf16[64,1152]{1,0:T(8,128)(2,1)S(1)}, u32[]{:S(2)}, u32[]{:S(2)}) collective-permute-start(bf16[64,1152]{1,0:T(8,128)(2,1)S(1)} %shard_map.56.token_ref), channel_id=1, source_target_pairs={{0,6},{1,7},{2,4},{3,5},{4,2},{5,3},{6,0},{7,1},{8,14},{9,15},{10,... | collective-permute-start | bytes 442376 | tf_op jit(solution)/shard_map/ppermute | solution.py:22
  12.8 8.0 %collective-permute-start.3 = (bf16[64,1152]{1,0:T(8,128)(2,1)S(1)}, bf16[64,1152]{1,0:T(8,128)(2,1)S(1)}, u32[]{:S(2)}, u32[]{:S(2)}) collective-permute-start(bf16[64,1152]{1,0:T(8,128)(2,1)S(1)} %broadcast_select_fusion), channel_id=1, source_target_pairs={{0,6},{1,5},{2,4},{3,7},{4,2},{5,1},{6,0},{7,3},{8,14},{9,13},{10,... | collective-permute-start | bytes 442376 | tf_op jit(solution)/shard_map/ppermute | solution.py:27
  16.0 6.3 %collective-permute-start.4 = (bf16[64,1152]{1,0:T(8,128)(2,1)S(1)}, bf16[64,1152]{1,0:T(8,128)(2,1)S(1)}, u32[]{:S(2)}, u32[]{:S(2)}) collective-permute-start(bf16[64,1152]{1,0:T(8,128)(2,1)S(1)} %broadcast_select_fusion), channel_id=1, source_target_pairs={{0,4},{1,3},{2,6},{3,1},{4,0},{5,7},{6,2},{7,5},{8,12},{9,11},{10,... | collective-permute-start | bytes 442376 | tf_op jit(solution)/shard_map/ppermute | solution.py:27
  16.0 7.2 %collective-permute-start.9 = (bf16[64,1152]{1,0:T(8,128)(2,1)S(1)}, bf16[64,1152]{1,0:T(8,128)(2,1)S(1)}, u32[]{:S(2)}, u32[]{:S(2)}) collective-permute-start(bf16[64,1152]{1,0:T(8,128)(2,1)S(1)} %broadcast_select_fusion), channel_id=1, source_target_pairs={{0,2},{1,7},{2,0},{3,5},{4,6},{5,3},{6,4},{7,1},{8,10},{9,15},{10,... | collective-permute-start | bytes 442376 | tf_op jit(solution)/shard_map/ppermute | solution.py:27
  17.0 2.1 %collective-permute-start.7 = (bf16[256,1152]{1,0:T(8,128)(2,1)S(1)}, bf16[256,1152]{1,0:T(8,128)(2,1)S(1)}, u32[]{:S(2)}, u32[]{:S(2)}) collective-permute-start(bf16[256,1152]{1,0:T(8,128)(2,1)S(1)} %shard_map.58), channel_id=1, source_target_pairs={{0,1},{1,0},{2,3},{3,2},{4,5},{5,4},{6,7},{7,6},{8,9},{9,8},{10,11... | collective-permute-start | bytes 1769480 | tf_op jit(solution)/shard_map/ppermute | solution.py:22
  22.3 2.3 %copy-start = (f32[1024,128]{1,0:T(8,128)S(1)}, f32[1024,128]{1,0:T(8,128)}, u32[]{:S(2)}) copy-start(f32[1024,128]{1,0:T(8,128)} %refs_5_.1) | copy-start | bytes 1572868
  22.3 2.3 %copy-start.1 = (f32[1024,128]{1,0:T(8,128)S(1)}, f32[1024,128]{1,0:T(8,128)}, u32[]{:S(2)}) copy-start(f32[1024,128]{1,0:T(8,128)} %refs_6_.1) | copy-start | bytes 1572868
  22.3 2.3 %collective-permute-start.8 = (bf16[128,1152]{1,0:T(8,128)(2,1)S(1)}, bf16[128,1152]{1,0:T(8,128)(2,1)S(1)}, u32[]{:S(2)}, u32[]{:S(2)}) collective-permute-start(bf16[128,1152]{1,0:T(8,128)(2,1)S(1)} %shard_map.61), channel_id=1, source_target_pairs={{0,1},{1,0},{2,3},{3,2},{4,5},{5,4},{6,7},{7,6},{8,9},{9,8},{10,11... | collective-permute-start | bytes 884744 | tf_op jit(solution)/shard_map/ppermute | solution.py:22
  23.2 1.4 %collective-permute-start.10 = (bf16[64,1152]{1,0:T(8,128)(2,1)S(1)}, bf16[64,1152]{1,0:T(8,128)(2,1)S(1)}, u32[]{:S(2)}, u32[]{:S(2)}) collective-permute-start(bf16[64,1152]{1,0:T(8,128)(2,1)S(1)} %collective-permute-done.9.refs_2_), channel_id=1, source_target_pairs={{0,1},{1,0},{2,3},{3,2},{4,5},{5,4},{6,7},{7,6},{8,9},{9,8},{10,11... | collective-permute-start | bytes 442376 | tf_op jit(solution)/shard_map/ppermute | solution.py:22
  25.8 1.2 %collective-permute-start.11 = (f32[1,128]{1,0:T(1,128)S(1)}, f32[1,128]{1,0:T(1,128)S(1)}, u32[]{:S(2)}, u32[]{:S(2)}) collective-permute-start(f32[1,128]{1,0:T(1,128)S(1)} %get-tuple-element.26), channel_id=1, source_target_pairs={{0,1},{1,0},{2,3},{3,2},{4,5},{5,4},{6,7},{7,6},{8,9},{9,8},{10,11... | collective-permute-start | bytes 1544 | tf_op jit(solution)/shard_map/ppermute | solution.py:22
  27.0 3.5 %collective-permute-start.12 = (f32[1,128]{1,0:T(1,128)S(1)}, f32[1,128]{1,0:T(1,128)S(1)}, u32[]{:S(2)}, u32[]{:S(2)}) collective-permute-start(f32[1,128]{1,0:T(1,128)S(1)} %add.36), channel_id=1, source_target_pairs={{0,4},{1,7},{2,6},{3,5},{4,0},{5,3},{6,2},{7,1},{8,12},{9,15},{10,... | collective-permute-start | bytes 1544 | tf_op jit(solution)/shard_map/ppermute | solution.py:27
  27.9 3.5 %collective-permute-start.13 = (f32[1,128]{1,0:T(1,128)S(1)}, f32[1,128]{1,0:T(1,128)S(1)}, u32[]{:S(2)}, u32[]{:S(2)}) collective-permute-start(f32[1,128]{1,0:T(1,128)S(1)} %add.36), channel_id=1, source_target_pairs={{0,2},{1,5},{2,0},{3,7},{4,6},{5,1},{6,4},{7,3},{8,10},{9,13},{10,... | collective-permute-start | bytes 1544 | tf_op jit(solution)/shard_map/ppermute | solution.py:27
  31.5 1.1 %collective-permute-start.14 = (f32[1,128]{1,0:T(1,128)S(1)}, f32[1,128]{1,0:T(1,128)S(1)}, u32[]{:S(2)}, u32[]{:S(2)}) collective-permute-start(f32[1,128]{1,0:T(1,128)S(1)} %broadcast_select_fusion.1), channel_id=1, source_target_pairs={{0,1},{1,0},{2,3},{3,2},{4,5},{5,4},{6,7},{7,6},{8,9},{9,8},{10,11... | collective-permute-start | bytes 1544 | tf_op jit(solution)/shard_map/ppermute | solution.py:22
  32.6 4.8 %collective-permute-start.15 = (f32[1,128]{1,0:T(1,128)S(1)}, f32[1,128]{1,0:T(1,128)S(1)}, u32[]{:S(2)}, u32[]{:S(2)}) collective-permute-start(f32[1,128]{1,0:T(1,128)S(1)} %add.39), channel_id=1, source_target_pairs={{0,8},{1,9},{2,10},{3,11},{4,12},{5,13},{6,14},{7,15},{8,0},{9,1},... | collective-permute-start | bytes 1544 | tf_op jit(solution)/shard_map/ppermute | solution.py:22
